TPU v7x, 32 devices: a whole 2x2x4 slice. The times are simulated.
32 devices in a mesh: row: 4 (over y, core), col: 8 (over z, x).
Axes of the slice: x: 2, y: 2, z: 4, core: 2. Of those that a mesh axis runs over, the one named last changes fastest.
Arguments:
- row_points: bfloat16 [64, 1024], P(None, 'row'), may hold values from -6 to 6
- col_points: bfloat16 [64, 65536], P(None, 'col'), may hold values from -6 to 6
- random_panel: bfloat16 [65536, 128], P('col'), may hold values from -6 to 6
Outputs:
- left_basis: float32 [1024, 128], P('row')
- coefficients: bfloat16 [128, 65536], P('row', 'col')
All inputs are finite; a program needn't handle non-finite values.
Results may differ from a plain program's by a relative error of at most 0.015.
Values may be sent and summed in bfloat16 or wider, within the bound.
No kernel may reach another device: no remote copies, remote signals or barrier semaphores. Data moves between devices by JAX's collectives and lax.ppermute only.
A program may use at most 64 MiB of HBM per device.

v0:
```python
import math

import jax
import jax.numpy as jnp
from jax import lax
from jax.sharding import PartitionSpec as P


def kernel_tile(points_left, left_sq, col_block, exp_scale):
    cross = jnp.einsum("kr,kc->rc", points_left, col_block, preferred_element_type=jnp.float32)
    col_sq = jnp.sum(jnp.square(col_block.astype(jnp.float32)), axis=0)
    return jnp.exp((2.0 * cross - left_sq[:, None] - col_sq[None, :]) * exp_scale)


def per_device(row_points, col_points, random_panel):
    feature_dim, row_dev = row_points.shape
    col_dev, sketch_width = random_panel.shape
    exp_scale = 2.0 / feature_dim
    row_sq = jnp.sum(jnp.square(row_points.astype(jnp.float32)), axis=0)
    block_width = math.gcd(col_dev, 2048)
    block_count = col_dev // block_width
    blocks = col_points.reshape(feature_dim, block_count, block_width).transpose(1, 0, 2)
    panel_blocks = random_panel.reshape(block_count, block_width, sketch_width)
    start_sum = jnp.zeros((row_dev, sketch_width), jnp.float32)

    def add_only(accum_sum, block_pair):
        kernel = kernel_tile(row_points, row_sq, block_pair[0], exp_scale).astype(jnp.bfloat16)
        return (
            accum_sum + jnp.dot(kernel, block_pair[1], preferred_element_type=jnp.float32),
            None,
        )

    partial_value, _ = lax.scan(add_only, start_sum, (blocks, panel_blocks))
    sketch = lax.psum(partial_value, "col")
    local_gram = jnp.dot(
        sketch.T, sketch, precision=lax.Precision.HIGHEST, preferred_element_type=jnp.float32
    )
    gram_matrix = lax.psum(local_gram, "row")
    factor = jnp.linalg.cholesky(gram_matrix)
    orthonormal = jax.scipy.linalg.solve_triangular(factor, sketch.T, lower=True).T
    left_basis = orthonormal * math.sqrt(row_dev * lax.axis_size("row"))
    orth_bf = orthonormal.astype(jnp.bfloat16)
    all_points, all_orth = (
        lax.all_gather(row_points, "row", axis=1, tiled=True),
        lax.all_gather(orth_bf, "row", axis=0, tiled=True),
    )
    all_sq = jnp.sum(jnp.square(all_points.astype(jnp.float32)), axis=0)
    col_share = col_dev // lax.axis_size("row")
    my_columns = lax.dynamic_slice_in_dim(
        col_points, lax.axis_index("row") * col_share, col_share, 1
    )
    fine_width = math.gcd(col_share, 512)
    fine_count = col_share // fine_width
    fine_blocks = my_columns.reshape(feature_dim, fine_count, fine_width).transpose(1, 0, 2)

    def column_part(col_block):
        kernel = kernel_tile(all_points, all_sq, col_block, exp_scale).astype(jnp.bfloat16)
        return jnp.einsum("rq,rc->qc", all_orth, kernel, preferred_element_type=jnp.float32)

    pieces = lax.map(column_part, fine_blocks)
    finished = pieces.transpose(1, 0, 2).reshape(sketch_width, col_share).astype(jnp.bfloat16)
    coefficients = lax.all_to_all(finished, "row", split_axis=0, concat_axis=1, tiled=True)
    return (left_basis, coefficients)


def solution(mesh):
    placed = (P(None, "row"), P(None, "col"), P("col", None))
    return jax.shard_map(
        per_device,
        mesh=mesh,
        in_specs=placed,
        out_specs=(P("row", None), P("row", "col")),
        check_vma=False,
    )
```

profile of v0, /device:TPU:0, one launch (start us, length us, event | category | flops | bytes accessed | tf_op | source)
XLA Modules:
  0.0 181.1 jit_solution(18354700522800073453)
XLA Ops:
  7.2 1.9 %reshape.33 = bf16[64,4,2048]{2,1,0:T(4,128)(2,1)S(1)} reshape(bf16[64,8192]{1,0:T(8,128)(2,1)} %param.8) | data formatting | bytes 2097152 | tf_op jit(solution)/shard_map/reshape | solution.py:22
  9.7 9.7 %while.22 = (s32[]{:T(128)}, f32[256,128]{1,0:T(8,128)S(1)}, bf16[4,64,2048]{2,1,0:T(8,128)(2,1)S(1)}, bf16[64,256]{1,0:T(8,128)(2,1)S(1)}, f32[256]{0:T(256)S(1...) while((s32[]{:T(128)}, f32[256,128]{1,0:T(8,128)S(1)}, ...), condition=%wide.region_3.4_spmd.clone, body=%wide.region_1.3_spmd.clone.sunk | while | flops 204404736 | bytes 1362019 | solution.py:33
  9.8 2.3 %fusion.63 = f32[256,128]{1,0:T(8,128)S(1)} fusion(bf16[64,256]{1,0:T(8,128)(2,1)S(1)} %get-tuple-element.232, f32[2048]{0:T(1024)S(1)} %multiply_reduce_fusion.7, f32[256]{0:T(256)S(1)} %get-tuple-element.233, bf16[4,2048,128]{2,1,0:T(8,128)(2,1)} %get-tuple-element.234, s32[]{:T(128)} %get-tuple-element.221, ...), kind=kOutput, calls=%fused_computation.21.clone.1 | convolution fusion | flops 204013568 | bytes 1091585 | tf_op jit(solution)/shard_map/while/body/eval_jaxpr/dot_general | solution.py:29
  12.2 2.3 %fusion.63 = f32[256,128]{1,0:T(8,128)S(1)} fusion(bf16[64,256]{1,0:T(8,128)(2,1)S(1)} %get-tuple-element.232, f32[2048]{0:T(1024)S(1)} %multiply_reduce_fusion.7, f32[256]{0:T(256)S(1)} %get-tuple-element.233, bf16[4,2048,128]{2,1,0:T(8,128)(2,1)} %get-tuple-element.234, s32[]{:T(128)} %get-tuple-element.221, ...), kind=kOutput, calls=%fused_computation.21.clone.1 | convolution fusion | flops 204013568 | bytes 1091585 | tf_op jit(solution)/shard_map/while/body/eval_jaxpr/dot_general | solution.py:29
  14.6 2.3 %fusion.63 = f32[256,128]{1,0:T(8,128)S(1)} fusion(bf16[64,256]{1,0:T(8,128)(2,1)S(1)} %get-tuple-element.232, f32[2048]{0:T(1024)S(1)} %multiply_reduce_fusion.7, f32[256]{0:T(256)S(1)} %get-tuple-element.233, bf16[4,2048,128]{2,1,0:T(8,128)(2,1)} %get-tuple-element.234, s32[]{:T(128)} %get-tuple-element.221, ...), kind=kOutput, calls=%fused_computation.21.clone.1 | convolution fusion | flops 204013568 | bytes 1091585 | tf_op jit(solution)/shard_map/while/body/eval_jaxpr/dot_general | solution.py:29
  17.1 2.3 %fusion.63 = f32[256,128]{1,0:T(8,128)S(1)} fusion(bf16[64,256]{1,0:T(8,128)(2,1)S(1)} %get-tuple-element.232, f32[2048]{0:T(1024)S(1)} %multiply_reduce_fusion.7, f32[256]{0:T(256)S(1)} %get-tuple-element.233, bf16[4,2048,128]{2,1,0:T(8,128)(2,1)} %get-tuple-element.234, s32[]{:T(128)} %get-tuple-element.221, ...), kind=kOutput, calls=%fused_computation.21.clone.1 | convolution fusion | flops 204013568 | bytes 1091585 | tf_op jit(solution)/shard_map/while/body/eval_jaxpr/dot_general | solution.py:29
  20.1 1.0 constant_dynamic-slice_fusion
  21.1 6.5 %all_gather.6 = bf16[64,1024]{1,0:T(8,128)(2,1)S(1)} all-gather(bf16[64,256]{1,0:T(8,128)(2,1)S(1)} %get-tuple-element.264), channel_id=1, replica_groups=mesh['row'=4,'col'=8] {'row'}, dimensions={1}, use_global_device_ids=true | all-gather | bytes 163840 | tf_op jit(solution)/shard_map/all_gather | solution.py:44
  27.6 65.0 %all-reduce.3.cloned.1.call-done = f32[256,128]{1,0:T(8,128)} async-done(((f32[256,128]{1,0:T(8,128)}), f32[256,128]{1,0:T(8,128)}) %all-reduce.3.cloned.1.call-update) | async-done | bytes 131088 | tf_op jit(solution)/shard_map/psum | solution.py:34
  92.6 2.1 %fusion.41 = f32[128,128]{0,1:T(8,128)} fusion(f32[256,128]{1,0:T(8,128)} %all-reduce.3.cloned.1.call-done), kind=kOutput, calls=%fused_computation.50 | convolution fusion | flops 50331648 | bytes 196608 | tf_op jit(solution)/shard_map/dot_general | solution.py:35
  95.0 31.0 %all-reduce.5.cloned.1.call-done = f32[128,128]{0,1:T(8,128)} async-done(((f32[128,128]{0,1:T(8,128)}), f32[128,128]{0,1:T(8,128)}) %all-reduce.5.cloned.1.call-update) | async-done | bytes 65552 | tf_op jit(solution)/shard_map/psum | solution.py:38
  126.0 0.9 copy.15
  126.9 0.9 fusion.39
  127.8 11.7 %cholesky.16 = f32[128,128]{1,0:T(8,128)S(1)} custom-call(f32[128,128]{1,0:T(8,128)S(1)} %fusion.39), custom_call_target="Cholesky" | custom-call | tf_op jit(solution)/shard_map/jit(cholesky)/cholesky | solution.py:39
  140.9 9.8 %custom-call.7 = f32[1,128,128]{1,2,0:T(8,128)S(1)} custom-call(f32[1,128,128]{2,1,0:T(8,128)S(1)} %fusion.36), custom_call_target="InvertDiagBlocksLowerTriangular" | custom-call | tf_op jit(solution)/shard_map/jit(_solve_triangular)/triangular_solve | solution.py:40
  150.7 0.9 fusion.40
  151.6 5.8 %all_gather.7 = bf16[1024,128]{1,0:T(8,128)(2,1)S(1)} all-gather(bf16[256,128]{1,0:T(8,128)(2,1)S(1)} %get-tuple-element.137), channel_id=1, replica_groups=mesh['row'=4,'col'=8] {'row'}, dimensions={0}, use_global_device_ids=true | all-gather | bytes 327680 | tf_op jit(solution)/shard_map/all_gather | solution.py:45
  157.4 4.1 %while.21 = (s32[]{:T(128)}, bf16[4,128,512]{1,2,0:T(8,128)(2,1)S(1)}, bf16[4,64,512]{2,1,0:T(8,128)(2,1)S(1)}, bf16[64,1024]{1,0:T(8,128)(2,1)S(1)}, f32[1024]{...) while((s32[]{:T(128)}, bf16[4,128,512]{1,2,0:T(8,128)(2,1)S(1)}, ...), condition=%wide.region_11.12_spmd, body=%wide.region_9.11_spmd.sunk | while | flops 204045824 | bytes 795729 | solution.py:60
  157.4 1.0 fusion.59
  158.4 1.0 fusion.59
  159.4 1.0 fusion.59
  160.5 1.0 fusion.59
  162.2 11.2 %all_to_all.16 = bf16[4,32,2048]{2,1,0:T(8,128)(2,1)S(1)} all-to-all(bf16[4,32,2048]{2,1,0:T(8,128)(2,1)S(1)} %convert_element_type.36), channel_id=1, replica_groups=mesh['row'=4,'col'=8] {'row'}, dimensions={0} | all-to-all | bytes 1048576 | tf_op jit(solution)/shard_map/all_to_all | solution.py:62
  173.5 0.8 copy.20
  (30 shorter events, 4.2 us)
Async XLA Ops:
  7.2 85.5 %all-reduce.3.cloned.1.call-start = ((), (), s32[]{:S(2)}) async-start(), calls=%async_computation.1 | async-start | bytes 262144 | tf_op jit(solution)/shard_map/psum | solution.py:34
  7.2 2.5 %copy-start.1 = (bf16[64,256]{1,0:T(8,128)(2,1)S(1)}, bf16[64,256]{1,0:T(8,128)(2,1)}, u32[]{:S(2)}) copy-start(bf16[64,256]{1,0:T(8,128)(2,1)} %param.7) | copy-start | bytes 98308
  19.4 0.7 copy-start.2
  20.1 105.9 %all-reduce.5.cloned.1.call-start = ((), (), s32[]{:S(2)}) async-start(), calls=%async_computation.2 | async-start | bytes 131072 | tf_op jit(solution)/shard_map/psum | solution.py:38
  92.6 58.0 %copy-start = (f32[256,128]{1,0:T(8,128)S(1)}, f32[256,128]{1,0:T(8,128)}, u32[]{:S(2)}) copy-start(f32[256,128]{1,0:T(8,128)} %all-reduce.3.cloned.1.call-done) | copy-start | bytes 393220
Sparse Core Ops, SparseCore 0:
  20.2 72.4 all-reduce.2
  95.6 30.3 all-reduce.4
where the time goes:
time: 182 us; the launch traced here: 181 us
  waiting for transfers between devices  96 us (53%)
  other arithmetic  24.2 us (13%)
  blocking collectives  23.5 us (13%)
  matrix products  16.1 us (9%)
  between operations  14.2 us (8%)
  local copies, waits for them, and re-layouts  6.82 us (4%)
    psum x1, waiting for transfers between devices, per_device(): sketch = lax.psum(partial_value, 'col')  65 us
    psum x1, waiting for transfers between devices, per_device(): gram_matrix = lax.psum(local_gram, 'row')  31 us
    another operation x3, other arithmetic, per_device(): factor = jnp.linalg.cholesky(gram_matrix)  12.4 us
    all_to_all x1, blocking collectives, per_device(): lax.all_to_all(finished, 'row', split_axis=0, concat_axis=1, tiled=True)  11.2 us
    another operation x2, other arithmetic, per_device(): jax.scipy.linalg.solve_triangular(factor, sketch.T, lower=True)  10.5 us
    dot_general x4, matrix products, add_only(): jnp.dot(kernel, block_pair[1], preferred_element_type=jnp.float32)  9.23 us
    all_gather x1, blocking collectives, per_device(): lax.all_gather(row_points, 'row', axis=1, tiled=True)  6.51 us
    all_gather x1, blocking collectives, per_device(): lax.all_gather(orth_bf, 'row', axis=0, tiled=True)  5.77 us
  transfers between devices with their start and end apart: 2, of which 2 were waited for; matrix products, arithmetic and copies ran while one was open for 1% of the time, Pallas kernels for 0%

commit v1 on v0

v1 whole, which is shorter than its diff:
```python
import functools
import math

import jax
import jax.numpy as jnp
from jax import lax
from jax.experimental import pallas as pl
from jax.experimental.pallas import tpu as pltpu
from jax.sharding import PartitionSpec as P

F32 = jnp.float32
BF16 = jnp.bfloat16
EXACT = lax.Precision.HIGHEST
VMEM_BYTES = 48 << 20


def contract(a, b, a_dim, b_dim, precision=None):
    dims = (((a_dim,), (b_dim,)), ((), ()))
    return lax.dot_general(a, b, dims, precision=precision, preferred_element_type=F32)


def widened(points, scale, factor, first):
    wide = points.astype(F32)
    terms_sum = -scale * jnp.sum(wide * wide, axis=0, keepdims=True)
    place = lax.broadcasted_iota(jnp.int32, (16, points.shape[1]), 0)
    terms_at, ones_at = (0, 3) if first else (3, 0)
    extra = jnp.where((place >= ones_at) & (place < ones_at + 3), 1.0, 0.0)
    for k in range(3):
        term = terms_sum.astype(BF16).astype(F32)
        extra = jnp.where(place == terms_at + k, term, extra)
        terms_sum = terms_sum - term
    return jnp.concatenate([(wide * factor).astype(BF16), extra.astype(BF16)], axis=0)


def kernel_values(left, col_points, scale):
    return jnp.exp(contract(left, widened(col_points, scale, 1.0, False), 1, 0)).astype(BF16)


def sketch_body(scale, chunk, row_ref, col_ref, panel_ref, half_ref, keep_ref, send_ref, total_ref):
    left = widened(row_ref[...], scale, 2.0 * scale, True).T
    total = jnp.zeros(total_ref.shape, F32)
    for c in range(0, col_ref.shape[1], chunk):
        tile = kernel_values(left, col_ref[:, c : c + chunk], scale)
        total = total + contract(tile, panel_ref[c : c + chunk, :], 1, 0)
    total_ref[...] = total
    half, rows = half_ref[0], keep_ref.shape[0]
    keep_ref[...] = total_ref[pl.ds(pl.multiple_of(half * rows, rows), rows), :]
    send_ref[...] = total_ref[pl.ds(pl.multiple_of((1 - half) * rows, rows), rows), :]


def sketch_halves(row_points, col_points, panel, half):
    dim, rows = row_points.shape
    col_dev, width = panel.shape
    part = jax.ShapeDtypeStruct((rows // 2, width), F32)
    whole = pl.BlockSpec(memory_space=pltpu.VMEM)
    return pl.pallas_call(
        functools.partial(sketch_body, 2.0 / dim, math.gcd(col_dev, 1024)),
        in_specs=[whole, whole, whole, pl.BlockSpec(memory_space=pltpu.SMEM)],
        out_specs=[whole, whole],
        out_shape=[part, part],
        scratch_shapes=[pltpu.VMEM((rows, width), F32)],
        compiler_params=pltpu.CompilerParams(vmem_limit_bytes=VMEM_BYTES),
        name="sketch",
    )(row_points, col_points, panel, half)


def inverse_factor(gram):
    n = gram.shape[0]
    tiles = n // 8
    left = [gram[8 * t : 8 * t + 8, :] for t in range(tiles)]
    lane = lax.broadcasted_iota(jnp.int32, (8, n), 1)
    sub = lax.broadcasted_iota(jnp.int32, (8, n), 0)
    right = [jnp.where(lane == sub + 8 * t, 1.0, 0.0) for t in range(tiles)]
    inverse = []

    def row(tile, k):
        return jnp.broadcast_to(tile[k : k + 1, :], (8, n))

    def column(tile, k):
        return jnp.broadcast_to(tile[:, k : k + 1], (8, n))

    def weighted(weights, rows):
        pairs = [w * r for w, r in zip(weights, rows)]
        while len(pairs) > 1:
            pairs = [a + b for a, b in zip(pairs[::2], pairs[1::2])]
        return pairs[0]

    for b in range(tiles):
        upper, lower = left[b], right[b]
        block = [column(upper, 8 * b + k) for k in range(8)]
        root, below = [], []
        for k in range(8):
            root.append(lax.rsqrt(row(block[k], k)))
            step = jnp.where(sub > k, block[k] * root[k], 0.0)
            below.append({j: row(step, j) for j in range(k + 1, 8)})
            for j in range(k + 1, 8):
                block[j] = block[j] - step * below[k][j]
            upper_row, lower_row = row(upper, k) * root[k], row(lower, k) * root[k]
            upper, lower = upper - step * upper_row, lower - step * lower_row
        scales = root[0]
        for k in range(1, 8):
            scales = jnp.where(sub == k, root[k], scales)
        upper, lower = upper * scales, lower * scales
        inverse.append(lower)
        upper_rows = [row(upper, k) for k in range(8)]
        lower_rows = [row(lower, k) for k in range(8)]
        for t in range(b + 1, tiles):
            entry = [column(left[t], 8 * b + k) for k in range(8)]
            for k in range(8):
                entry[k] = entry[k] * root[k]
                for j in range(k + 1, 8):
                    entry[j] = entry[j] - entry[k] * below[k][j]
            left[t] = left[t] - weighted(entry, upper_rows)
            right[t] = right[t] - weighted(entry, lower_rows)
    return inverse


def factor_body(norm, rank_ref, sketch_ref, left_basis_ref, ranks_ref, inverse_ref):
    sketch = sketch_ref[...]
    gram = contract(sketch, sketch, 0, 0, EXACT)
    for t, tile in enumerate(inverse_factor(gram)):
        inverse_ref[8 * t : 8 * t + 8, :] = tile
    own = sketch_ref[: left_basis_ref.shape[0], :]
    left_basis_ref[...] = contract(own, inverse_ref[...], 1, 1, EXACT) * norm
    count = ranks_ref.shape[0]
    mine = inverse_ref[pl.ds(pl.multiple_of(rank_ref[0] * count, count), count), :]
    ranks_ref[...] = contract(mine, sketch, 1, 1, EXACT).astype(BF16)


def factor(sketch, rows, share, index):
    total, width = sketch.shape
    whole = pl.BlockSpec(memory_space=pltpu.VMEM)
    return pl.pallas_call(
        functools.partial(factor_body, math.sqrt(total)),
        in_specs=[pl.BlockSpec(memory_space=pltpu.SMEM), whole],
        out_specs=[whole, whole],
        out_shape=[jax.ShapeDtypeStruct((rows, width), F32), jax.ShapeDtypeStruct((share, total), BF16)],
        scratch_shapes=[pltpu.VMEM((width, width), F32)],
        compiler_params=pltpu.CompilerParams(vmem_limit_bytes=VMEM_BYTES),
        name="factor",
    )(index, sketch)


def project_body(scale, chunk, ranks_ref, row_ref, col_ref, out_ref, left_ref):
    @pl.when(pl.program_id(0) == 0)
    def _():
        rows = row_ref.shape[2]
        for k in range(row_ref.shape[0]):
            left_ref[k * rows : (k + 1) * rows, :] = widened(row_ref[k], scale, 2.0 * scale, True).T

    ranks = ranks_ref[...]
    for c in range(0, col_ref.shape[1], chunk):
        tile = kernel_values(left_ref[...], col_ref[:, c : c + chunk], scale)
        out_ref[:, c : c + chunk] = contract(ranks, tile, 1, 0).astype(BF16)


def project(ranks, row_blocks, col_points):
    count, total = ranks.shape
    blocks, dim, rows = row_blocks.shape
    col_dev = col_points.shape[1]
    width = math.gcd(col_dev, 2048)
    return pl.pallas_call(
        functools.partial(project_body, 2.0 / dim, math.gcd(width, 512)),
        grid=(col_dev // width,),
        in_specs=[
            pl.BlockSpec((count, total), lambda i: (0, 0)),
            pl.BlockSpec((blocks, dim, rows), lambda i: (0, 0, 0)),
            pl.BlockSpec((dim, width), lambda i: (0, i)),
        ],
        out_specs=pl.BlockSpec((count, width), lambda i: (0, i)),
        out_shape=jax.ShapeDtypeStruct((count, col_dev), BF16),
        scratch_shapes=[pltpu.VMEM((total, dim + 16), BF16)],
        compiler_params=pltpu.CompilerParams(vmem_limit_bytes=VMEM_BYTES),
        name="project",
    )(ranks, row_blocks, col_points)


def swapped(value, axis, bit):
    return lax.ppermute(value, axis, [(i, i ^ bit) for i in range(lax.axis_size(axis))])


def bits_down(size):
    return [1 << k for k in reversed(range(size.bit_length() - 1))]


def per_device(row_points, col_points, random_panel):
    rows = row_points.shape[1]
    width = random_panel.shape[1]
    row_count, col_count = lax.axis_size("row"), lax.axis_size("col")
    row_at, col_at = lax.axis_index("row"), lax.axis_index("col")

    row_blocks = row_points[None]
    for bit in bits_down(row_count):
        row_blocks = jnp.concatenate([row_blocks, swapped(row_blocks, "row", bit)], axis=0)

    half = col_at % 2
    keep, send = sketch_halves(row_points, col_points, random_panel, half.reshape(1))
    part = keep + swapped(send, "col", 1)
    for bit in reversed(bits_down(col_count)[:-1]):
        part = part + swapped(part, "col", bit)
    other = swapped(part, "col", 1)
    first = half == 0
    sketch = jnp.concatenate([jnp.where(first, part, other), jnp.where(first, other, part)], axis=0)
    for bit in bits_down(row_count):
        sketch = jnp.concatenate([sketch, swapped(sketch, "row", bit)], axis=0)

    left_basis, ranks = factor(sketch, rows, width // row_count, row_at.reshape(1))
    return (left_basis, project(ranks, row_blocks, col_points))


def solution(mesh):
    placed = (P(None, "row"), P(None, "col"), P("col", None))
    return jax.shard_map(
        per_device,
        mesh=mesh,
        in_specs=placed,
        out_specs=(P("row", None), P("row", "col")),
        check_vma=False,
    )
```

time: 182 us -> 48 us (0.26)
  waiting for transfers between devices: 96 us -> 14.1 us
  other arithmetic: 24.2 us -> 0.13 us
  blocking collectives: 23.5 us -> 0 us
  Pallas kernels: 0 us -> 16.8 us
  matrix products: 16.1 us -> 0 us
  between operations: 14.2 us -> 0.75 us
  starting transfers between devices: 0.08 us -> 12.4 us
  local copies, waits for them, and re-layouts: 6.82 us -> 3.58 us
    psum x2 -> x0, waiting for transfers between devices: 96 us -> none  [the longest x1 65 us: per_device(): sketch = lax.psum(partial_value, 'col')]
    another operation x5 -> x0, other arithmetic: 22.9 us -> none  [the longest x3 12.4 us: per_device(): factor = jnp.linalg.cholesky(gram_matrix)]
    pallas_call x0 -> x3, Pallas kernels: none -> 16.8 us  [the longest x1 8.55 us: project(): pl.pallas_call(functools.partial(project_body, 2.0 / dim, math.gcd(width,...]
    dot_general x9 -> x0, matrix products: 15.2 us -> none  [the longest x4 9.23 us: add_only(): jnp.dot(kernel, block_pair[1], preferred_element_type=jnp.float32)]
    ppermute x0 -> x8, waiting for transfers between devices: none -> 14.1 us  [swapped(): lax.ppermute(value, axis, [(i, i ^ bit) for i in range(lax.axis_size(axis...]
    ppermute x0 -> x8, starting transfers between devices: none -> 12.4 us  [swapped(): lax.ppermute(value, axis, [(i, i ^ bit) for i in range(lax.axis_size(axis...]
    all_gather x2 -> x0, blocking collectives: 12.3 us -> none  [the longest x1 6.51 us: per_device(): lax.all_gather(row_points, 'row', axis=1, tiled=True)]
    all_to_all x1 -> x0, blocking collectives: 11.2 us -> none  [per_device(): lax.all_to_all(finished, 'row', split_axis=0, concat_axis=1, tiled=True)]
  transfers between devices with their start and end apart: 2 -> 8, of which waited for: 2 -> 7; matrix products, arithmetic and copies ran while one was open for 1% -> 0% of each run, Pallas kernels for 0% -> 0%
where the time goes in v1:
time: 48 us; the launch traced here: 47.7 us
  Pallas kernels  16.8 us (35%)
  waiting for transfers between devices  14.1 us (29%)
  starting transfers between devices  12.4 us (26%)
  local copies, waits for them, and re-layouts  3.58 us (7%)
  between operations  0.75 us (2%)
    ppermute x8, waiting for transfers between devices, swapped(): lax.ppermute(value, axis, [(i, i ^ bit) for i in range(lax.axis_size(axis...  14.1 us
    ppermute x8, starting transfers between devices, swapped(): lax.ppermute(value, axis, [(i, i ^ bit) for i in range(lax.axis_size(axis...  12.4 us
    pallas_call x1, Pallas kernels, project(): pl.pallas_call(functools.partial(project_body, 2.0 / dim, math.gcd(width,...  8.55 us
    pallas_call x1, Pallas kernels, factor(): pl.pallas_call(functools.partial(factor_body, math.sqrt(total)), in_specs...  5.85 us
    unnamed x10, local copies, waits for them, and re-layouts  3.58 us
    pallas_call x1, Pallas kernels, sketch_halves(): pl.pallas_call(functools.partial(sketch_body, 2.0 / dim, math.gcd(col_dev...  2.41 us
  transfers between devices with their start and end apart: 8, of which 7 were waited for; matrix products, arithmetic and copies ran while one was open for 0% of the time, Pallas kernels for 0%

profile of v1, /device:TPU:0, one launch (start us, length us, event | category | flops | bytes accessed | tf_op | source)
XLA Modules:
  0.0 47.7 jit_solution(11289856704605955879)
XLA Ops:
  0.6 0.0 copy-start
  0.7 1.2 %copy-done = bf16[64,8192]{1,0:T(8,128)(2,1)S(1)} copy-done((bf16[64,8192]{1,0:T(8,128)(2,1)S(1)}, bf16[64,8192]{1,0:T(8,128)(2,1)}, u32[]{:S(2)}) %copy-start) | copy-done | bytes 1048600
  1.9 1.6 %copy-done.2 = bf16[8192,128]{1,0:T(8,128)(2,1)S(1)} copy-done((bf16[8192,128]{1,0:T(8,128)(2,1)S(1)}, bf16[8192,128]{1,0:T(8,128)(2,1)}, u32[]{:S(2)}) %copy-start.2) | copy-done | bytes 2097176
  3.5 0.8 %copy-done.3 = bf16[64,256]{1,0:T(8,128)(2,1)S(1)} copy-done((bf16[64,256]{1,0:T(8,128)(2,1)S(1)}, bf16[64,256]{1,0:T(8,128)(2,1)}, u32[]{:S(2)}) %copy-start.3) | copy-done | bytes 32792
  4.2 2.4 %sketch.1 = (f32[128,128]{1,0:T(8,128)S(1)}, f32[128,128]{1,0:T(8,128)S(1)}) custom-call(bf16[64,256]{1,0:T(8,128)(2,1)S(1)} %copy-done.3, bf16[64,8192]{1,0:T(8,128)(2,1)S(1)} %copy-done, bf16[8192,128]{1,0:T(8,128)(2,1)S(1)} %copy-done.2, s32[1]{0:T(128)} %bitcast.1.half_ref), custom_call_target="tpu_custom_call" | custom-call | tf_op jit(solution)/shard_map/sketch/pallas_call | solution.py:56
  6.6 0.0 copy-start.1
  6.7 3.0 %collective-permute-start = (f32[128,128]{1,0:T(8,128)S(1)}, f32[128,128]{1,0:T(8,128)S(1)}, u32[]{:S(2)}, u32[]{:S(2)}) collective-permute-start(f32[128,128]{1,0:T(8,128)S(1)} %get-tuple-element.7), channel_id=1, source_target_pairs={{0,1},{1,0},{2,3},{3,2},{4,5},{5,4},{6,7},{7,6},{8,9},{9,8},{10,11... | collective-permute-start | bytes 196616 | tf_op jit(solution)/shard_map/ppermute | solution.py:179
  9.7 2.2 %collective-permute-done = f32[128,128]{1,0:T(8,128)S(1)} collective-permute-done((f32[128,128]{1,0:T(8,128)S(1)}, f32[128,128]{1,0:T(8,128)S(1)}, u32[]{:S(2)}, u32[]{:S(2)}) %collective-permute-start) | collective-permute-done | bytes 65568 | tf_op jit(solution)/shard_map/ppermute | solution.py:179
  11.9 2.2 %collective-permute-start.1 = (f32[128,128]{1,0:T(8,128)S(1)}, f32[128,128]{1,0:T(8,128)S(1)}, u32[]{:S(2)}, u32[]{:S(2)}) collective-permute-start(f32[128,128]{1,0:T(8,128)S(1)} %add.14), channel_id=1, source_target_pairs={{0,2},{1,3},{2,0},{3,1},{4,6},{5,7},{6,4},{7,5},{8,10},{9,11},{10,... | collective-permute-start | bytes 196616 | tf_op jit(solution)/shard_map/ppermute | solution.py:179
  14.1 2.2 %collective-permute-done.1 = f32[128,128]{1,0:T(8,128)S(1)} collective-permute-done((f32[128,128]{1,0:T(8,128)S(1)}, f32[128,128]{1,0:T(8,128)S(1)}, u32[]{:S(2)}, u32[]{:S(2)}) %collective-permute-start.1) | collective-permute-done | bytes 65568 | tf_op jit(solution)/shard_map/ppermute | solution.py:179
  16.3 3.1 %collective-permute-start.2 = (f32[128,128]{1,0:T(8,128)S(1)}, f32[128,128]{1,0:T(8,128)S(1)}, u32[]{:S(2)}, u32[]{:S(2)}) collective-permute-start(f32[128,128]{1,0:T(8,128)S(1)} %add.15), channel_id=1, source_target_pairs={{0,4},{1,5},{2,6},{3,7},{4,0},{5,1},{6,2},{7,3},{8,12},{9,13},{10,... | collective-permute-start | bytes 196616 | tf_op jit(solution)/shard_map/ppermute | solution.py:179
  19.4 2.2 %collective-permute-done.2 = f32[128,128]{1,0:T(8,128)S(1)} collective-permute-done((f32[128,128]{1,0:T(8,128)S(1)}, f32[128,128]{1,0:T(8,128)S(1)}, u32[]{:S(2)}, u32[]{:S(2)}) %collective-permute-start.2) | collective-permute-done | bytes 65568 | tf_op jit(solution)/shard_map/ppermute | solution.py:179
  21.7 1.9 %collective-permute-start.3 = (f32[128,128]{1,0:T(8,128)S(1)}, f32[128,128]{1,0:T(8,128)S(1)}, u32[]{:S(2)}, u32[]{:S(2)}) collective-permute-start(f32[128,128]{1,0:T(8,128)S(1)} %add.16), channel_id=1, source_target_pairs={{0,1},{1,0},{2,3},{3,2},{4,5},{5,4},{6,7},{7,6},{8,9},{9,8},{10,11... | collective-permute-start | bytes 196616 | tf_op jit(solution)/shard_map/ppermute | solution.py:179
  23.6 2.4 %collective-permute-done.3 = f32[128,128]{1,0:T(8,128)S(1)} collective-permute-done((f32[128,128]{1,0:T(8,128)S(1)}, f32[128,128]{1,0:T(8,128)S(1)}, u32[]{:S(2)}, u32[]{:S(2)}) %collective-permute-start.3) | collective-permute-done | bytes 65568 | tf_op jit(solution)/shard_map/ppermute | solution.py:179
  26.1 1.9 %collective-permute-start.4 = (f32[256,128]{1,0:T(8,128)S(1)}, f32[256,128]{1,0:T(8,128)S(1)}, u32[]{:S(2)}, u32[]{:S(2)}) collective-permute-start(f32[256,128]{1,0:T(8,128)S(1)} %pad_maximum_fusion.2), channel_id=1, source_target_pairs={{0,16},{8,24},{16,0},{24,8},{1,17},{9,25},{17,1},{25,9},{2,18},{10... | collective-permute-start | bytes 393224 | tf_op jit(solution)/shard_map/ppermute | solution.py:179
  28.0 0.2 collective-permute-start.6
  28.2 2.9 %collective-permute-done.4 = f32[256,128]{1,0:T(8,128)S(1)} collective-permute-done((f32[256,128]{1,0:T(8,128)S(1)}, f32[256,128]{1,0:T(8,128)S(1)}, u32[]{:S(2)}, u32[]{:S(2)}) %collective-permute-start.4) | collective-permute-done | bytes 131104 | tf_op jit(solution)/shard_map/ppermute | solution.py:179
  31.1 0.1 collective-permute-start.5
  31.2 0.7 %collective-permute-done.6 = bf16[1,64,256]{2,1,0:T(8,128)(2,1)S(1)} collective-permute-done((bf16[1,64,256]{2,1,0:T(8,128)(2,1)S(1)}, bf16[1,64,256]{2,1,0:T(8,128)(2,1)S(1)}, u32[]{:S(2)}, u32[]{:S(2)}) %collective-permute-start.6) | collective-permute-done | bytes 32800 | tf_op jit(solution)/shard_map/ppermute | solution.py:179
  31.9 0.1 collective-permute-start.7
  32.0 1.2 %collective-permute-done.7 = bf16[2,64,256]{2,1,0:T(8,128)(2,1)S(1)} collective-permute-done((bf16[2,64,256]{2,1,0:T(8,128)(2,1)S(1)}, bf16[2,64,256]{2,1,0:T(8,128)(2,1)S(1)}, u32[]{:S(2)}, u32[]{:S(2)}) %collective-permute-start.7) | collective-permute-done | bytes 65568 | tf_op jit(solution)/shard_map/ppermute | solution.py:179
  33.3 0.0 collective-permute-done.5
  33.3 5.8 %factor.1 = (f32[256,128]{1,0:T(8,128)}, bf16[32,1024]{1,0:T(8,128)(2,1)S(1)}) custom-call(s32[1]{0:T(128)} %bitcast.rank_ref, f32[1024,128]{1,0:T(8,128)S(1)} %pad_maximum_fusion.sketch_ref), custom_call_target="tpu_custom_call" | custom-call | tf_op jit(solution)/shard_map/factor/pallas_call | solution.py:133
  39.2 8.6 %project.1 = bf16[32,8192]{1,0:T(8,128)(2,1)} custom-call(bf16[32,1024]{1,0:T(8,128)(2,1)S(1)} %get-tuple-element.9.ranks_ref, bf16[4,64,256]{2,1,0:T(8,128)(2,1)S(1)} %pad_maximum_fusion.3.row_ref, bf16[64,8192]{1,0:T(8,128)(2,1)S(1)} %copy-done.1), custom_call_target="tpu_custom_call" | custom-call | tf_op jit(solution)/shard_map/project/pallas_call | solution.py:162
  (14 shorter events, 0.1 us)
Async XLA Ops:
  0.6 1.2 %copy-start = (bf16[64,8192]{1,0:T(8,128)(2,1)S(1)}, bf16[64,8192]{1,0:T(8,128)(2,1)}, u32[]{:S(2)}) copy-start(bf16[64,8192]{1,0:T(8,128)(2,1)} %col_ref.3) | copy-start | bytes 3145732
  1.9 1.6 %copy-start.2 = (bf16[8192,128]{1,0:T(8,128)(2,1)S(1)}, bf16[8192,128]{1,0:T(8,128)(2,1)}, u32[]{:S(2)}) copy-start(bf16[8192,128]{1,0:T(8,128)(2,1)} %panel_ref.1) | copy-start | bytes 6291460
  3.5 0.8 %copy-start.3 = (bf16[64,256]{1,0:T(8,128)(2,1)S(1)}, bf16[64,256]{1,0:T(8,128)(2,1)}, u32[]{:S(2)}) copy-start(bf16[64,256]{1,0:T(8,128)(2,1)} %row_ref.1) | copy-start | bytes 98308
  4.2 23.8 %copy-start.4 = (bf16[64,256]{1,0:T(8,128)(2,1)S(1)}, bf16[64,256]{1,0:T(8,128)(2,1)}, u32[]{:S(2)}) copy-start(bf16[64,256]{1,0:T(8,128)(2,1)} %row_ref.1) | copy-start | bytes 98308
  6.6 32.5 %copy-start.1 = (bf16[64,8192]{1,0:T(8,128)(2,1)S(1)}, bf16[64,8192]{1,0:T(8,128)(2,1)}, u32[]{:S(2)}) copy-start(bf16[64,8192]{1,0:T(8,128)(2,1)} %col_ref.3) | copy-start | bytes 3145732
  6.7 5.2 %collective-permute-start = (f32[128,128]{1,0:T(8,128)S(1)}, f32[128,128]{1,0:T(8,128)S(1)}, u32[]{:S(2)}, u32[]{:S(2)}) collective-permute-start(f32[128,128]{1,0:T(8,128)S(1)} %get-tuple-element.7), channel_id=1, source_target_pairs={{0,1},{1,0},{2,3},{3,2},{4,5},{5,4},{6,7},{7,6},{8,9},{9,8},{10,11... | collective-permute-start | bytes 196616 | tf_op jit(solution)/shard_map/ppermute | solution.py:179
  11.9 4.4 %collective-permute-start.1 = (f32[128,128]{1,0:T(8,128)S(1)}, f32[128,128]{1,0:T(8,128)S(1)}, u32[]{:S(2)}, u32[]{:S(2)}) collective-permute-start(f32[128,128]{1,0:T(8,128)S(1)} %add.14), channel_id=1, source_target_pairs={{0,2},{1,3},{2,0},{3,1},{4,6},{5,7},{6,4},{7,5},{8,10},{9,11},{10,... | collective-permute-start | bytes 196616 | tf_op jit(solution)/shard_map/ppermute | solution.py:179
  16.3 5.3 %collective-permute-start.2 = (f32[128,128]{1,0:T(8,128)S(1)}, f32[128,128]{1,0:T(8,128)S(1)}, u32[]{:S(2)}, u32[]{:S(2)}) collective-permute-start(f32[128,128]{1,0:T(8,128)S(1)} %add.15), channel_id=1, source_target_pairs={{0,4},{1,5},{2,6},{3,7},{4,0},{5,1},{6,2},{7,3},{8,12},{9,13},{10,... | collective-permute-start | bytes 196616 | tf_op jit(solution)/shard_map/ppermute | solution.py:179
  21.7 4.3 %collective-permute-start.3 = (f32[128,128]{1,0:T(8,128)S(1)}, f32[128,128]{1,0:T(8,128)S(1)}, u32[]{:S(2)}, u32[]{:S(2)}) collective-permute-start(f32[128,128]{1,0:T(8,128)S(1)} %add.16), channel_id=1, source_target_pairs={{0,1},{1,0},{2,3},{3,2},{4,5},{5,4},{6,7},{7,6},{8,9},{9,8},{10,11... | collective-permute-start | bytes 196616 | tf_op jit(solution)/shard_map/ppermute | solution.py:179
  26.1 5.0 %collective-permute-start.4 = (f32[256,128]{1,0:T(8,128)S(1)}, f32[256,128]{1,0:T(8,128)S(1)}, u32[]{:S(2)}, u32[]{:S(2)}) collective-permute-start(f32[256,128]{1,0:T(8,128)S(1)} %pad_maximum_fusion.2), channel_id=1, source_target_pairs={{0,16},{8,24},{16,0},{24,8},{1,17},{9,25},{17,1},{25,9},{2,18},{10... | collective-permute-start | bytes 393224 | tf_op jit(solution)/shard_map/ppermute | solution.py:179
  28.0 3.9 %collective-permute-start.6 = (bf16[1,64,256]{2,1,0:T(8,128)(2,1)S(1)}, bf16[1,64,256]{2,1,0:T(8,128)(2,1)S(1)}, u32[]{:S(2)}, u32[]{:S(2)}) collective-permute-start(bf16[1,64,256]{2,1,0:T(8,128)(2,1)S(1)} %bitcast.3), channel_id=1, source_target_pairs={{0,16},{8,24},{16,0},{24,8},{1,17},{9,25},{17,1},{25,9},{2,18},{10... | collective-permute-start | bytes 98312 | tf_op jit(solution)/shard_map/ppermute | solution.py:179
  31.1 2.1 %collective-permute-start.5 = (f32[512,128]{1,0:T(8,128)S(1)}, f32[512,128]{1,0:T(8,128)S(1)}, u32[]{:S(2)}, u32[]{:S(2)}) collective-permute-start(f32[512,128]{1,0:T(8,128)S(1)} %pad_maximum_fusion.1), channel_id=1, source_target_pairs={{0,8},{8,0},{16,24},{24,16},{1,9},{9,1},{17,25},{25,17},{2,10},{10... | collective-permute-start | bytes 786440 | tf_op jit(solution)/shard_map/ppermute | solution.py:179
  31.9 1.3 %collective-permute-start.7 = (bf16[2,64,256]{2,1,0:T(8,128)(2,1)S(1)}, bf16[2,64,256]{2,1,0:T(8,128)(2,1)S(1)}, u32[]{:S(2)}, u32[]{:S(2)}) collective-permute-start(bf16[2,64,256]{2,1,0:T(8,128)(2,1)S(1)} %pad_maximum_fusion.4), channel_id=1, source_target_pairs={{0,8},{8,0},{16,24},{24,16},{1,9},{9,1},{17,25},{25,17},{2,10},{10... | collective-permute-start | bytes 196616 | tf_op jit(solution)/shard_map/ppermute | solution.py:179

commit v2 on v1

--- a/solution.py
+++ b/solution.py
@@ -11,7 +11,8 @@
 F32 = jnp.float32
 BF16 = jnp.bfloat16
 EXACT = lax.Precision.HIGHEST
-VMEM_BYTES = 48 << 20
+VMEM_BYTES = 24 << 20
+TILE_BYTES = 16 << 20
 
 
 def contract(a, b, a_dim, b_dim, precision=None):
@@ -32,16 +33,41 @@
     return jnp.concatenate([(wide * factor).astype(BF16), extra.astype(BF16)], axis=0)
 
 
-def kernel_values(left, col_points, scale):
-    return jnp.exp(contract(left, widened(col_points, scale, 1.0, False), 1, 0)).astype(BF16)
-
-
-def sketch_body(scale, chunk, row_ref, col_ref, panel_ref, half_ref, keep_ref, send_ref, total_ref):
+def exponent(left, right):
+    return jnp.exp(contract(left, right, 1, 0)).astype(BF16)
+
+
+def chunk_width(col_dev):
+    return math.gcd(col_dev, 1024)
+
+
+def sketch_body(
+    scale, half_ref, row_hbm, col_hbm, panel_hbm, keep_ref, send_ref, tile_ref, right_ref,
+    row_ref, col_ref, panel_ref, total_ref, row_sem, col_sem, panel_sem,
+):
+    chunk = chunk_width(col_hbm.shape[1])
+    count = col_hbm.shape[1] // chunk
+    row_copy = pltpu.make_async_copy(row_hbm, row_ref, row_sem)
+    row_copy.start()
+    col_copies, panel_copies = [], []
+    for k in range(count):
+        at = slice(k * chunk, (k + 1) * chunk)
+        col_copies.append(pltpu.make_async_copy(col_hbm.at[:, at], col_ref.at[:, at], col_sem.at[k]))
+        panel_copies.append(pltpu.make_async_copy(panel_hbm.at[at, :], panel_ref.at[at, :], panel_sem.at[k]))
+        col_copies[k].start()
+        panel_copies[k].start()
+    row_copy.wait()
     left = widened(row_ref[...], scale, 2.0 * scale, True).T
     total = jnp.zeros(total_ref.shape, F32)
-    for c in range(0, col_ref.shape[1], chunk):
-        tile = kernel_values(left, col_ref[:, c : c + chunk], scale)
-        total = total + contract(tile, panel_ref[c : c + chunk, :], 1, 0)
+    for k in range(count):
+        at = slice(k * chunk, (k + 1) * chunk)
+        col_copies[k].wait()
+        right = widened(col_ref[:, at], scale, 1.0, False)
+        right_ref[:, at] = right
+        tile = exponent(left, right)
+        tile_ref[:, at] = tile
+        panel_copies[k].wait()
+        total = total + contract(tile, panel_ref[at, :], 1, 0)
     total_ref[...] = total
     half, rows = half_ref[0], keep_ref.shape[0]
     keep_ref[...] = total_ref[pl.ds(pl.multiple_of(half * rows, rows), rows), :]
@@ -51,17 +77,57 @@
 def sketch_halves(row_points, col_points, panel, half):
     dim, rows = row_points.shape
     col_dev, width = panel.shape
+    count = col_dev // chunk_width(col_dev)
     part = jax.ShapeDtypeStruct((rows // 2, width), F32)
+    whole, remote = pl.BlockSpec(memory_space=pltpu.VMEM), pl.BlockSpec(memory_space=pltpu.HBM)
+    return pl.pallas_call(
+        functools.partial(sketch_body, 2.0 / dim),
+        in_specs=[pl.BlockSpec(memory_space=pltpu.SMEM), remote, remote, remote],
+        out_specs=[whole] * 4,
+        out_shape=[
+            part,
+            part,
+            jax.ShapeDtypeStruct((rows, col_dev), BF16),
+            jax.ShapeDtypeStruct((dim + 16, col_dev), BF16),
+        ],
+        scratch_shapes=[
+            pltpu.VMEM((dim, rows), BF16),
+            pltpu.VMEM((dim, col_dev), BF16),
+            pltpu.VMEM((col_dev, width), BF16),
+            pltpu.VMEM((rows, width), F32),
+            pltpu.SemaphoreType.DMA,
+            pltpu.SemaphoreType.DMA((count,)),
+            pltpu.SemaphoreType.DMA((count,)),
+        ],
+        compiler_params=pltpu.CompilerParams(vmem_limit_bytes=VMEM_BYTES),
+        name="sketch",
+    )(half, *[pltpu.with_memory_space_constraint(a, pltpu.HBM) for a in (row_points, col_points, panel)])
+
+
+def tile_body(scale, row_ref, right_ref, tile_ref):
+    left = widened(row_ref[...], scale, 2.0 * scale, True).T
+    chunk = chunk_width(right_ref.shape[1])
+    for c in range(0, right_ref.shape[1], chunk):
+        tile_ref[:, c : c + chunk] = exponent(left, right_ref[:, c : c + chunk])
+
+
+def kernel_tile(row_points, right):
+    dim, rows = row_points.shape
+    depth, col_dev = right.shape
     whole = pl.BlockSpec(memory_space=pltpu.VMEM)
     return pl.pallas_call(
-        functools.partial(sketch_body, 2.0 / dim, math.gcd(col_dev, 1024)),
-        in_specs=[whole, whole, whole, pl.BlockSpec(memory_space=pltpu.SMEM)],
-        out_specs=[whole, whole],
-        out_shape=[part, part],
-        scratch_shapes=[pltpu.VMEM((rows, width), F32)],
-        compiler_params=pltpu.CompilerParams(vmem_limit_bytes=VMEM_BYTES),
-        name="sketch",
-    )(row_points, col_points, panel, half)
+        functools.partial(tile_body, 2.0 / dim),
+        in_specs=[whole, whole],
+        out_specs=whole,
+        out_shape=jax.ShapeDtypeStruct((rows, col_dev), BF16),
+        compiler_params=pltpu.CompilerParams(vmem_limit_bytes=VMEM_BYTES),
+        cost_estimate=pl.CostEstimate(
+            flops=2 * rows * depth * col_dev,
+            bytes_accessed=2 * (rows + depth) * col_dev,
+            transcendentals=rows * col_dev,
+        ),
+        name="kernel_tile",
+    )(row_points, right)
 
 
 def inverse_factor(gram):
@@ -141,42 +207,65 @@
     )(index, sketch)
 
 
-def project_body(scale, chunk, ranks_ref, row_ref, col_ref, out_ref, left_ref):
+def project_body(ranks_ref, *refs):
+    *tile_refs, out_ref = refs
+    chunk = chunk_width(out_ref.shape[1])
+    rows = tile_refs[0].shape[0]
+    for c in range(0, out_ref.shape[1], chunk):
+        total = None
+        for k, tile_ref in enumerate(tile_refs):
+            piece = contract(ranks_ref[:, k * rows : (k + 1) * rows], tile_ref[:, c : c + chunk], 1, 0)
+            total = piece if total is None else total + piece
+        out_ref[:, c : c + chunk] = total.astype(BF16)
+
+
+def project(ranks, tiles):
+    whole = pl.BlockSpec(memory_space=pltpu.VMEM)
+    return pl.pallas_call(
+        project_body,
+        in_specs=[whole] * (1 + len(tiles)),
+        out_specs=whole,
+        out_shape=jax.ShapeDtypeStruct((ranks.shape[0], tiles[0].shape[1]), BF16),
+        compiler_params=pltpu.CompilerParams(vmem_limit_bytes=VMEM_BYTES),
+        name="project",
+    )(ranks, *tiles)
+
+
+def project_anew_body(scale, ranks_ref, row_ref, right_ref, out_ref, left_ref):
     @pl.when(pl.program_id(0) == 0)
     def _():
         rows = row_ref.shape[2]
         for k in range(row_ref.shape[0]):
             left_ref[k * rows : (k + 1) * rows, :] = widened(row_ref[k], scale, 2.0 * scale, True).T
 
-    ranks = ranks_ref[...]
-    for c in range(0, col_ref.shape[1], chunk):
-        tile = kernel_values(left_ref[...], col_ref[:, c : c + chunk], scale)
-        out_ref[:, c : c + chunk] = contract(ranks, tile, 1, 0).astype(BF16)
-
-
-def project(ranks, row_blocks, col_points):
+    out_ref[...] = contract(ranks_ref[...], exponent(left_ref[...], right_ref[...]), 1, 0).astype(BF16)
+
+
+def project_anew(ranks, row_blocks, right):
     count, total = ranks.shape
     blocks, dim, rows = row_blocks.shape
-    col_dev = col_points.shape[1]
-    width = math.gcd(col_dev, 2048)
-    return pl.pallas_call(
-        functools.partial(project_body, 2.0 / dim, math.gcd(width, 512)),
+    depth, col_dev = right.shape
+    width = math.gcd(col_dev, 512)
+    return pl.pallas_call(
+        functools.partial(project_anew_body, 2.0 / dim),
         grid=(col_dev // width,),
         in_specs=[
             pl.BlockSpec((count, total), lambda i: (0, 0)),
             pl.BlockSpec((blocks, dim, rows), lambda i: (0, 0, 0)),
-            pl.BlockSpec((dim, width), lambda i: (0, i)),
+            pl.BlockSpec((depth, width), lambda i: (0, i)),
         ],
         out_specs=pl.BlockSpec((count, width), lambda i: (0, i)),
         out_shape=jax.ShapeDtypeStruct((count, col_dev), BF16),
-        scratch_shapes=[pltpu.VMEM((total, dim + 16), BF16)],
-        compiler_params=pltpu.CompilerParams(vmem_limit_bytes=VMEM_BYTES),
-        name="project",
-    )(ranks, row_blocks, col_points)
-
-
-def swapped(value, axis, bit):
-    return lax.ppermute(value, axis, [(i, i ^ bit) for i in range(lax.axis_size(axis))])
+        scratch_shapes=[pltpu.VMEM((total, depth), BF16)],
+        compiler_params=pltpu.CompilerParams(vmem_limit_bytes=VMEM_BYTES),
+        name="project_anew",
+    )(ranks, row_blocks, right)
+
+
+def swapped(value, row_bit, col_bit):
+    rows, cols = lax.axis_size("row"), lax.axis_size("col")
+    pairs = [(r * cols + c, (r ^ row_bit) * cols + (c ^ col_bit)) for r in range(rows) for c in range(cols)]
+    return lax.ppermute(value, ("row", "col"), pairs)
 
 
 def bits_down(size):
@@ -185,27 +274,47 @@
 
 def per_device(row_points, col_points, random_panel):
     rows = row_points.shape[1]
-    width = random_panel.shape[1]
+    col_dev, width = random_panel.shape
     row_count, col_count = lax.axis_size("row"), lax.axis_size("col")
     row_at, col_at = lax.axis_index("row"), lax.axis_index("col")
-
-    row_blocks = row_points[None]
+    half = col_at % 2
+    keep, send, tile, right = sketch_halves(row_points, col_points, random_panel, half.reshape(1))
+    tiles = [tile]
+    fits = row_count * rows * col_dev * 2 <= TILE_BYTES
+
+    part = keep + swapped(send, 0, 1)
+    blocks = [lax.optimization_barrier((row_points, keep))[0]]
     for bit in bits_down(row_count):
-        row_blocks = jnp.concatenate([row_blocks, swapped(row_blocks, "row", bit)], axis=0)
-
-    half = col_at % 2
-    keep, send = sketch_halves(row_points, col_points, random_panel, half.reshape(1))
-    part = keep + swapped(send, "col", 1)
+        blocks = blocks + [swapped(block, bit, 0) for block in blocks]
+
+    def beside(transferred):
+        if not fits or len(tiles) == row_count:
+            return transferred
+        transferred, tile = lax.optimization_barrier((transferred, kernel_tile(blocks[len(tiles)], right)))
+        tiles.append(tile)
+        return transferred
+
     for bit in reversed(bits_down(col_count)[:-1]):
-        part = part + swapped(part, "col", bit)
-    other = swapped(part, "col", 1)
+        part = part + beside(swapped(part, 0, bit))
+
+    row_bits = bits_down(row_count)
     first = half == 0
-    sketch = jnp.concatenate([jnp.where(first, part, other), jnp.where(first, other, part)], axis=0)
-    for bit in bits_down(row_count):
-        sketch = jnp.concatenate([sketch, swapped(sketch, "row", bit)], axis=0)
+
+    def ordered(mine, other):
+        return jnp.concatenate([jnp.where(first, mine, other), jnp.where(first, other, mine)], axis=0)
+
+    bit = row_bits[0]
+    moved = beside((swapped(part, 0, 1), swapped(part, bit, 0), swapped(part, bit, 1)))
+    sketch = jnp.concatenate([ordered(part, moved[0]), ordered(moved[1], moved[2])], axis=0)
+    for bit in row_bits[1:]:
+        sketch = jnp.concatenate([sketch, swapped(sketch, bit, 0)], axis=0)
 
     left_basis, ranks = factor(sketch, rows, width // row_count, row_at.reshape(1))
-    return (left_basis, project(ranks, row_blocks, col_points))
+    if fits:
+        while len(tiles) < row_count:
+            tiles.append(kernel_tile(blocks[len(tiles)], right))
+        return (left_basis, project(ranks, tiles))
+    return (left_basis, project_anew(ranks, jnp.stack(blocks), right))
 
 
 def solution(mesh):

time: 48 us -> 59.7 us (1.24)
  local copies, waits for them, and re-layouts: 3.58 us -> 16.6 us
  waiting for transfers between devices: 14.1 us -> 8.64 us
  Pallas kernels: 16.8 us -> 20.2 us
  starting transfers between devices: 12.4 us -> 13.1 us
    unnamed x10 -> x18, local copies, waits for them, and re-layouts: 3.58 us -> 16.6 us
    ppermute x8 -> x10, waiting for transfers between devices: 14.1 us -> 8.64 us  [swapped(): return lax.ppermute(value, ('row', 'col'), pairs)]
    pallas_call x2 -> x5, Pallas kernels: 11 us -> 14.2 us  [the longest x1 6.62 us: sketch_halves(): pl.pallas_call(functools.partial(sketch_body, 2.0 / dim), in_specs=[pl.Bl...]
    ppermute x8 -> x10, starting transfers between devices: 12.4 us -> 13.1 us  [swapped(): return lax.ppermute(value, ('row', 'col'), pairs)]
  transfers between devices with their start and end apart: 8 -> 10, of which waited for: 7 -> 5; matrix products, arithmetic and copies ran while one was open for 0% -> 0% of each run, Pallas kernels for 0% -> 6%
where the time goes in v2:
time: 59.7 us; the launch traced here: 59.5 us
  Pallas kernels  20.2 us (34%)
  local copies, waits for them, and re-layouts  16.6 us (28%)
  starting transfers between devices  13.1 us (22%)
  waiting for transfers between devices  8.64 us (14%)
  between operations  0.79 us (1%)
    unnamed x18, local copies, waits for them, and re-layouts  16.6 us
    ppermute x10, starting transfers between devices, swapped(): return lax.ppermute(value, ('row', 'col'), pairs)  13.1 us
    ppermute x10, waiting for transfers between devices, swapped(): return lax.ppermute(value, ('row', 'col'), pairs)  8.64 us
    pallas_call x1, Pallas kernels, sketch_halves(): pl.pallas_call(functools.partial(sketch_body, 2.0 / dim), in_specs=[pl.Bl...  6.62 us
    pallas_call x1, Pallas kernels, factor(): pl.pallas_call(functools.partial(factor_body, math.sqrt(total)), in_specs...  5.99 us
    pallas_call x3, Pallas kernels, kernel_tile(): pl.pallas_call(functools.partial(tile_body, 2.0 / dim), in_specs=[whole,...  3.84 us
    pallas_call x1, Pallas kernels, project(): pl.pallas_call(project_body, in_specs=[whole] * (1 + len(tiles)), out_spe...  3.78 us
  transfers between devices with their start and end apart: 10, of which 5 were waited for; matrix products, arithmetic and copies ran while one was open for 0% of the time, Pallas kernels for 6%

profile of v2, /device:TPU:0, one launch (start us, length us, event | category | flops | bytes accessed | tf_op | source)
XLA Modules:
  0.0 59.5 jit_solution(8301852162068070251)
XLA Ops:
  0.7 6.6 %sketch.1 = (f32[128,128]{1,0:T(8,128)S(1)}, f32[128,128]{1,0:T(8,128)S(1)}, bf16[256,8192]{1,0:T(8,128)(2,1)S(1)}, bf16[80,8192]{1,0:T(8,128)(2,1)S(1)}) custom-call(s32[1]{0:T(128)} %bitcast.1.half_ref, bf16[64,256]{1,0:T(8,128)(2,1)} %row_hbm.1, bf16[64,8192]{1,0:T(8,128)(2,1)} %col_hbm.1, bf16[8192,128]{1,0:T(8,128)(2,1)} %panel_hbm.1), custom_call_target="tpu_custom_call" | custom-call | tf_op jit(solution)/shard_map/sketch/pallas_call | solution.py:83
  7.3 1.9 %copy-done.6 = bf16[256,8192]{1,0:T(8,128)(2,1)} copy-done((bf16[256,8192]{1,0:T(8,128)(2,1)}, bf16[256,8192]{1,0:T(8,128)(2,1)S(1)}, u32[]{:S(2)}) %copy-start.6) | copy-done | bytes 4194328
  9.2 2.9 %collective-permute-start = (f32[128,128]{1,0:T(8,128)S(1)}, f32[128,128]{1,0:T(8,128)S(1)}, u32[]{:S(2)}, u32[]{:S(2)}) collective-permute-start(f32[128,128]{1,0:T(8,128)S(1)} %get-tuple-element.18), channel_id=1, source_target_pairs={{0,1},{1,0},{2,3},{3,2},{4,5},{5,4},{6,7},{7,6},{8,9},{9,8},{10,11... | collective-permute-start | bytes 196616 | tf_op jit(solution)/shard_map/ppermute | solution.py:268
  12.2 2.2 %collective-permute-done = f32[128,128]{1,0:T(8,128)S(1)} collective-permute-done((f32[128,128]{1,0:T(8,128)S(1)}, f32[128,128]{1,0:T(8,128)S(1)}, u32[]{:S(2)}, u32[]{:S(2)}) %collective-permute-start) | collective-permute-done | bytes 65568 | tf_op jit(solution)/shard_map/ppermute | solution.py:268
  14.4 2.2 %collective-permute-start.1 = (f32[128,128]{1,0:T(8,128)S(1)}, f32[128,128]{1,0:T(8,128)S(1)}, u32[]{:S(2)}, u32[]{:S(2)}) collective-permute-start(f32[128,128]{1,0:T(8,128)S(1)} %add.14), channel_id=1, source_target_pairs={{0,2},{1,3},{2,0},{3,1},{4,6},{5,7},{6,4},{7,5},{8,10},{9,11},{10,... | collective-permute-start | bytes 196616 | tf_op jit(solution)/shard_map/ppermute | solution.py:268
  16.6 1.5 %collective-permute-start.2 = (bf16[64,256]{1,0:T(8,128)(2,1)}, bf16[64,256]{1,0:T(8,128)(2,1)S(1)}, u32[]{:S(2)}, u32[]{:S(2)}) collective-permute-start(bf16[64,256]{1,0:T(8,128)(2,1)} %row_hbm.1), channel_id=1, source_target_pairs={{0,16},{1,17},{2,18},{3,19},{4,20},{5,21},{6,22},{7,23},{8,24},{9,... | collective-permute-start | bytes 98312 | tf_op jit(solution)/shard_map/ppermute | solution.py:268
  18.1 2.6 %collective-permute-done.2.row_ref = bf16[64,256]{1,0:T(8,128)(2,1)S(1)} collective-permute-done((bf16[64,256]{1,0:T(8,128)(2,1)}, bf16[64,256]{1,0:T(8,128)(2,1)S(1)}, u32[]{:S(2)}, u32[]{:S(2)}) %collective-permute-start.2) | collective-permute-done | bytes 32800 | tf_op jit(solution)/shard_map/ppermute | solution.py:268
  20.7 1.3 %kernel_tile.3.refs_1_ = bf16[256,8192]{1,0:T(8,128)(2,1)S(1)} custom-call(bf16[64,256]{1,0:T(8,128)(2,1)S(1)} %collective-permute-done.2.row_ref, bf16[80,8192]{1,0:T(8,128)(2,1)S(1)} %get-tuple-element.20.right_ref), custom_call_target="tpu_custom_call" | custom-call | flops 335544320 | bytes 5505024 | tf_op jit(solution)/shard_map/kernel_tile/pallas_call | solution.py:118
  22.0 2.0 %copy-done = bf16[256,8192]{1,0:T(8,128)(2,1)} copy-done((bf16[256,8192]{1,0:T(8,128)(2,1)}, bf16[256,8192]{1,0:T(8,128)(2,1)S(1)}, u32[]{:S(2)}) %copy-start) | copy-done | bytes 4194328
  24.0 2.7 %collective-permute-start.3 = (f32[128,128]{1,0:T(8,128)S(1)}, f32[128,128]{1,0:T(8,128)S(1)}, u32[]{:S(2)}, u32[]{:S(2)}) collective-permute-start(f32[128,128]{1,0:T(8,128)S(1)} %add.15), channel_id=1, source_target_pairs={{0,4},{1,5},{2,6},{3,7},{4,0},{5,1},{6,2},{7,3},{8,12},{9,13},{10,... | collective-permute-start | bytes 196616 | tf_op jit(solution)/shard_map/ppermute | solution.py:268
  26.7 1.2 %collective-permute-done.4.row_ref = bf16[64,256]{1,0:T(8,128)(2,1)S(1)} collective-permute-done((bf16[64,256]{1,0:T(8,128)(2,1)S(1)}, bf16[64,256]{1,0:T(8,128)(2,1)S(1)}, u32[]{:S(2)}, u32[]{:S(2)}) %collective-permute-start.4) | collective-permute-done | bytes 32800 | tf_op jit(solution)/shard_map/ppermute | solution.py:268
  27.9 1.3 %kernel_tile.4.refs_2_ = bf16[256,8192]{1,0:T(8,128)(2,1)S(1)} custom-call(bf16[64,256]{1,0:T(8,128)(2,1)S(1)} %collective-permute-done.4.row_ref, bf16[80,8192]{1,0:T(8,128)(2,1)S(1)} %get-tuple-element.20.right_ref), custom_call_target="tpu_custom_call" | custom-call | flops 335544320 | bytes 5505024 | tf_op jit(solution)/shard_map/kernel_tile/pallas_call | solution.py:118
  29.2 2.0 %copy-done.2 = bf16[256,8192]{1,0:T(8,128)(2,1)} copy-done((bf16[256,8192]{1,0:T(8,128)(2,1)}, bf16[256,8192]{1,0:T(8,128)(2,1)S(1)}, u32[]{:S(2)}) %copy-start.2) | copy-done | bytes 4194328
  31.2 2.5 %collective-permute-start.7 = (f32[128,128]{1,0:T(8,128)S(1)}, f32[128,128]{1,0:T(8,128)S(1)}, u32[]{:S(2)}, u32[]{:S(2)}) collective-permute-start(f32[128,128]{1,0:T(8,128)S(1)} %add.16), channel_id=1, source_target_pairs={{0,17},{1,16},{2,19},{3,18},{4,21},{5,20},{6,23},{7,22},{8,25},{9,... | collective-permute-start | bytes 196616 | tf_op jit(solution)/shard_map/ppermute | solution.py:268
  34.8 1.2 %collective-permute-done.8.row_ref = bf16[64,256]{1,0:T(8,128)(2,1)S(1)} collective-permute-done((bf16[64,256]{1,0:T(8,128)(2,1)S(1)}, bf16[64,256]{1,0:T(8,128)(2,1)S(1)}, u32[]{:S(2)}, u32[]{:S(2)}) %collective-permute-start.8) | collective-permute-done | bytes 32800 | tf_op jit(solution)/shard_map/ppermute | solution.py:268
  36.0 1.3 %kernel_tile.5.refs_3_ = bf16[256,8192]{1,0:T(8,128)(2,1)S(1)} custom-call(bf16[64,256]{1,0:T(8,128)(2,1)S(1)} %collective-permute-done.8.row_ref, bf16[80,8192]{1,0:T(8,128)(2,1)S(1)} %get-tuple-element.20.right_ref), custom_call_target="tpu_custom_call" | custom-call | flops 335544320 | bytes 5505024 | tf_op jit(solution)/shard_map/kernel_tile/pallas_call | solution.py:118
  37.3 1.9 %copy-done.4 = bf16[256,8192]{1,0:T(8,128)(2,1)} copy-done((bf16[256,8192]{1,0:T(8,128)(2,1)}, bf16[256,8192]{1,0:T(8,128)(2,1)S(1)}, u32[]{:S(2)}) %copy-start.4) | copy-done | bytes 4194328
  39.5 1.4 %collective-permute-done.9 = f32[512,128]{1,0:T(8,128)S(1)} collective-permute-done((f32[512,128]{1,0:T(8,128)S(1)}, f32[512,128]{1,0:T(8,128)S(1)}, u32[]{:S(2)}, u32[]{:S(2)}) %collective-permute-start.9) | collective-permute-done | bytes 262176 | tf_op jit(solution)/shard_map/ppermute | solution.py:268
  40.9 6.0 %factor.1 = (f32[256,128]{1,0:T(8,128)}, bf16[32,1024]{1,0:T(8,128)(2,1)S(1)}) custom-call(s32[1]{0:T(128)} %bitcast.rank_ref, f32[1024,128]{1,0:T(8,128)S(1)} %constant_dynamic-update-slice_fusion.sketch_ref), custom_call_target="tpu_custom_call" | custom-call | tf_op jit(solution)/shard_map/factor/pallas_call | solution.py:199
  46.9 2.2 %copy-done.1 = bf16[256,8192]{1,0:T(8,128)(2,1)S(1)} copy-done((bf16[256,8192]{1,0:T(8,128)(2,1)S(1)}, bf16[256,8192]{1,0:T(8,128)(2,1)}, u32[]{:S(2)}) %copy-start.1) | copy-done | bytes 4194328
  49.1 2.2 %copy-done.3 = bf16[256,8192]{1,0:T(8,128)(2,1)S(1)} copy-done((bf16[256,8192]{1,0:T(8,128)(2,1)S(1)}, bf16[256,8192]{1,0:T(8,128)(2,1)}, u32[]{:S(2)}) %copy-start.3) | copy-done | bytes 4194328
  51.3 2.2 %copy-done.5 = bf16[256,8192]{1,0:T(8,128)(2,1)S(1)} copy-done((bf16[256,8192]{1,0:T(8,128)(2,1)S(1)}, bf16[256,8192]{1,0:T(8,128)(2,1)}, u32[]{:S(2)}) %copy-start.5) | copy-done | bytes 4194328
  53.5 2.2 %copy-done.7 = bf16[256,8192]{1,0:T(8,128)(2,1)S(1)} copy-done((bf16[256,8192]{1,0:T(8,128)(2,1)S(1)}, bf16[256,8192]{1,0:T(8,128)(2,1)}, u32[]{:S(2)}) %copy-start.7) | copy-done | bytes 4194328
  55.7 3.8 %project.1 = bf16[32,8192]{1,0:T(8,128)(2,1)} custom-call(bf16[32,1024]{1,0:T(8,128)(2,1)S(1)} %get-tuple-element.27.ranks_ref, bf16[256,8192]{1,0:T(8,128)(2,1)S(1)} %copy-done.7, bf16[256,8192]{1,0:T(8,128)(2,1)S(1)} %copy-done.1, bf16[256,8192]{1,0:T(8,128)(2,1)S(1)} %copy-done.3, bf16[256,8192]{1,0:T(8,128)(2,1)S(1)} %copy-done.5), custom_call_target="tpu_custom_call" | custom-call | tf_op jit(solution)/shard_map/project/pallas_call | solution.py:224
  (29 shorter events, 1.4 us)
Async XLA Ops:
  0.6 26.0 %copy-start.8 = (bf16[64,256]{1,0:T(8,128)(2,1)S(1)}, bf16[64,256]{1,0:T(8,128)(2,1)}, u32[]{:S(2)}) copy-start(bf16[64,256]{1,0:T(8,128)(2,1)} %row_hbm.1) | copy-start | bytes 98308
  7.3 1.9 %copy-start.6 = (bf16[256,8192]{1,0:T(8,128)(2,1)}, bf16[256,8192]{1,0:T(8,128)(2,1)S(1)}, u32[]{:S(2)}) copy-start(bf16[256,8192]{1,0:T(8,128)(2,1)S(1)} %get-tuple-element.28.refs_0_) | copy-start | bytes 12582916
  9.2 5.2 %collective-permute-start = (f32[128,128]{1,0:T(8,128)S(1)}, f32[128,128]{1,0:T(8,128)S(1)}, u32[]{:S(2)}, u32[]{:S(2)}) collective-permute-start(f32[128,128]{1,0:T(8,128)S(1)} %get-tuple-element.18), channel_id=1, source_target_pairs={{0,1},{1,0},{2,3},{3,2},{4,5},{5,4},{6,7},{7,6},{8,9},{9,8},{10,11... | collective-permute-start | bytes 196616 | tf_op jit(solution)/shard_map/ppermute | solution.py:268
  14.4 9.6 %collective-permute-start.1 = (f32[128,128]{1,0:T(8,128)S(1)}, f32[128,128]{1,0:T(8,128)S(1)}, u32[]{:S(2)}, u32[]{:S(2)}) collective-permute-start(f32[128,128]{1,0:T(8,128)S(1)} %add.14), channel_id=1, source_target_pairs={{0,2},{1,3},{2,0},{3,1},{4,6},{5,7},{6,4},{7,5},{8,10},{9,11},{10,... | collective-permute-start | bytes 196616 | tf_op jit(solution)/shard_map/ppermute | solution.py:268
  16.6 4.1 %collective-permute-start.2 = (bf16[64,256]{1,0:T(8,128)(2,1)}, bf16[64,256]{1,0:T(8,128)(2,1)S(1)}, u32[]{:S(2)}, u32[]{:S(2)}) collective-permute-start(bf16[64,256]{1,0:T(8,128)(2,1)} %row_hbm.1), channel_id=1, source_target_pairs={{0,16},{1,17},{2,18},{3,19},{4,20},{5,21},{6,22},{7,23},{8,24},{9,... | collective-permute-start | bytes 98312 | tf_op jit(solution)/shard_map/ppermute | solution.py:268
  22.0 2.0 %copy-start = (bf16[256,8192]{1,0:T(8,128)(2,1)}, bf16[256,8192]{1,0:T(8,128)(2,1)S(1)}, u32[]{:S(2)}) copy-start(bf16[256,8192]{1,0:T(8,128)(2,1)S(1)} %kernel_tile.3.refs_1_) | copy-start | bytes 12582916
  24.0 7.2 %collective-permute-start.3 = (f32[128,128]{1,0:T(8,128)S(1)}, f32[128,128]{1,0:T(8,128)S(1)}, u32[]{:S(2)}, u32[]{:S(2)}) collective-permute-start(f32[128,128]{1,0:T(8,128)S(1)} %add.15), channel_id=1, source_target_pairs={{0,4},{1,5},{2,6},{3,7},{4,0},{5,1},{6,2},{7,3},{8,12},{9,13},{10,... | collective-permute-start | bytes 196616 | tf_op jit(solution)/shard_map/ppermute | solution.py:268
  26.7 1.2 %collective-permute-start.4 = (bf16[64,256]{1,0:T(8,128)(2,1)S(1)}, bf16[64,256]{1,0:T(8,128)(2,1)S(1)}, u32[]{:S(2)}, u32[]{:S(2)}) collective-permute-start(bf16[64,256]{1,0:T(8,128)(2,1)S(1)} %copy-done.8), channel_id=1, source_target_pairs={{0,8},{1,9},{2,10},{3,11},{4,12},{5,13},{6,14},{7,15},{8,0},{9,1},... | collective-permute-start | bytes 98312 | tf_op jit(solution)/shard_map/ppermute | solution.py:268
  29.2 2.0 %copy-start.2 = (bf16[256,8192]{1,0:T(8,128)(2,1)}, bf16[256,8192]{1,0:T(8,128)(2,1)S(1)}, u32[]{:S(2)}) copy-start(bf16[256,8192]{1,0:T(8,128)(2,1)S(1)} %kernel_tile.4.refs_2_) | copy-start | bytes 12582916
  31.2 8.0 %collective-permute-start.7 = (f32[128,128]{1,0:T(8,128)S(1)}, f32[128,128]{1,0:T(8,128)S(1)}, u32[]{:S(2)}, u32[]{:S(2)}) collective-permute-start(f32[128,128]{1,0:T(8,128)S(1)} %add.16), channel_id=1, source_target_pairs={{0,17},{1,16},{2,19},{3,18},{4,21},{5,20},{6,23},{7,22},{8,25},{9,... | collective-permute-start | bytes 196616 | tf_op jit(solution)/shard_map/ppermute | solution.py:268
  33.7 5.5 %collective-permute-start.6 = (f32[128,128]{1,0:T(8,128)S(1)}, f32[128,128]{1,0:T(8,128)S(1)}, u32[]{:S(2)}, u32[]{:S(2)}) collective-permute-start(f32[128,128]{1,0:T(8,128)S(1)} %add.16), channel_id=1, source_target_pairs={{0,16},{1,17},{2,18},{3,19},{4,20},{5,21},{6,22},{7,23},{8,24},{9,... | collective-permute-start | bytes 196616 | tf_op jit(solution)/shard_map/ppermute | solution.py:268
  34.2 5.0 %collective-permute-start.5 = (f32[128,128]{1,0:T(8,128)S(1)}, f32[128,128]{1,0:T(8,128)S(1)}, u32[]{:S(2)}, u32[]{:S(2)}) collective-permute-start(f32[128,128]{1,0:T(8,128)S(1)} %add.16), channel_id=1, source_target_pairs={{0,1},{1,0},{2,3},{3,2},{4,5},{5,4},{6,7},{7,6},{8,9},{9,8},{10,11... | collective-permute-start | bytes 196616 | tf_op jit(solution)/shard_map/ppermute | solution.py:268
  34.7 1.2 %collective-permute-start.8 = (bf16[64,256]{1,0:T(8,128)(2,1)S(1)}, bf16[64,256]{1,0:T(8,128)(2,1)S(1)}, u32[]{:S(2)}, u32[]{:S(2)}) collective-permute-start(bf16[64,256]{1,0:T(8,128)(2,1)S(1)} %collective-permute-done.2.row_ref), channel_id=1, source_target_pairs={{0,8},{1,9},{2,10},{3,11},{4,12},{5,13},{6,14},{7,15},{8,0},{9,1},... | collective-permute-start | bytes 98312 | tf_op jit(solution)/shard_map/ppermute | solution.py:268
  37.2 1.9 %copy-start.4 = (bf16[256,8192]{1,0:T(8,128)(2,1)}, bf16[256,8192]{1,0:T(8,128)(2,1)S(1)}, u32[]{:S(2)}) copy-start(bf16[256,8192]{1,0:T(8,128)(2,1)S(1)} %kernel_tile.5.refs_3_) | copy-start | bytes 12582916
  39.3 1.6 %collective-permute-start.9 = (f32[512,128]{1,0:T(8,128)S(1)}, f32[512,128]{1,0:T(8,128)S(1)}, u32[]{:S(2)}, u32[]{:S(2)}) collective-permute-start(f32[512,128]{1,0:T(8,128)S(1)} %pad_maximum_fusion), channel_id=1, source_target_pairs={{0,8},{1,9},{2,10},{3,11},{4,12},{5,13},{6,14},{7,15},{8,0},{9,1},... | collective-permute-start | bytes 786440 | tf_op jit(solution)/shard_map/ppermute | solution.py:268
  46.9 2.2 %copy-start.1 = (bf16[256,8192]{1,0:T(8,128)(2,1)S(1)}, bf16[256,8192]{1,0:T(8,128)(2,1)}, u32[]{:S(2)}) copy-start(bf16[256,8192]{1,0:T(8,128)(2,1)} %copy-done) | copy-start | bytes 12582916
  49.1 2.2 %copy-start.3 = (bf16[256,8192]{1,0:T(8,128)(2,1)S(1)}, bf16[256,8192]{1,0:T(8,128)(2,1)}, u32[]{:S(2)}) copy-start(bf16[256,8192]{1,0:T(8,128)(2,1)} %copy-done.2) | copy-start | bytes 12582916
  51.3 2.2 %copy-start.5 = (bf16[256,8192]{1,0:T(8,128)(2,1)S(1)}, bf16[256,8192]{1,0:T(8,128)(2,1)}, u32[]{:S(2)}) copy-start(bf16[256,8192]{1,0:T(8,128)(2,1)} %copy-done.4) | copy-start | bytes 12582916
  53.5 2.2 %copy-start.7 = (bf16[256,8192]{1,0:T(8,128)(2,1)S(1)}, bf16[256,8192]{1,0:T(8,128)(2,1)}, u32[]{:S(2)}) copy-start(bf16[256,8192]{1,0:T(8,128)(2,1)} %copy-done.6) | copy-start | bytes 12582916

commit v3 on v1

v3 whole, which is shorter than its diff:
```python
import functools
import math

import jax
import jax.numpy as jnp
from jax import lax
from jax.experimental import pallas as pl
from jax.experimental.pallas import tpu as pltpu
from jax.sharding import PartitionSpec as P

F32 = jnp.float32
BF16 = jnp.bfloat16
EXACT = lax.Precision.HIGHEST
VMEM_BYTES = 40 << 20
TILE_BYTES = 16 << 20


def contract(a, b, a_dim, b_dim, precision=None):
    dims = (((a_dim,), (b_dim,)), ((), ()))
    return lax.dot_general(a, b, dims, precision=precision, preferred_element_type=F32)


def widened(points, scale, factor, first):
    wide = points.astype(F32)
    terms_sum = -scale * jnp.sum(wide * wide, axis=0, keepdims=True)
    place = lax.broadcasted_iota(jnp.int32, (16, points.shape[1]), 0)
    terms_at, ones_at = (0, 3) if first else (3, 0)
    extra = jnp.where((place >= ones_at) & (place < ones_at + 3), 1.0, 0.0)
    for k in range(3):
        term = terms_sum.astype(BF16).astype(F32)
        extra = jnp.where(place == terms_at + k, term, extra)
        terms_sum = terms_sum - term
    return jnp.concatenate([(wide * factor).astype(BF16), extra.astype(BF16)], axis=0)


def exponent(left, right):
    return jnp.exp(contract(left, right, 1, 0)).astype(BF16)


def chunk_width(col_dev):
    return math.gcd(col_dev, 1024)


def sketch_body(
    scale, half_ref, row_hbm, col_hbm, panel_hbm, keep_ref, send_ref,
    row_ref, col_ref, panel_ref, tile_ref, total_ref, row_sem, col_sem, panel_sem,
):
    row_copy = pltpu.make_async_copy(row_hbm, row_ref, row_sem)
    col_copy = pltpu.make_async_copy(col_hbm, col_ref, col_sem)
    panel_copy = pltpu.make_async_copy(panel_hbm, panel_ref, panel_sem)
    row_copy.start()
    col_copy.start()
    panel_copy.start()
    chunk = chunk_width(col_ref.shape[1])
    row_copy.wait()
    left = widened(row_ref[...], scale, 2.0 * scale, True).T
    col_copy.wait()
    for c in range(0, col_ref.shape[1], chunk):
        right = widened(col_ref[:, c : c + chunk], scale, 1.0, False)
        tile_ref[:, c : c + chunk] = exponent(left, right)
    panel_copy.wait()
    total_ref[...] = contract(tile_ref[...], panel_ref[...], 1, 0)
    half, rows = half_ref[0], keep_ref.shape[0]
    keep_ref[...] = total_ref[pl.ds(pl.multiple_of(half * rows, rows), rows), :]
    send_ref[...] = total_ref[pl.ds(pl.multiple_of((1 - half) * rows, rows), rows), :]


def sketch_halves(row_points, col_points, panel, half):
    dim, rows = row_points.shape
    col_dev, width = panel.shape
    part = jax.ShapeDtypeStruct((rows // 2, width), F32)
    whole, remote = pl.BlockSpec(memory_space=pltpu.VMEM), pl.BlockSpec(memory_space=pltpu.HBM)
    return pl.pallas_call(
        functools.partial(sketch_body, 2.0 / dim),
        in_specs=[pl.BlockSpec(memory_space=pltpu.SMEM), remote, remote, remote],
        out_specs=[whole, whole],
        out_shape=[part, part],
        scratch_shapes=[
            pltpu.VMEM((dim, rows), BF16),
            pltpu.VMEM((dim, col_dev), BF16),
            pltpu.VMEM((col_dev, width), BF16),
            pltpu.VMEM((rows, col_dev), BF16),
            pltpu.VMEM((rows, width), F32),
            pltpu.SemaphoreType.DMA,
            pltpu.SemaphoreType.DMA,
            pltpu.SemaphoreType.DMA,
        ],
        compiler_params=pltpu.CompilerParams(vmem_limit_bytes=VMEM_BYTES),
        name="sketch",
    )(half, *[pltpu.with_memory_space_constraint(a, pltpu.HBM) for a in (row_points, col_points, panel)])


def inverse_factor(gram, after_step):
    n = gram.shape[0]
    tiles = n // 8
    left = [gram[8 * t : 8 * t + 8, :] for t in range(tiles)]
    lane = lax.broadcasted_iota(jnp.int32, (8, n), 1)
    sub = lax.broadcasted_iota(jnp.int32, (8, n), 0)
    right = [jnp.where(lane == sub + 8 * t, 1.0, 0.0) for t in range(tiles)]
    inverse = []

    def row(tile, k):
        return jnp.broadcast_to(tile[k : k + 1, :], (8, n))

    def column(tile, k):
        return jnp.broadcast_to(tile[:, k : k + 1], (8, n))

    def weighted(weights, rows):
        pairs = [w * r for w, r in zip(weights, rows)]
        while len(pairs) > 1:
            pairs = [a + b for a, b in zip(pairs[::2], pairs[1::2])]
        return pairs[0]

    for b in range(tiles):
        upper, lower = left[b], right[b]
        block = [column(upper, 8 * b + k) for k in range(8)]
        root, below = [], []
        for k in range(8):
            root.append(lax.rsqrt(row(block[k], k)))
            step = jnp.where(sub > k, block[k] * root[k], 0.0)
            below.append({j: row(step, j) for j in range(k + 1, 8)})
            for j in range(k + 1, 8):
                block[j] = block[j] - step * below[k][j]
            upper_row, lower_row = row(upper, k) * root[k], row(lower, k) * root[k]
            upper, lower = upper - step * upper_row, lower - step * lower_row
        scales = root[0]
        for k in range(1, 8):
            scales = jnp.where(sub == k, root[k], scales)
        upper, lower = upper * scales, lower * scales
        inverse.append(lower)
        after_step((b + 1) / tiles)
        upper_rows = [row(upper, k) for k in range(8)]
        lower_rows = [row(lower, k) for k in range(8)]
        for t in range(b + 1, tiles):
            entry = [column(left[t], 8 * b + k) for k in range(8)]
            for k in range(8):
                entry[k] = entry[k] * root[k]
                for j in range(k + 1, 8):
                    entry[j] = entry[j] - entry[k] * below[k][j]
            left[t] = left[t] - weighted(entry, upper_rows)
            right[t] = right[t] - weighted(entry, lower_rows)
    return inverse


def finish_body(
    scale, norm, stored, rank_ref, sketch_ref, row_ref, col_ref, left_basis_ref, out_ref, inverse_ref, left_ref, tile_ref
):
    blocks, _, rows = row_ref.shape
    total, col_dev = left_ref.shape[0], col_ref.shape[1]
    chunk = tile_ref.shape[1] if not stored else chunk_width(col_dev) // 2
    sketch = sketch_ref[...]
    gram = contract(sketch, sketch, 0, 0, EXACT)
    for k in range(blocks):
        left_ref[k * rows : (k + 1) * rows, :] = widened(row_ref[k], scale, 2.0 * scale, True).T
    work = [(k, c) for c in range(0, col_dev, chunk) for k in range(blocks)] if stored else []
    done = 0

    def tiles_until(share):
        nonlocal done
        upto = int(len(work) * share)
        for k, c in work[done:upto]:
            at = slice(k * rows, (k + 1) * rows)
            right = widened(col_ref[:, c : c + chunk], scale, 1.0, False)
            tile_ref[at, c : c + chunk] = exponent(left_ref[at, :], right)
        done = upto

    for t, tile in enumerate(inverse_factor(gram, tiles_until)):
        inverse_ref[8 * t : 8 * t + 8, :] = tile
    left_basis_ref[...] = contract(sketch_ref[:rows, :], inverse_ref[...], 1, 1, EXACT) * norm
    count = out_ref.shape[0]
    mine = inverse_ref[pl.ds(pl.multiple_of(rank_ref[0] * count, count), count), :]
    ranks = contract(mine, sketch_ref[...], 1, 1, EXACT).astype(BF16)
    if stored:
        for c in range(0, col_dev, 2 * chunk):
            at = slice(c, c + 2 * chunk)
            out_ref[:, at] = contract(ranks, tile_ref[:, at], 1, 0).astype(BF16)
    else:

        @pl.loop(0, col_dev // chunk)
        def _(k):
            at = pl.ds(pl.multiple_of(k * chunk, chunk), chunk)
            tile_ref[...] = exponent(left_ref[...], widened(col_ref[:, at], scale, 1.0, False))
            out_ref[:, at] = contract(ranks, tile_ref[...], 1, 0).astype(BF16)


def finish(index, sketch, row_blocks, col_points):
    total, width = sketch.shape
    blocks, dim, rows = row_blocks.shape
    col_dev = col_points.shape[1]
    stored = total * col_dev * 2 <= TILE_BYTES
    count = width // blocks
    whole = pl.BlockSpec(memory_space=pltpu.VMEM)
    return pl.pallas_call(
        functools.partial(finish_body, 2.0 / dim, math.sqrt(total), stored),
        in_specs=[pl.BlockSpec(memory_space=pltpu.SMEM), whole, whole, whole],
        out_specs=[whole, whole],
        out_shape=[jax.ShapeDtypeStruct((rows, width), F32), jax.ShapeDtypeStruct((count, col_dev), BF16)],
        scratch_shapes=[
            pltpu.VMEM((width, width), F32),
            pltpu.VMEM((total, dim + 16), BF16),
            pltpu.VMEM((total, col_dev if stored else math.gcd(col_dev, 512)), BF16),
        ],
        compiler_params=pltpu.CompilerParams(vmem_limit_bytes=VMEM_BYTES),
        name="finish",
    )(index, sketch, row_blocks, col_points)


def swapped(value, row_bit, col_bit):
    rows, cols = lax.axis_size("row"), lax.axis_size("col")
    pairs = [(r * cols + c, (r ^ row_bit) * cols + (c ^ col_bit)) for r in range(rows) for c in range(cols)]
    return lax.ppermute(value, ("row", "col"), pairs)


def bits_down(size):
    return [1 << k for k in reversed(range(size.bit_length() - 1))]


def per_device(row_points, col_points, random_panel):
    row_count, col_count = lax.axis_size("row"), lax.axis_size("col")
    half = lax.axis_index("col") % 2
    row_bits, col_bits = bits_down(row_count), bits_down(col_count)
    keep, send = sketch_halves(row_points, col_points, random_panel, half.reshape(1))

    def both(blocks, moved):
        return jnp.concatenate([blocks, moved], axis=0)

    first = half == 0
    row_blocks = lax.optimization_barrier((row_points, keep))[0][None]
    moved = (swapped(send, 0, 1), swapped(row_blocks, row_bits[0], 0))
    moved_part, moved_blocks = lax.optimization_barrier(moved)
    part, row_blocks = keep + moved_part, both(row_blocks, moved_blocks)
    for bit in reversed(col_bits[:-1]):
        part = part + swapped(part, 0, bit)

    def ordered(mine, other):
        return both(jnp.where(first, mine, other), jnp.where(first, other, mine))

    bit = row_bits[0]
    near, far, cross = swapped(part, 0, 1), swapped(part, bit, 0), swapped(part, bit, 1)
    sketch = both(ordered(part, near), ordered(far, cross))
    for bit in row_bits[1:]:
        sketch, row_blocks = [both(a, swapped(a, bit, 0)) for a in (sketch, row_blocks)]
    return finish(lax.axis_index("row").reshape(1), sketch, row_blocks, col_points)


def solution(mesh):
    placed = (P(None, "row"), P(None, "col"), P("col", None))
    return jax.shard_map(
        per_device,
        mesh=mesh,
        in_specs=placed,
        out_specs=(P("row", None), P("row", "col")),
        check_vma=False,
    )
```

time: 48 us -> 41.1 us (0.86)
  local copies, waits for them, and re-layouts: 3.58 us -> 0.03 us
  Pallas kernels: 16.8 us -> 14.6 us
  waiting for transfers between devices: 14.1 us -> 12.4 us
  starting transfers between devices: 12.4 us -> 13 us
    unnamed x10 -> x4, local copies, waits for them, and re-layouts: 3.58 us -> 0.01 us
    pallas_call x3 -> x2, Pallas kernels: 16.8 us -> 14.6 us  [the longest x1 10.8 us: finish(): pl.pallas_call(functools.partial(finish_body, 2.0 / dim, math.sqrt(total)...]
    ppermute x8 -> x9, waiting for transfers between devices: 14.1 us -> 12.4 us  [swapped(): return lax.ppermute(value, ('row', 'col'), pairs)]
    ppermute x8 -> x9, starting transfers between devices: 12.4 us -> 13 us  [swapped(): return lax.ppermute(value, ('row', 'col'), pairs)]
  transfers between devices with their start and end apart: 8 -> 9, of which waited for: 7 -> 7; matrix products, arithmetic and copies ran while one was open for 0% -> 0% of each run, Pallas kernels for 0% -> 0%
where the time goes in v3:
time: 41.1 us; the launch traced here: 40.9 us
  Pallas kernels  14.6 us (36%)
  starting transfers between devices  13 us (32%)
  waiting for transfers between devices  12.4 us (30%)
  between operations  0.76 us (2%)
    ppermute x9, starting transfers between devices, swapped(): return lax.ppermute(value, ('row', 'col'), pairs)  13 us
    ppermute x9, waiting for transfers between devices, swapped(): return lax.ppermute(value, ('row', 'col'), pairs)  12.4 us
    pallas_call x1, Pallas kernels, finish(): pl.pallas_call(functools.partial(finish_body, 2.0 / dim, math.sqrt(total)...  10.8 us
    pallas_call x1, Pallas kernels, sketch_halves(): pl.pallas_call(functools.partial(sketch_body, 2.0 / dim), in_specs=[pl.Bl...  3.82 us
  transfers between devices with their start and end apart: 9, of which 7 were waited for; matrix products, arithmetic and copies ran while one was open for 0% of the time, Pallas kernels for 0%

profile of v3, /device:TPU:0, one launch (start us, length us, event | category | flops | bytes accessed | tf_op | source)
XLA Modules:
  0.0 40.9 jit_solution(538605654566253789)
XLA Ops:
  0.6 0.0 copy-start.1
  0.7 3.8 %sketch.1 = (f32[128,128]{1,0:T(8,128)S(1)}, f32[128,128]{1,0:T(8,128)S(1)}) custom-call(s32[1]{0:T(128)} %bitcast.1.half_ref, bf16[64,256]{1,0:T(8,128)(2,1)} %row_hbm.1, bf16[64,8192]{1,0:T(8,128)(2,1)} %col_ref.1, bf16[8192,128]{1,0:T(8,128)(2,1)} %panel_hbm.1), custom_call_target="tpu_custom_call" | custom-call | tf_op jit(solution)/shard_map/sketch/pallas_call | solution.py:73
  4.5 0.0 copy-start
  4.5 3.0 %collective-permute-start = (f32[128,128]{1,0:T(8,128)S(1)}, f32[128,128]{1,0:T(8,128)S(1)}, u32[]{:S(2)}, u32[]{:S(2)}) collective-permute-start(f32[128,128]{1,0:T(8,128)S(1)} %get-tuple-element.8), channel_id=1, source_target_pairs={{0,1},{1,0},{2,3},{3,2},{4,5},{5,4},{6,7},{7,6},{8,9},{9,8},{10,11... | collective-permute-start | bytes 196616 | tf_op jit(solution)/shard_map/ppermute | solution.py:211
  7.5 0.0 copy-done.1
  7.5 1.5 %collective-permute-start.1 = (bf16[1,64,256]{2,1,0:T(8,128)(2,1)S(1)}, bf16[1,64,256]{2,1,0:T(8,128)(2,1)S(1)}, u32[]{:S(2)}, u32[]{:S(2)}) collective-permute-start(bf16[1,64,256]{2,1,0:T(8,128)(2,1)S(1)} %bitcast.3), channel_id=1, source_target_pairs={{0,16},{1,17},{2,18},{3,19},{4,20},{5,21},{6,22},{7,23},{8,24},{9,... | collective-permute-start | bytes 98312 | tf_op jit(solution)/shard_map/ppermute | solution.py:211
  9.0 2.4 %collective-permute-done.1 = bf16[1,64,256]{2,1,0:T(8,128)(2,1)S(1)} collective-permute-done((bf16[1,64,256]{2,1,0:T(8,128)(2,1)S(1)}, bf16[1,64,256]{2,1,0:T(8,128)(2,1)S(1)}, u32[]{:S(2)}, u32[]{:S(2)}) %collective-permute-start.1) | collective-permute-done | bytes 32800 | tf_op jit(solution)/shard_map/ppermute | solution.py:211
  11.4 0.0 collective-permute-done
  11.4 1.6 %collective-permute-start.2 = (f32[128,128]{1,0:T(8,128)S(1)}, f32[128,128]{1,0:T(8,128)S(1)}, u32[]{:S(2)}, u32[]{:S(2)}) collective-permute-start(f32[128,128]{1,0:T(8,128)S(1)} %add.14), channel_id=1, source_target_pairs={{0,2},{1,3},{2,0},{3,1},{4,6},{5,7},{6,4},{7,5},{8,10},{9,11},{10,... | collective-permute-start | bytes 196616 | tf_op jit(solution)/shard_map/ppermute | solution.py:211
  13.1 2.7 %collective-permute-done.2 = f32[128,128]{1,0:T(8,128)S(1)} collective-permute-done((f32[128,128]{1,0:T(8,128)S(1)}, f32[128,128]{1,0:T(8,128)S(1)}, u32[]{:S(2)}, u32[]{:S(2)}) %collective-permute-start.2) | collective-permute-done | bytes 65568 | tf_op jit(solution)/shard_map/ppermute | solution.py:211
  15.8 2.7 %collective-permute-start.3 = (f32[128,128]{1,0:T(8,128)S(1)}, f32[128,128]{1,0:T(8,128)S(1)}, u32[]{:S(2)}, u32[]{:S(2)}) collective-permute-start(f32[128,128]{1,0:T(8,128)S(1)} %add.15), channel_id=1, source_target_pairs={{0,4},{1,5},{2,6},{3,7},{4,0},{5,1},{6,2},{7,3},{8,12},{9,13},{10,... | collective-permute-start | bytes 196616 | tf_op jit(solution)/shard_map/ppermute | solution.py:211
  18.4 2.6 %collective-permute-done.3 = f32[128,128]{1,0:T(8,128)S(1)} collective-permute-done((f32[128,128]{1,0:T(8,128)S(1)}, f32[128,128]{1,0:T(8,128)S(1)}, u32[]{:S(2)}, u32[]{:S(2)}) %collective-permute-start.3) | collective-permute-done | bytes 65568 | tf_op jit(solution)/shard_map/ppermute | solution.py:211
  21.0 0.4 %collective-permute-start.4 = (f32[128,128]{1,0:T(8,128)S(1)}, f32[128,128]{1,0:T(8,128)S(1)}, u32[]{:S(2)}, u32[]{:S(2)}) collective-permute-start(f32[128,128]{1,0:T(8,128)S(1)} %add.16), channel_id=1, source_target_pairs={{0,1},{1,0},{2,3},{3,2},{4,5},{5,4},{6,7},{7,6},{8,9},{9,8},{10,11... | collective-permute-start | bytes 196616 | tf_op jit(solution)/shard_map/ppermute | solution.py:211
  21.4 1.7 %collective-permute-start.5 = (f32[128,128]{1,0:T(8,128)S(1)}, f32[128,128]{1,0:T(8,128)S(1)}, u32[]{:S(2)}, u32[]{:S(2)}) collective-permute-start(f32[128,128]{1,0:T(8,128)S(1)} %add.16), channel_id=1, source_target_pairs={{0,16},{1,17},{2,18},{3,19},{4,20},{5,21},{6,22},{7,23},{8,24},{9,... | collective-permute-start | bytes 196616 | tf_op jit(solution)/shard_map/ppermute | solution.py:211
  23.1 1.4 %collective-permute-start.6 = (f32[128,128]{1,0:T(8,128)S(1)}, f32[128,128]{1,0:T(8,128)S(1)}, u32[]{:S(2)}, u32[]{:S(2)}) collective-permute-start(f32[128,128]{1,0:T(8,128)S(1)} %add.16), channel_id=1, source_target_pairs={{0,17},{1,16},{2,19},{3,18},{4,21},{5,20},{6,23},{7,22},{8,25},{9,... | collective-permute-start | bytes 196616 | tf_op jit(solution)/shard_map/ppermute | solution.py:211
  24.6 0.8 %collective-permute-done.4 = f32[128,128]{1,0:T(8,128)S(1)} collective-permute-done((f32[128,128]{1,0:T(8,128)S(1)}, f32[128,128]{1,0:T(8,128)S(1)}, u32[]{:S(2)}, u32[]{:S(2)}) %collective-permute-start.4) | collective-permute-done | bytes 65568 | tf_op jit(solution)/shard_map/ppermute | solution.py:211
  25.4 0.3 collective-permute-done.5
  25.7 2.6 %collective-permute-done.6 = f32[128,128]{1,0:T(8,128)S(1)} collective-permute-done((f32[128,128]{1,0:T(8,128)S(1)}, f32[128,128]{1,0:T(8,128)S(1)}, u32[]{:S(2)}, u32[]{:S(2)}) %collective-permute-start.6) | collective-permute-done | bytes 65568 | tf_op jit(solution)/shard_map/ppermute | solution.py:211
  28.4 0.1 collective-permute-start.7
  28.5 0.5 %collective-permute-start.8 = (bf16[2,64,256]{2,1,0:T(8,128)(2,1)S(1)}, bf16[2,64,256]{2,1,0:T(8,128)(2,1)S(1)}, u32[]{:S(2)}, u32[]{:S(2)}) collective-permute-start(bf16[2,64,256]{2,1,0:T(8,128)(2,1)S(1)} %pad_maximum_fusion.2), channel_id=1, source_target_pairs={{0,8},{1,9},{2,10},{3,11},{4,12},{5,13},{6,14},{7,15},{8,0},{9,1},... | collective-permute-start | bytes 196616 | tf_op jit(solution)/shard_map/ppermute | solution.py:211
  29.0 1.1 %collective-permute-done.8 = bf16[2,64,256]{2,1,0:T(8,128)(2,1)S(1)} collective-permute-done((bf16[2,64,256]{2,1,0:T(8,128)(2,1)S(1)}, bf16[2,64,256]{2,1,0:T(8,128)(2,1)S(1)}, u32[]{:S(2)}, u32[]{:S(2)}) %collective-permute-start.8) | collective-permute-done | bytes 65568 | tf_op jit(solution)/shard_map/ppermute | solution.py:211
  30.1 0.0 collective-permute-done.7
  30.1 0.0 copy-done
  30.1 10.8 %finish.1 = (f32[256,128]{1,0:T(8,128)}, bf16[32,8192]{1,0:T(8,128)(2,1)}) custom-call(s32[1]{0:T(128)} %bitcast.rank_ref, f32[1024,128]{1,0:T(8,128)S(1)} %constant_dynamic-update-slice_fusion.sketch_ref, bf16[4,64,256]{2,1,0:T(8,128)(2,1)S(1)} %pad_maximum_fusion.1.row_ref, bf16[64,8192]{1,0:T(8,128)(2,1)S(1)} %copy-done), custom_call_target="tpu_custom_call" | custom-call | tf_op jit(solution)/shard_map/finish/pallas_call | solution.py:193
  (11 shorter events, 0.1 us)
Async XLA Ops:
  0.6 6.9 %copy-start.1 = (bf16[64,256]{1,0:T(8,128)(2,1)S(1)}, bf16[64,256]{1,0:T(8,128)(2,1)}, u32[]{:S(2)}) copy-start(bf16[64,256]{1,0:T(8,128)(2,1)} %row_hbm.1) | copy-start | bytes 98308
  4.5 25.6 %copy-start = (bf16[64,8192]{1,0:T(8,128)(2,1)S(1)}, bf16[64,8192]{1,0:T(8,128)(2,1)}, u32[]{:S(2)}) copy-start(bf16[64,8192]{1,0:T(8,128)(2,1)} %col_ref.1) | copy-start | bytes 3145732
  4.5 6.9 %collective-permute-start = (f32[128,128]{1,0:T(8,128)S(1)}, f32[128,128]{1,0:T(8,128)S(1)}, u32[]{:S(2)}, u32[]{:S(2)}) collective-permute-start(f32[128,128]{1,0:T(8,128)S(1)} %get-tuple-element.8), channel_id=1, source_target_pairs={{0,1},{1,0},{2,3},{3,2},{4,5},{5,4},{6,7},{7,6},{8,9},{9,8},{10,11... | collective-permute-start | bytes 196616 | tf_op jit(solution)/shard_map/ppermute | solution.py:211
  7.5 3.9 %collective-permute-start.1 = (bf16[1,64,256]{2,1,0:T(8,128)(2,1)S(1)}, bf16[1,64,256]{2,1,0:T(8,128)(2,1)S(1)}, u32[]{:S(2)}, u32[]{:S(2)}) collective-permute-start(bf16[1,64,256]{2,1,0:T(8,128)(2,1)S(1)} %bitcast.3), channel_id=1, source_target_pairs={{0,16},{1,17},{2,18},{3,19},{4,20},{5,21},{6,22},{7,23},{8,24},{9,... | collective-permute-start | bytes 98312 | tf_op jit(solution)/shard_map/ppermute | solution.py:211
  11.4 4.3 %collective-permute-start.2 = (f32[128,128]{1,0:T(8,128)S(1)}, f32[128,128]{1,0:T(8,128)S(1)}, u32[]{:S(2)}, u32[]{:S(2)}) collective-permute-start(f32[128,128]{1,0:T(8,128)S(1)} %add.14), channel_id=1, source_target_pairs={{0,2},{1,3},{2,0},{3,1},{4,6},{5,7},{6,4},{7,5},{8,10},{9,11},{10,... | collective-permute-start | bytes 196616 | tf_op jit(solution)/shard_map/ppermute | solution.py:211
  15.8 5.2 %collective-permute-start.3 = (f32[128,128]{1,0:T(8,128)S(1)}, f32[128,128]{1,0:T(8,128)S(1)}, u32[]{:S(2)}, u32[]{:S(2)}) collective-permute-start(f32[128,128]{1,0:T(8,128)S(1)} %add.15), channel_id=1, source_target_pairs={{0,4},{1,5},{2,6},{3,7},{4,0},{5,1},{6,2},{7,3},{8,12},{9,13},{10,... | collective-permute-start | bytes 196616 | tf_op jit(solution)/shard_map/ppermute | solution.py:211
  21.0 4.3 %collective-permute-start.4 = (f32[128,128]{1,0:T(8,128)S(1)}, f32[128,128]{1,0:T(8,128)S(1)}, u32[]{:S(2)}, u32[]{:S(2)}) collective-permute-start(f32[128,128]{1,0:T(8,128)S(1)} %add.16), channel_id=1, source_target_pairs={{0,1},{1,0},{2,3},{3,2},{4,5},{5,4},{6,7},{7,6},{8,9},{9,8},{10,11... | collective-permute-start | bytes 196616 | tf_op jit(solution)/shard_map/ppermute | solution.py:211
  21.4 4.3 %collective-permute-start.5 = (f32[128,128]{1,0:T(8,128)S(1)}, f32[128,128]{1,0:T(8,128)S(1)}, u32[]{:S(2)}, u32[]{:S(2)}) collective-permute-start(f32[128,128]{1,0:T(8,128)S(1)} %add.16), channel_id=1, source_target_pairs={{0,16},{1,17},{2,18},{3,19},{4,20},{5,21},{6,22},{7,23},{8,24},{9,... | collective-permute-start | bytes 196616 | tf_op jit(solution)/shard_map/ppermute | solution.py:211
  23.1 5.2 %collective-permute-start.6 = (f32[128,128]{1,0:T(8,128)S(1)}, f32[128,128]{1,0:T(8,128)S(1)}, u32[]{:S(2)}, u32[]{:S(2)}) collective-permute-start(f32[128,128]{1,0:T(8,128)S(1)} %add.16), channel_id=1, source_target_pairs={{0,17},{1,16},{2,19},{3,18},{4,21},{5,20},{6,23},{7,22},{8,25},{9,... | collective-permute-start | bytes 196616 | tf_op jit(solution)/shard_map/ppermute | solution.py:211
  28.4 1.7 %collective-permute-start.7 = (f32[512,128]{1,0:T(8,128)S(1)}, f32[512,128]{1,0:T(8,128)S(1)}, u32[]{:S(2)}, u32[]{:S(2)}) collective-permute-start(f32[512,128]{1,0:T(8,128)S(1)} %pad_maximum_fusion), channel_id=1, source_target_pairs={{0,8},{1,9},{2,10},{3,11},{4,12},{5,13},{6,14},{7,15},{8,0},{9,1},... | collective-permute-start | bytes 786440 | tf_op jit(solution)/shard_map/ppermute | solution.py:211
  28.5 1.6 %collective-permute-start.8 = (bf16[2,64,256]{2,1,0:T(8,128)(2,1)S(1)}, bf16[2,64,256]{2,1,0:T(8,128)(2,1)S(1)}, u32[]{:S(2)}, u32[]{:S(2)}) collective-permute-start(bf16[2,64,256]{2,1,0:T(8,128)(2,1)S(1)} %pad_maximum_fusion.2), channel_id=1, source_target_pairs={{0,8},{1,9},{2,10},{3,11},{4,12},{5,13},{6,14},{7,15},{8,0},{9,1},... | collective-permute-start | bytes 196616 | tf_op jit(solution)/shard_map/ppermute | solution.py:211

commit v4 on v3

--- a/solution.py
+++ b/solution.py
@@ -111,16 +111,23 @@
             pairs = [a + b for a, b in zip(pairs[::2], pairs[1::2])]
         return pairs[0]
 
+    def terms(x):
+        high = x.astype(BF16).astype(F32)
+        middle = (x - high).astype(BF16).astype(F32)
+        return high, middle, x - high - middle
+
     for b in range(tiles):
         upper, lower = left[b], right[b]
         block = [column(upper, 8 * b + k) for k in range(8)]
         root, below = [], []
         for k in range(8):
+            under = {j: row(block[k], j) for j in range(k + 1, 8)}
             root.append(lax.rsqrt(row(block[k], k)))
+            square = root[k] * root[k]
             step = jnp.where(sub > k, block[k] * root[k], 0.0)
-            below.append({j: row(step, j) for j in range(k + 1, 8)})
             for j in range(k + 1, 8):
-                block[j] = block[j] - step * below[k][j]
+                block[j] = block[j] - (block[k] * under[j]) * square
+            below.append({j: under[j] * root[k] for j in under})
             upper_row, lower_row = row(upper, k) * root[k], row(lower, k) * root[k]
             upper, lower = upper - step * upper_row, lower - step * lower_row
         scales = root[0]
@@ -129,16 +136,29 @@
         upper, lower = upper * scales, lower * scales
         inverse.append(lower)
         after_step((b + 1) / tiles)
-        upper_rows = [row(upper, k) for k in range(8)]
-        lower_rows = [row(lower, k) for k in range(8)]
-        for t in range(b + 1, tiles):
-            entry = [column(left[t], 8 * b + k) for k in range(8)]
-            for k in range(8):
-                entry[k] = entry[k] * root[k]
-                for j in range(k + 1, 8):
-                    entry[j] = entry[j] - entry[k] * below[k][j]
-            left[t] = left[t] - weighted(entry, upper_rows)
-            right[t] = right[t] - weighted(entry, lower_rows)
+        if b + 1 == tiles:
+            break
+        t = b + 1
+        entry = [column(left[t], 8 * b + k) for k in range(8)]
+        for k in range(8):
+            entry[k] = entry[k] * root[k]
+            for j in range(k + 1, 8):
+                entry[j] = entry[j] - entry[k] * below[k][j]
+        left[t] = left[t] - weighted(entry, [row(upper, k) for k in range(8)])
+        right[t] = right[t] - weighted(entry, [row(lower, k) for k in range(8)])
+        if t + 1 < tiles:
+            high, middle, low = terms(upper)
+            right_high, right_middle, right_low = terms(lower)
+            weights = jnp.concatenate([high, high, middle, high, low, middle], axis=0)
+            uppers = jnp.concatenate([high, middle, high, low, high, middle], axis=0)
+            lowers = jnp.concatenate(
+                [right_high, right_middle, right_high, right_low, right_high, right_middle], axis=0
+            )
+            both_sides = jnp.concatenate([uppers, lowers], axis=1).astype(BF16)
+            update = contract(weights.astype(BF16), both_sides, 0, 0)
+            for t in range(b + 2, tiles):
+                left[t] = left[t] - update[8 * t : 8 * t + 8, :n]
+                right[t] = right[t] - update[8 * t : 8 * t + 8, n:]
     return inverse
 
 
@@ -152,16 +172,15 @@
     gram = contract(sketch, sketch, 0, 0, EXACT)
     for k in range(blocks):
         left_ref[k * rows : (k + 1) * rows, :] = widened(row_ref[k], scale, 2.0 * scale, True).T
-    work = [(k, c) for c in range(0, col_dev, chunk) for k in range(blocks)] if stored else []
+    work = list(range(0, col_dev, chunk)) if stored else []
     done = 0
 
     def tiles_until(share):
         nonlocal done
         upto = int(len(work) * share)
-        for k, c in work[done:upto]:
-            at = slice(k * rows, (k + 1) * rows)
+        for c in work[done:upto]:
             right = widened(col_ref[:, c : c + chunk], scale, 1.0, False)
-            tile_ref[at, c : c + chunk] = exponent(left_ref[at, :], right)
+            tile_ref[:, c : c + chunk] = exponent(left_ref[...], right)
         done = upto
 
     for t, tile in enumerate(inverse_factor(gram, tiles_until)):
@@ -225,20 +244,24 @@
         return jnp.concatenate([blocks, moved], axis=0)
 
     first = half == 0
-    row_blocks = lax.optimization_barrier((row_points, keep))[0][None]
-    moved = (swapped(send, 0, 1), swapped(row_blocks, row_bits[0], 0))
-    moved_part, moved_blocks = lax.optimization_barrier(moved)
-    part, row_blocks = keep + moved_part, both(row_blocks, moved_blocks)
+
+    def ordered(mine, other, axis=0):
+        return jnp.concatenate([jnp.where(first, mine, other), jnp.where(first, other, mine)], axis=axis)
+
+    part = keep + swapped(send, 0, 1)
     for bit in reversed(col_bits[:-1]):
         part = part + swapped(part, 0, bit)
 
-    def ordered(mine, other):
-        return both(jnp.where(first, mine, other), jnp.where(first, other, mine))
-
-    bit = row_bits[0]
-    near, far, cross = swapped(part, 0, 1), swapped(part, bit, 0), swapped(part, bit, 1)
-    sketch = both(ordered(part, near), ordered(far, cross))
-    for bit in row_bits[1:]:
+    bit, *more_bits = row_bits
+    dim, rows = row_points.shape
+    points = lax.dynamic_slice_in_dim(row_points, half * (rows // 2), rows // 2, 1).astype(F32)
+    message, part = lax.optimization_barrier((both(part, points), part))
+    cross, far, near = swapped(message, bit, 1), swapped(message, bit, 0), swapped(part, 0, 1)
+    split = part.shape[0]
+    sketch = both(ordered(part, near), ordered(far[:split], cross[:split]))
+    moved = ordered(far[split:], cross[split:], 1).astype(BF16)
+    row_blocks = jnp.stack([row_points, moved])
+    for bit in more_bits:
         sketch, row_blocks = [both(a, swapped(a, bit, 0)) for a in (sketch, row_blocks)]
     return finish(lax.axis_index("row").reshape(1), sketch, row_blocks, col_points)
 

time: 41.1 us -> 40 us (0.973)
  Pallas kernels: 14.6 us -> 13.8 us
  starting transfers between devices: 13 us -> 12.4 us
    pallas_call x1, Pallas kernels: 10.8 us -> 9.99 us  [finish(): pl.pallas_call(functools.partial(finish_body, 2.0 / dim, math.sqrt(total)...]
    ppermute x9 -> x8, starting transfers between devices: 13 us -> 12.4 us  [swapped(): return lax.ppermute(value, ('row', 'col'), pairs)]
    ppermute x9 -> x8, waiting for transfers between devices: 12.4 us -> 12.6 us  [swapped(): return lax.ppermute(value, ('row', 'col'), pairs)]
  transfers between devices with their start and end apart: 9 -> 8, of which waited for: 7 -> 7; matrix products, arithmetic and copies ran while one was open for 0% -> 0% of each run, Pallas kernels for 0% -> 0%
where the time goes in v4:
time: 40 us; the launch traced here: 39.8 us
  Pallas kernels  13.8 us (34%)
  waiting for transfers between devices  12.6 us (32%)
  starting transfers between devices  12.4 us (31%)
  between operations  0.77 us (2%)
    ppermute x8, waiting for transfers between devices, swapped(): return lax.ppermute(value, ('row', 'col'), pairs)  12.6 us
    ppermute x8, starting transfers between devices, swapped(): return lax.ppermute(value, ('row', 'col'), pairs)  12.4 us
    pallas_call x1, Pallas kernels, finish(): pl.pallas_call(functools.partial(finish_body, 2.0 / dim, math.sqrt(total)...  9.99 us
    pallas_call x1, Pallas kernels, sketch_halves(): pl.pallas_call(functools.partial(sketch_body, 2.0 / dim), in_specs=[pl.Bl...  3.82 us
  transfers between devices with their start and end apart: 8, of which 7 were waited for; matrix products, arithmetic and copies ran while one was open for 0% of the time, Pallas kernels for 0%

profile of v4, /device:TPU:0, one launch (start us, length us, event | category | flops | bytes accessed | tf_op | source)
XLA Modules:
  0.0 39.8 jit_solution(5589935540674046805)
XLA Ops:
  0.6 0.0 copy-start.1
  0.7 3.8 %sketch.1 = (f32[128,128]{1,0:T(8,128)S(1)}, f32[128,128]{1,0:T(8,128)S(1)}) custom-call(s32[1]{0:T(128)} %bitcast.1.half_ref, bf16[64,256]{1,0:T(8,128)(2,1)} %row_hbm.1, bf16[64,8192]{1,0:T(8,128)(2,1)} %col_ref.1, bf16[8192,128]{1,0:T(8,128)(2,1)} %panel_hbm.1), custom_call_target="tpu_custom_call" | custom-call | tf_op jit(solution)/shard_map/sketch/pallas_call | solution.py:73
  4.5 0.0 copy-start
  4.5 3.0 %collective-permute-start = (f32[128,128]{1,0:T(8,128)S(1)}, f32[128,128]{1,0:T(8,128)S(1)}, u32[]{:S(2)}, u32[]{:S(2)}) collective-permute-start(f32[128,128]{1,0:T(8,128)S(1)} %get-tuple-element.7), channel_id=1, source_target_pairs={{0,1},{1,0},{2,3},{3,2},{4,5},{5,4},{6,7},{7,6},{8,9},{9,8},{10,11... | collective-permute-start | bytes 196616 | tf_op jit(solution)/shard_map/ppermute | solution.py:230
  7.5 2.2 %collective-permute-done = f32[128,128]{1,0:T(8,128)S(1)} collective-permute-done((f32[128,128]{1,0:T(8,128)S(1)}, f32[128,128]{1,0:T(8,128)S(1)}, u32[]{:S(2)}, u32[]{:S(2)}) %collective-permute-start) | collective-permute-done | bytes 65568 | tf_op jit(solution)/shard_map/ppermute | solution.py:230
  9.8 2.2 %collective-permute-start.1 = (f32[128,128]{1,0:T(8,128)S(1)}, f32[128,128]{1,0:T(8,128)S(1)}, u32[]{:S(2)}, u32[]{:S(2)}) collective-permute-start(f32[128,128]{1,0:T(8,128)S(1)} %add.17), channel_id=1, source_target_pairs={{0,2},{1,3},{2,0},{3,1},{4,6},{5,7},{6,4},{7,5},{8,10},{9,11},{10,... | collective-permute-start | bytes 196616 | tf_op jit(solution)/shard_map/ppermute | solution.py:230
  11.9 2.2 %collective-permute-done.1 = f32[128,128]{1,0:T(8,128)S(1)} collective-permute-done((f32[128,128]{1,0:T(8,128)S(1)}, f32[128,128]{1,0:T(8,128)S(1)}, u32[]{:S(2)}, u32[]{:S(2)}) %collective-permute-start.1) | collective-permute-done | bytes 65568 | tf_op jit(solution)/shard_map/ppermute | solution.py:230
  14.2 3.1 %collective-permute-start.2 = (f32[128,128]{1,0:T(8,128)S(1)}, f32[128,128]{1,0:T(8,128)S(1)}, u32[]{:S(2)}, u32[]{:S(2)}) collective-permute-start(f32[128,128]{1,0:T(8,128)S(1)} %add.18), channel_id=1, source_target_pairs={{0,4},{1,5},{2,6},{3,7},{4,0},{5,1},{6,2},{7,3},{8,12},{9,13},{10,... | collective-permute-start | bytes 196616 | tf_op jit(solution)/shard_map/ppermute | solution.py:230
  17.3 0.0 copy-done.1
  17.3 2.2 %collective-permute-done.2 = f32[128,128]{1,0:T(8,128)S(1)} collective-permute-done((f32[128,128]{1,0:T(8,128)S(1)}, f32[128,128]{1,0:T(8,128)S(1)}, u32[]{:S(2)}, u32[]{:S(2)}) %collective-permute-start.2) | collective-permute-done | bytes 65568 | tf_op jit(solution)/shard_map/ppermute | solution.py:230
  19.6 1.9 %collective-permute-start.3 = (f32[128,128]{1,0:T(8,128)S(1)}, f32[128,128]{1,0:T(8,128)S(1)}, u32[]{:S(2)}, u32[]{:S(2)}) collective-permute-start(f32[128,128]{1,0:T(8,128)S(1)} %add.19), channel_id=1, source_target_pairs={{0,1},{1,0},{2,3},{3,2},{4,5},{5,4},{6,7},{7,6},{8,9},{9,8},{10,11... | collective-permute-start | bytes 196616 | tf_op jit(solution)/shard_map/ppermute | solution.py:230
  21.4 1.5 %collective-permute-start.5 = (f32[192,128]{1,0:T(8,128)S(1)}, f32[192,128]{1,0:T(8,128)S(1)}, u32[]{:S(2)}, u32[]{:S(2)}) collective-permute-start(f32[192,128]{1,0:T(8,128)S(1)} %pad_maximum_fusion.2), channel_id=1, source_target_pairs={{0,17},{1,16},{2,19},{3,18},{4,21},{5,20},{6,23},{7,22},{8,25},{9,... | collective-permute-start | bytes 294920 | tf_op jit(solution)/shard_map/ppermute | solution.py:230
  22.9 0.2 collective-permute-start.4
  23.1 0.8 %collective-permute-done.3 = f32[128,128]{1,0:T(8,128)S(1)} collective-permute-done((f32[128,128]{1,0:T(8,128)S(1)}, f32[128,128]{1,0:T(8,128)S(1)}, u32[]{:S(2)}, u32[]{:S(2)}) %collective-permute-start.3) | collective-permute-done | bytes 65568 | tf_op jit(solution)/shard_map/ppermute | solution.py:230
  23.9 3.1 %collective-permute-done.5 = f32[192,128]{1,0:T(8,128)S(1)} collective-permute-done((f32[192,128]{1,0:T(8,128)S(1)}, f32[192,128]{1,0:T(8,128)S(1)}, u32[]{:S(2)}, u32[]{:S(2)}) %collective-permute-start.5) | collective-permute-done | bytes 98336 | tf_op jit(solution)/shard_map/ppermute | solution.py:230
  27.0 1.0 %collective-permute-done.4 = f32[192,128]{1,0:T(8,128)S(1)} collective-permute-done((f32[192,128]{1,0:T(8,128)S(1)}, f32[192,128]{1,0:T(8,128)S(1)}, u32[]{:S(2)}, u32[]{:S(2)}) %collective-permute-start.4) | collective-permute-done | bytes 98336 | tf_op jit(solution)/shard_map/ppermute | solution.py:230
  28.1 0.1 collective-permute-start.6
  28.2 0.5 %collective-permute-start.7 = (bf16[2,64,256]{2,1,0:T(8,128)(2,1)S(1)}, bf16[2,64,256]{2,1,0:T(8,128)(2,1)S(1)}, u32[]{:S(2)}, u32[]{:S(2)}) collective-permute-start(bf16[2,64,256]{2,1,0:T(8,128)(2,1)S(1)} %maximum_maximum_fusion), channel_id=1, source_target_pairs={{0,8},{1,9},{2,10},{3,11},{4,12},{5,13},{6,14},{7,15},{8,0},{9,1},... | collective-permute-start | bytes 196616 | tf_op jit(solution)/shard_map/ppermute | solution.py:230
  28.7 1.0 %collective-permute-done.7 = bf16[2,64,256]{2,1,0:T(8,128)(2,1)S(1)} collective-permute-done((bf16[2,64,256]{2,1,0:T(8,128)(2,1)S(1)}, bf16[2,64,256]{2,1,0:T(8,128)(2,1)S(1)}, u32[]{:S(2)}, u32[]{:S(2)}) %collective-permute-start.7) | collective-permute-done | bytes 65568 | tf_op jit(solution)/shard_map/ppermute | solution.py:230
  29.8 0.0 collective-permute-done.6
  29.8 0.0 copy-done
  29.8 10.0 %finish.1 = (f32[256,128]{1,0:T(8,128)}, bf16[32,8192]{1,0:T(8,128)(2,1)}) custom-call(s32[1]{0:T(128)} %bitcast.rank_ref, f32[1024,128]{1,0:T(8,128)S(1)} %constant_dynamic-update-slice_fusion.sketch_ref, bf16[4,64,256]{2,1,0:T(8,128)(2,1)S(1)} %pad_maximum_fusion.1.row_ref, bf16[64,8192]{1,0:T(8,128)(2,1)S(1)} %copy-done), custom_call_target="tpu_custom_call" | custom-call | tf_op jit(solution)/shard_map/finish/pallas_call | solution.py:212
  (14 shorter events, 0.2 us)
Async XLA Ops:
  0.6 16.7 %copy-start.1 = (bf16[64,256]{1,0:T(8,128)(2,1)S(1)}, bf16[64,256]{1,0:T(8,128)(2,1)}, u32[]{:S(2)}) copy-start(bf16[64,256]{1,0:T(8,128)(2,1)} %row_hbm.1) | copy-start | bytes 98308
  4.5 25.3 %copy-start = (bf16[64,8192]{1,0:T(8,128)(2,1)S(1)}, bf16[64,8192]{1,0:T(8,128)(2,1)}, u32[]{:S(2)}) copy-start(bf16[64,8192]{1,0:T(8,128)(2,1)} %col_ref.1) | copy-start | bytes 3145732
  4.5 5.2 %collective-permute-start = (f32[128,128]{1,0:T(8,128)S(1)}, f32[128,128]{1,0:T(8,128)S(1)}, u32[]{:S(2)}, u32[]{:S(2)}) collective-permute-start(f32[128,128]{1,0:T(8,128)S(1)} %get-tuple-element.7), channel_id=1, source_target_pairs={{0,1},{1,0},{2,3},{3,2},{4,5},{5,4},{6,7},{7,6},{8,9},{9,8},{10,11... | collective-permute-start | bytes 196616 | tf_op jit(solution)/shard_map/ppermute | solution.py:230
  9.8 4.4 %collective-permute-start.1 = (f32[128,128]{1,0:T(8,128)S(1)}, f32[128,128]{1,0:T(8,128)S(1)}, u32[]{:S(2)}, u32[]{:S(2)}) collective-permute-start(f32[128,128]{1,0:T(8,128)S(1)} %add.17), channel_id=1, source_target_pairs={{0,2},{1,3},{2,0},{3,1},{4,6},{5,7},{6,4},{7,5},{8,10},{9,11},{10,... | collective-permute-start | bytes 196616 | tf_op jit(solution)/shard_map/ppermute | solution.py:230
  14.2 5.3 %collective-permute-start.2 = (f32[128,128]{1,0:T(8,128)S(1)}, f32[128,128]{1,0:T(8,128)S(1)}, u32[]{:S(2)}, u32[]{:S(2)}) collective-permute-start(f32[128,128]{1,0:T(8,128)S(1)} %add.18), channel_id=1, source_target_pairs={{0,4},{1,5},{2,6},{3,7},{4,0},{5,1},{6,2},{7,3},{8,12},{9,13},{10,... | collective-permute-start | bytes 196616 | tf_op jit(solution)/shard_map/ppermute | solution.py:230
  19.6 4.3 %collective-permute-start.3 = (f32[128,128]{1,0:T(8,128)S(1)}, f32[128,128]{1,0:T(8,128)S(1)}, u32[]{:S(2)}, u32[]{:S(2)}) collective-permute-start(f32[128,128]{1,0:T(8,128)S(1)} %add.19), channel_id=1, source_target_pairs={{0,1},{1,0},{2,3},{3,2},{4,5},{5,4},{6,7},{7,6},{8,9},{9,8},{10,11... | collective-permute-start | bytes 196616 | tf_op jit(solution)/shard_map/ppermute | solution.py:230
  21.4 5.6 %collective-permute-start.5 = (f32[192,128]{1,0:T(8,128)S(1)}, f32[192,128]{1,0:T(8,128)S(1)}, u32[]{:S(2)}, u32[]{:S(2)}) collective-permute-start(f32[192,128]{1,0:T(8,128)S(1)} %pad_maximum_fusion.2), channel_id=1, source_target_pairs={{0,17},{1,16},{2,19},{3,18},{4,21},{5,20},{6,23},{7,22},{8,25},{9,... | collective-permute-start | bytes 294920 | tf_op jit(solution)/shard_map/ppermute | solution.py:230
  22.9 5.1 %collective-permute-start.4 = (f32[192,128]{1,0:T(8,128)S(1)}, f32[192,128]{1,0:T(8,128)S(1)}, u32[]{:S(2)}, u32[]{:S(2)}) collective-permute-start(f32[192,128]{1,0:T(8,128)S(1)} %pad_maximum_fusion.2), channel_id=1, source_target_pairs={{0,16},{1,17},{2,18},{3,19},{4,20},{5,21},{6,22},{7,23},{8,24},{9,... | collective-permute-start | bytes 294920 | tf_op jit(solution)/shard_map/ppermute | solution.py:230
  28.1 1.7 %collective-permute-start.6 = (f32[512,128]{1,0:T(8,128)S(1)}, f32[512,128]{1,0:T(8,128)S(1)}, u32[]{:S(2)}, u32[]{:S(2)}) collective-permute-start(f32[512,128]{1,0:T(8,128)S(1)} %pad_maximum_fusion), channel_id=1, source_target_pairs={{0,8},{1,9},{2,10},{3,11},{4,12},{5,13},{6,14},{7,15},{8,0},{9,1},... | collective-permute-start | bytes 786440 | tf_op jit(solution)/shard_map/ppermute | solution.py:230
  28.2 1.6 %collective-permute-start.7 = (bf16[2,64,256]{2,1,0:T(8,128)(2,1)S(1)}, bf16[2,64,256]{2,1,0:T(8,128)(2,1)S(1)}, u32[]{:S(2)}, u32[]{:S(2)}) collective-permute-start(bf16[2,64,256]{2,1,0:T(8,128)(2,1)S(1)} %maximum_maximum_fusion), channel_id=1, source_target_pairs={{0,8},{1,9},{2,10},{3,11},{4,12},{5,13},{6,14},{7,15},{8,0},{9,1},... | collective-permute-start | bytes 196616 | tf_op jit(solution)/shard_map/ppermute | solution.py:230

commit v5 on v3

--- a/solution.py
+++ b/solution.py
@@ -12,7 +12,7 @@
 BF16 = jnp.bfloat16
 EXACT = lax.Precision.HIGHEST
 VMEM_BYTES = 40 << 20
-TILE_BYTES = 16 << 20
+CHUNK = 512
 
 
 def contract(a, b, a_dim, b_dim, precision=None):
@@ -142,105 +142,174 @@
     return inverse
 
 
+def bf16_terms(x):
+    high = x.astype(BF16)
+    rest = x - high.astype(F32)
+    middle = rest.astype(BF16)
+    return high, middle, (rest - middle.astype(F32)).astype(BF16)
+
+
 def finish_body(
-    scale, norm, stored, rank_ref, sketch_ref, row_ref, col_ref, left_basis_ref, out_ref, inverse_ref, left_ref, tile_ref
+    scale, norm, chunk, rank_ref, sketch_ref, row_ref, col_ref, left_basis_ref, keep_ref, send_ref,
+    inverse_ref, left_ref, sketch_t_ref, *term_refs,
 ):
     blocks, _, rows = row_ref.shape
-    total, col_dev = left_ref.shape[0], col_ref.shape[1]
-    chunk = tile_ref.shape[1] if not stored else chunk_width(col_dev) // 2
     sketch = sketch_ref[...]
+    width = sketch.shape[1]
     gram = contract(sketch, sketch, 0, 0, EXACT)
+    high, middle, _ = bf16_terms(sketch)
+    sketch_t_ref[:width, :] = high.T
+    sketch_t_ref[width:, :] = middle.T
     for k in range(blocks):
         left_ref[k * rows : (k + 1) * rows, :] = widened(row_ref[k], scale, 2.0 * scale, True).T
-    work = [(k, c) for c in range(0, col_dev, chunk) for k in range(blocks)] if stored else []
-    done = 0
-
-    def tiles_until(share):
+    starts = list(range(0, col_ref.shape[1], chunk))
+    pending, done = [], 0
+
+    def finish_pending():
+        for c, tile in pending:
+            product = contract(sketch_t_ref[...], tile, 1, 0)
+            for ref, term in zip(term_refs, bf16_terms(product[:width] + product[width:])):
+                ref[:, c : c + chunk] = term
+        pending.clear()
+
+    def projected_until(share):
         nonlocal done
-        upto = int(len(work) * share)
-        for k, c in work[done:upto]:
-            at = slice(k * rows, (k + 1) * rows)
-            right = widened(col_ref[:, c : c + chunk], scale, 1.0, False)
-            tile_ref[at, c : c + chunk] = exponent(left_ref[at, :], right)
+        upto = int(len(starts) * share)
+        for c in starts[done:upto]:
+            finish_pending()
+            tile = exponent(left_ref[...], widened(col_ref[:, c : c + chunk], scale, 1.0, False))
+            pending.append((c, tile))
         done = upto
-
-    for t, tile in enumerate(inverse_factor(gram, tiles_until)):
+        if share == 1.0:
+            finish_pending()
+
+    for t, tile in enumerate(inverse_factor(gram, projected_until)):
         inverse_ref[8 * t : 8 * t + 8, :] = tile
     left_basis_ref[...] = contract(sketch_ref[:rows, :], inverse_ref[...], 1, 1, EXACT) * norm
-    count = out_ref.shape[0]
-    mine = inverse_ref[pl.ds(pl.multiple_of(rank_ref[0] * count, count), count), :]
-    ranks = contract(mine, sketch_ref[...], 1, 1, EXACT).astype(BF16)
-    if stored:
-        for c in range(0, col_dev, 2 * chunk):
-            at = slice(c, c + 2 * chunk)
-            out_ref[:, at] = contract(ranks, tile_ref[:, at], 1, 0).astype(BF16)
-    else:
-
-        @pl.loop(0, col_dev // chunk)
-        def _(k):
-            at = pl.ds(pl.multiple_of(k * chunk, chunk), chunk)
-            tile_ref[...] = exponent(left_ref[...], widened(col_ref[:, at], scale, 1.0, False))
-            out_ref[:, at] = contract(ranks, tile_ref[...], 1, 0).astype(BF16)
+    count = keep_ref.shape[0]
+    mine = [inverse_ref[pl.ds(pl.multiple_of(rank_ref[k] * count, count), count), :] for k in range(2)]
+    terms = bf16_terms(jnp.concatenate(mine, axis=0))
+    for c in range(0, col_ref.shape[1], 2 * chunk):
+        at = slice(c, c + 2 * chunk)
+        total = None
+        for k, ref in enumerate(term_refs):
+            stack = jnp.concatenate(terms[: 3 - k], axis=0)
+            product = contract(stack, ref[:, at], 1, 0)
+            for j in range(3 - k):
+                piece = product[2 * count * j : 2 * count * (j + 1)]
+                total = piece if total is None else total + piece
+        keep_ref[:, at] = total[:count].astype(BF16)
+        send_ref[:, at] = total[count:].astype(BF16)
 
 
 def finish(index, sketch, row_blocks, col_points):
     total, width = sketch.shape
     blocks, dim, rows = row_blocks.shape
     col_dev = col_points.shape[1]
-    stored = total * col_dev * 2 <= TILE_BYTES
-    count = width // blocks
+    part = jax.ShapeDtypeStruct((width // blocks, col_dev), BF16)
     whole = pl.BlockSpec(memory_space=pltpu.VMEM)
     return pl.pallas_call(
-        functools.partial(finish_body, 2.0 / dim, math.sqrt(total), stored),
+        functools.partial(finish_body, 2.0 / dim, math.sqrt(total), math.gcd(col_dev, CHUNK)),
         in_specs=[pl.BlockSpec(memory_space=pltpu.SMEM), whole, whole, whole],
-        out_specs=[whole, whole],
-        out_shape=[jax.ShapeDtypeStruct((rows, width), F32), jax.ShapeDtypeStruct((count, col_dev), BF16)],
+        out_specs=[whole, whole, whole],
+        out_shape=[jax.ShapeDtypeStruct((rows, width), F32), part, part],
         scratch_shapes=[
             pltpu.VMEM((width, width), F32),
             pltpu.VMEM((total, dim + 16), BF16),
-            pltpu.VMEM((total, col_dev if stored else math.gcd(col_dev, 512)), BF16),
+            pltpu.VMEM((2 * width, total), BF16),
+            *[pltpu.VMEM((width, col_dev), BF16)] * 3,
         ],
         compiler_params=pltpu.CompilerParams(vmem_limit_bytes=VMEM_BYTES),
         name="finish",
     )(index, sketch, row_blocks, col_points)
 
 
+def place_body(at_ref, part_ref, *refs):
+    out_hbm, sem = refs[-2:]
+    width = part_ref.shape[1]
+    at = pl.ds(pl.multiple_of(at_ref[0] * width, width), width)
+    copy = pltpu.make_async_copy(part_ref, out_hbm.at[:, at], sem)
+    copy.start()
+    copy.wait()
+
+
+def placed(part, at, out=None):
+    count, width = part.shape
+    remote = pl.BlockSpec(memory_space=pltpu.HBM)
+    specs = [pl.BlockSpec(memory_space=pltpu.SMEM), pl.BlockSpec(memory_space=pltpu.VMEM)]
+    operands = [at.reshape(1), part]
+    if out is not None:
+        specs.append(remote)
+        operands.append(out)
+    return pl.pallas_call(
+        place_body,
+        in_specs=specs,
+        out_specs=remote,
+        out_shape=jax.ShapeDtypeStruct((count, 2 * width), part.dtype),
+        scratch_shapes=[pltpu.SemaphoreType.DMA],
+        input_output_aliases={} if out is None else {2: 0},
+        compiler_params=pltpu.CompilerParams(vmem_limit_bytes=VMEM_BYTES),
+        cost_estimate=pl.CostEstimate(flops=0, bytes_accessed=4 * count * width, transcendentals=0),
+        name="placed",
+    )(*operands)
+
+
 def swapped(value, row_bit, col_bit):
     rows, cols = lax.axis_size("row"), lax.axis_size("col")
     pairs = [(r * cols + c, (r ^ row_bit) * cols + (c ^ col_bit)) for r in range(rows) for c in range(cols)]
     return lax.ppermute(value, ("row", "col"), pairs)
 
 
-def bits_down(size):
-    return [1 << k for k in reversed(range(size.bit_length() - 1))]
+def bits_up(size):
+    return [1 << k for k in range(size.bit_length() - 1)]
 
 
 def per_device(row_points, col_points, random_panel):
-    row_count, col_count = lax.axis_size("row"), lax.axis_size("col")
+    core_bit, *y_bits = bits_up(lax.axis_size("row"))
+    x_bit, *z_bits = bits_up(lax.axis_size("col"))
     half = lax.axis_index("col") % 2
-    row_bits, col_bits = bits_down(row_count), bits_down(col_count)
     keep, send = sketch_halves(row_points, col_points, random_panel, half.reshape(1))
 
-    def both(blocks, moved):
-        return jnp.concatenate([blocks, moved], axis=0)
-
-    first = half == 0
-    row_blocks = lax.optimization_barrier((row_points, keep))[0][None]
-    moved = (swapped(send, 0, 1), swapped(row_blocks, row_bits[0], 0))
-    moved_part, moved_blocks = lax.optimization_barrier(moved)
-    part, row_blocks = keep + moved_part, both(row_blocks, moved_blocks)
-    for bit in reversed(col_bits[:-1]):
+    def both(a, b, axis=0):
+        return jnp.concatenate([a, b], axis=axis)
+
+    def ordered(mine, other, axis=0):
+        return both(jnp.where(half == 0, mine, other), jnp.where(half == 0, other, mine), axis)
+
+    part = keep + swapped(send, 0, x_bit)
+    for bit in z_bits:
         part = part + swapped(part, 0, bit)
 
-    def ordered(mine, other):
-        return both(jnp.where(first, mine, other), jnp.where(first, other, mine))
-
-    bit = row_bits[0]
-    near, far, cross = swapped(part, 0, 1), swapped(part, bit, 0), swapped(part, bit, 1)
-    sketch = both(ordered(part, near), ordered(far, cross))
-    for bit in row_bits[1:]:
+    dim, rows = row_points.shape
+    points = lax.dynamic_slice_in_dim(row_points, half * (rows // 2), rows // 2, 1).astype(F32)
+    message = both(part, points)
+    y_bit = y_bits[-1]
+    near = swapped(part, core_bit, x_bit)
+    cross, far = swapped(message, y_bit, x_bit), swapped(message, core_bit | y_bit, 0)
+    split = part.shape[0]
+    held = jnp.concatenate([part, near, far[:split], cross[:split]])
+    held_points = jnp.stack([row_points, both(far[split:], cross[split:], 1).astype(BF16)])
+    there, there_points = swapped(held, core_bit, 0), swapped(held_points, core_bit, 0)
+    part, near, far, cross = held.reshape(4, split, -1)
+    part_there, near_there, far_there, cross_there = there.reshape(4, split, -1)
+    (points, far_points, cross_points), (points_there, far_points_there, cross_points_there) = [
+        (a[0], a[1][:, : rows // 2], a[1][:, rows // 2 :]) for a in (held_points, there_points)
+    ]
+    sketch = [ordered(part, near_there), ordered(part_there, near)]
+    row_blocks = [points, points_there]
+    sketch += [ordered(far, cross_there), ordered(far_there, cross)]
+    row_blocks += [ordered(far_points, cross_points_there, 1), ordered(far_points_there, cross_points, 1)]
+    sketch, row_blocks = jnp.concatenate(sketch), jnp.stack(row_blocks)
+    for bit in y_bits[:-1]:
         sketch, row_blocks = [both(a, swapped(a, bit, 0)) for a in (sketch, row_blocks)]
-    return finish(lax.axis_index("row").reshape(1), sketch, row_blocks, col_points)
+
+    row_at = lax.axis_index("row")
+    core = row_at % 2
+    width = col_points.shape[1] // 2
+    columns = lax.dynamic_slice_in_dim(col_points, core * width, width, 1)
+    left_basis, kept, sent = finish(jnp.stack([row_at, row_at ^ core_bit]), sketch, row_blocks, columns)
+    received = swapped(sent, core_bit, 0)
+    return left_basis, placed(received, 1 - core, placed(kept, core))
 
 
 def solution(mesh):

time: 41.1 us -> 38.6 us (0.939)
  Pallas kernels: 14.6 us -> 12.5 us
    pallas_call x1, Pallas kernels: 10.8 us -> 7.16 us  [finish(): pl.pallas_call(functools.partial(finish_body, 2.0 / dim, math.sqrt(total)...]
    pallas_call x0 -> x2, Pallas kernels: none -> 1.42 us  [placed(): pl.pallas_call(place_body, in_specs=specs, out_specs=remote, out_shape=ja...]
  transfers between devices with their start and end apart: 9 -> 9, of which waited for: 7 -> 7; matrix products, arithmetic and copies ran while one was open for 0% -> 1% of each run, Pallas kernels for 0% -> 2%
where the time goes in v5:
time: 38.6 us; the launch traced here: 38.4 us
  starting transfers between devices  12.6 us (33%)
  Pallas kernels  12.5 us (32%)
  waiting for transfers between devices  12.1 us (31%)
  between operations  0.84 us (2%)
    ppermute x9, starting transfers between devices, swapped(): return lax.ppermute(value, ('row', 'col'), pairs)  12.6 us
    ppermute x9, waiting for transfers between devices, swapped(): return lax.ppermute(value, ('row', 'col'), pairs)  12.1 us
    pallas_call x1, Pallas kernels, finish(): pl.pallas_call(functools.partial(finish_body, 2.0 / dim, math.sqrt(total)...  7.16 us
    pallas_call x1, Pallas kernels, sketch_halves(): pl.pallas_call(functools.partial(sketch_body, 2.0 / dim), in_specs=[pl.Bl...  3.92 us
    pallas_call x2, Pallas kernels, placed(): pl.pallas_call(place_body, in_specs=specs, out_specs=remote, out_shape=ja...  1.42 us
  transfers between devices with their start and end apart: 9, of which 7 were waited for; matrix products, arithmetic and copies ran while one was open for 1% of the time, Pallas kernels for 2%

profile of v5, /device:TPU:0, one launch (start us, length us, event | category | flops | bytes accessed | tf_op | source)
XLA Modules:
  0.0 38.4 jit_solution(10607927243686201410)
XLA Ops:
  0.6 0.0 copy-start
  0.7 3.9 %sketch.1 = (f32[128,128]{1,0:T(8,128)S(1)}, f32[128,128]{1,0:T(8,128)S(1)}) custom-call(s32[1]{0:T(128)} %bitcast.2.half_ref, bf16[64,256]{1,0:T(8,128)(2,1)} %row_hbm.1, bf16[64,8192]{1,0:T(8,128)(2,1)} %col_hbm.1, bf16[8192,128]{1,0:T(8,128)(2,1)} %panel_hbm.1), custom_call_target="tpu_custom_call" | custom-call | tf_op jit(solution)/shard_map/sketch/pallas_call | solution.py:73
  4.6 3.0 %collective-permute-start = (f32[128,128]{1,0:T(8,128)S(1)}, f32[128,128]{1,0:T(8,128)S(1)}, u32[]{:S(2)}, u32[]{:S(2)}) collective-permute-start(f32[128,128]{1,0:T(8,128)S(1)} %get-tuple-element.8), channel_id=1, source_target_pairs={{0,1},{1,0},{2,3},{3,2},{4,5},{5,4},{6,7},{7,6},{8,9},{9,8},{10,11... | collective-permute-start | bytes 196616 | tf_op jit(solution)/shard_map/ppermute | solution.py:260
  7.6 2.2 %collective-permute-done = f32[128,128]{1,0:T(8,128)S(1)} collective-permute-done((f32[128,128]{1,0:T(8,128)S(1)}, f32[128,128]{1,0:T(8,128)S(1)}, u32[]{:S(2)}, u32[]{:S(2)}) %collective-permute-start) | collective-permute-done | bytes 65568 | tf_op jit(solution)/shard_map/ppermute | solution.py:260
  9.9 2.2 %collective-permute-start.1 = (f32[128,128]{1,0:T(8,128)S(1)}, f32[128,128]{1,0:T(8,128)S(1)}, u32[]{:S(2)}, u32[]{:S(2)}) collective-permute-start(f32[128,128]{1,0:T(8,128)S(1)} %add.23), channel_id=1, source_target_pairs={{0,2},{1,3},{2,0},{3,1},{4,6},{5,7},{6,4},{7,5},{8,10},{9,11},{10,... | collective-permute-start | bytes 196616 | tf_op jit(solution)/shard_map/ppermute | solution.py:260
  12.1 2.2 %collective-permute-done.1 = f32[128,128]{1,0:T(8,128)S(1)} collective-permute-done((f32[128,128]{1,0:T(8,128)S(1)}, f32[128,128]{1,0:T(8,128)S(1)}, u32[]{:S(2)}, u32[]{:S(2)}) %collective-permute-start.1) | collective-permute-done | bytes 65568 | tf_op jit(solution)/shard_map/ppermute | solution.py:260
  14.3 3.1 %collective-permute-start.2 = (f32[128,128]{1,0:T(8,128)S(1)}, f32[128,128]{1,0:T(8,128)S(1)}, u32[]{:S(2)}, u32[]{:S(2)}) collective-permute-start(f32[128,128]{1,0:T(8,128)S(1)} %add.24), channel_id=1, source_target_pairs={{0,4},{1,5},{2,6},{3,7},{4,0},{5,1},{6,2},{7,3},{8,12},{9,13},{10,... | collective-permute-start | bytes 196616 | tf_op jit(solution)/shard_map/ppermute | solution.py:260
  17.4 2.2 %collective-permute-done.2 = f32[128,128]{1,0:T(8,128)S(1)} collective-permute-done((f32[128,128]{1,0:T(8,128)S(1)}, f32[128,128]{1,0:T(8,128)S(1)}, u32[]{:S(2)}, u32[]{:S(2)}) %collective-permute-start.2) | collective-permute-done | bytes 65568 | tf_op jit(solution)/shard_map/ppermute | solution.py:260
  19.7 0.1 collective-permute-start.4
  19.7 0.1 pad_add_fusion.rank_ref
  19.8 2.8 %collective-permute-start.5 = (f32[192,128]{1,0:T(8,128)S(1)}, f32[192,128]{1,0:T(8,128)S(1)}, u32[]{:S(2)}, u32[]{:S(2)}) collective-permute-start(f32[192,128]{1,0:T(8,128)S(1)} %pad_maximum_fusion.2), channel_id=1, source_target_pairs={{0,17},{1,16},{2,19},{3,18},{4,21},{5,20},{6,23},{7,22},{8,25},{9,... | collective-permute-start | bytes 294920 | tf_op jit(solution)/shard_map/ppermute | solution.py:260
  22.6 0.3 collective-permute-start.3
  22.9 3.7 %collective-permute-done.4 = f32[192,128]{1,0:T(8,128)S(1)} collective-permute-done((f32[192,128]{1,0:T(8,128)S(1)}, f32[192,128]{1,0:T(8,128)S(1)}, u32[]{:S(2)}, u32[]{:S(2)}) %collective-permute-start.4) | collective-permute-done | bytes 98336 | tf_op jit(solution)/shard_map/ppermute | solution.py:260
  26.6 0.0 collective-permute-done.5
  26.6 0.5 %collective-permute-start.7 = (bf16[2,64,256]{2,1,0:T(8,128)(2,1)S(1)}, bf16[2,64,256]{2,1,0:T(8,128)(2,1)S(1)}, u32[]{:S(2)}, u32[]{:S(2)}) collective-permute-start(bf16[2,64,256]{2,1,0:T(8,128)(2,1)S(1)} %maximum_maximum_fusion), channel_id=1, source_target_pairs={{0,8},{1,9},{2,10},{3,11},{4,12},{5,13},{6,14},{7,15},{8,0},{9,1},... | collective-permute-start | bytes 196616 | tf_op jit(solution)/shard_map/ppermute | solution.py:260
  27.2 0.0 collective-permute-done.3
  27.2 0.3 collective-permute-start.6
  27.5 0.5 %collective-permute-done.7 = bf16[2,64,256]{2,1,0:T(8,128)(2,1)S(1)} collective-permute-done((bf16[2,64,256]{2,1,0:T(8,128)(2,1)S(1)}, bf16[2,64,256]{2,1,0:T(8,128)(2,1)S(1)}, u32[]{:S(2)}, u32[]{:S(2)}) %collective-permute-start.7) | collective-permute-done | bytes 65568 | tf_op jit(solution)/shard_map/ppermute | solution.py:260
  28.1 0.7 %collective-permute-done.6 = f32[512,128]{1,0:T(8,128)S(1)} collective-permute-done((f32[512,128]{1,0:T(8,128)S(1)}, f32[512,128]{1,0:T(8,128)S(1)}, u32[]{:S(2)}, u32[]{:S(2)}) %collective-permute-start.6) | collective-permute-done | bytes 262176 | tf_op jit(solution)/shard_map/ppermute | solution.py:260
  28.9 7.2 %finish.1 = (f32[256,128]{1,0:T(8,128)}, bf16[32,4096]{1,0:T(8,128)(2,1)S(1)}, bf16[32,4096]{1,0:T(8,128)(2,1)S(1)}) custom-call(s32[2]{0:T(128)S(1)} %pad_add_fusion.rank_ref, f32[1024,128]{1,0:T(8,128)S(1)} %select_dynamic-update-slice_fusion.sketch_ref, bf16[4,64,256]{2,1,0:T(8,128)(2,1)S(1)} %pad_maximum_fusion.1.row_ref, ...), custom_call_target="tpu_custom_call" | custom-call | tf_op jit(solution)/shard_map/finish/pallas_call | solution.py:211
  36.1 0.3 collective-permute-start.8
  36.4 0.7 %placed.2.refs_0_ = bf16[32,8192]{1,0:T(8,128)(2,1)} custom-call(s32[1]{0:T(128)} %bitcast.10.at_ref, bf16[32,4096]{1,0:T(8,128)(2,1)S(1)} %get-tuple-element.11.part_ref), custom_call_target="tpu_custom_call" | custom-call | bytes 524288 | tf_op jit(solution)/shard_map/placed/pallas_call | solution.py:244
  37.2 0.6 %collective-permute-done.8.part_ref = bf16[32,4096]{1,0:T(8,128)(2,1)S(1)} collective-permute-done((bf16[32,4096]{1,0:T(8,128)(2,1)S(1)}, bf16[32,4096]{1,0:T(8,128)(2,1)S(1)}, u32[]{:S(2)}, u32[]{:S(2)}) %collective-permute-start.8) | collective-permute-done | bytes 262176 | tf_op jit(solution)/shard_map/ppermute | solution.py:260
  37.7 0.7 %placed.3 = bf16[32,8192]{1,0:T(8,128)(2,1)} custom-call(s32[1]{0:T(128)} %bitcast.9.at_ref, bf16[32,4096]{1,0:T(8,128)(2,1)S(1)} %collective-permute-done.8.part_ref, bf16[32,8192]{1,0:T(8,128)(2,1)} %placed.2.refs_0_), custom_call_target="tpu_custom_call", output_to_operand_aliasing={{}: (2, {})} | custom-call | bytes 524288 | tf_op jit(solution)/shard_map/placed/pallas_call | solution.py:244
  (27 shorter events, 0.3 us)
Async XLA Ops:
  0.6 11.4 %copy-start = (bf16[64,8192]{1,0:T(8,128)(2,1)S(1)}, bf16[64,8192]{1,0:T(8,128)(2,1)}, u32[]{:S(2)}) copy-start(bf16[64,8192]{1,0:T(8,128)(2,1)} %col_hbm.1) | copy-start | bytes 3145732
  0.7 16.7 %copy-start.1 = (bf16[64,256]{1,0:T(8,128)(2,1)S(1)}, bf16[64,256]{1,0:T(8,128)(2,1)}, u32[]{:S(2)}) copy-start(bf16[64,256]{1,0:T(8,128)(2,1)} %row_hbm.1) | copy-start | bytes 98308
  4.6 5.3 %collective-permute-start = (f32[128,128]{1,0:T(8,128)S(1)}, f32[128,128]{1,0:T(8,128)S(1)}, u32[]{:S(2)}, u32[]{:S(2)}) collective-permute-start(f32[128,128]{1,0:T(8,128)S(1)} %get-tuple-element.8), channel_id=1, source_target_pairs={{0,1},{1,0},{2,3},{3,2},{4,5},{5,4},{6,7},{7,6},{8,9},{9,8},{10,11... | collective-permute-start | bytes 196616 | tf_op jit(solution)/shard_map/ppermute | solution.py:260
  9.9 4.4 %collective-permute-start.1 = (f32[128,128]{1,0:T(8,128)S(1)}, f32[128,128]{1,0:T(8,128)S(1)}, u32[]{:S(2)}, u32[]{:S(2)}) collective-permute-start(f32[128,128]{1,0:T(8,128)S(1)} %add.23), channel_id=1, source_target_pairs={{0,2},{1,3},{2,0},{3,1},{4,6},{5,7},{6,4},{7,5},{8,10},{9,11},{10,... | collective-permute-start | bytes 196616 | tf_op jit(solution)/shard_map/ppermute | solution.py:260
  14.3 5.3 %collective-permute-start.2 = (f32[128,128]{1,0:T(8,128)S(1)}, f32[128,128]{1,0:T(8,128)S(1)}, u32[]{:S(2)}, u32[]{:S(2)}) collective-permute-start(f32[128,128]{1,0:T(8,128)S(1)} %add.24), channel_id=1, source_target_pairs={{0,4},{1,5},{2,6},{3,7},{4,0},{5,1},{6,2},{7,3},{8,12},{9,13},{10,... | collective-permute-start | bytes 196616 | tf_op jit(solution)/shard_map/ppermute | solution.py:260
  19.7 7.0 %collective-permute-start.4 = (f32[192,128]{1,0:T(8,128)S(1)}, f32[192,128]{1,0:T(8,128)S(1)}, u32[]{:S(2)}, u32[]{:S(2)}) collective-permute-start(f32[192,128]{1,0:T(8,128)S(1)} %pad_maximum_fusion.2), channel_id=1, source_target_pairs={{0,24},{1,25},{2,26},{3,27},{4,28},{5,29},{6,30},{7,31},{8,16},{9,... | collective-permute-start | bytes 294920 | tf_op jit(solution)/shard_map/ppermute | solution.py:260
  19.8 6.8 %collective-permute-start.5 = (f32[192,128]{1,0:T(8,128)S(1)}, f32[192,128]{1,0:T(8,128)S(1)}, u32[]{:S(2)}, u32[]{:S(2)}) collective-permute-start(f32[192,128]{1,0:T(8,128)S(1)} %pad_maximum_fusion.2), channel_id=1, source_target_pairs={{0,17},{1,16},{2,19},{3,18},{4,21},{5,20},{6,23},{7,22},{8,25},{9,... | collective-permute-start | bytes 294920 | tf_op jit(solution)/shard_map/ppermute | solution.py:260
  22.6 4.6 %collective-permute-start.3 = (f32[128,128]{1,0:T(8,128)S(1)}, f32[128,128]{1,0:T(8,128)S(1)}, u32[]{:S(2)}, u32[]{:S(2)}) collective-permute-start(f32[128,128]{1,0:T(8,128)S(1)} %add.25), channel_id=1, source_target_pairs={{0,9},{1,8},{2,11},{3,10},{4,13},{5,12},{6,15},{7,14},{8,1},{9,0},... | collective-permute-start | bytes 196616 | tf_op jit(solution)/shard_map/ppermute | solution.py:260
  26.6 1.4 %collective-permute-start.7 = (bf16[2,64,256]{2,1,0:T(8,128)(2,1)S(1)}, bf16[2,64,256]{2,1,0:T(8,128)(2,1)S(1)}, u32[]{:S(2)}, u32[]{:S(2)}) collective-permute-start(bf16[2,64,256]{2,1,0:T(8,128)(2,1)S(1)} %maximum_maximum_fusion), channel_id=1, source_target_pairs={{0,8},{1,9},{2,10},{3,11},{4,12},{5,13},{6,14},{7,15},{8,0},{9,1},... | collective-permute-start | bytes 196616 | tf_op jit(solution)/shard_map/ppermute | solution.py:260
  27.2 1.6 %collective-permute-start.6 = (f32[512,128]{1,0:T(8,128)S(1)}, f32[512,128]{1,0:T(8,128)S(1)}, u32[]{:S(2)}, u32[]{:S(2)}) collective-permute-start(f32[512,128]{1,0:T(8,128)S(1)} %pad_maximum_fusion), channel_id=1, source_target_pairs={{0,8},{1,9},{2,10},{3,11},{4,12},{5,13},{6,14},{7,15},{8,0},{9,1},... | collective-permute-start | bytes 786440 | tf_op jit(solution)/shard_map/ppermute | solution.py:260
  36.1 1.6 %collective-permute-start.8 = (bf16[32,4096]{1,0:T(8,128)(2,1)S(1)}, bf16[32,4096]{1,0:T(8,128)(2,1)S(1)}, u32[]{:S(2)}, u32[]{:S(2)}) collective-permute-start(bf16[32,4096]{1,0:T(8,128)(2,1)S(1)} %get-tuple-element.10), channel_id=1, source_target_pairs={{0,8},{1,9},{2,10},{3,11},{4,12},{5,13},{6,14},{7,15},{8,0},{9,1},... | collective-permute-start | bytes 786440 | tf_op jit(solution)/shard_map/ppermute | solution.py:260

commit v6 on v5

--- a/solution.py
+++ b/solution.py
@@ -12,6 +12,7 @@
 BF16 = jnp.bfloat16
 EXACT = lax.Precision.HIGHEST
 VMEM_BYTES = 40 << 20
+SKETCH_VMEM_BYTES = 16 << 20
 CHUNK = 512
 
 
@@ -41,9 +42,15 @@
     return math.gcd(col_dev, 1024)
 
 
-def sketch_body(
-    scale, half_ref, row_hbm, col_hbm, panel_hbm, keep_ref, send_ref,
-    row_ref, col_ref, panel_ref, tile_ref, total_ref, row_sem, col_sem, panel_sem,
+def half_left(row_points, scale, half, left_ref):
+    left_ref[...] = widened(row_points, scale, 2.0 * scale, True).T
+    rows = left_ref.shape[0] // 2
+    return left_ref[pl.ds(pl.multiple_of(half * rows, rows), rows), :]
+
+
+def sketch_send_body(
+    scale, half_ref, row_hbm, col_hbm, panel_hbm, send_ref, col_ref, panel_ref,
+    row_ref, left_ref, tile_ref, row_sem, col_sem, panel_sem,
 ):
     row_copy = pltpu.make_async_copy(row_hbm, row_ref, row_sem)
     col_copy = pltpu.make_async_copy(col_hbm, col_ref, col_sem)
@@ -53,16 +60,23 @@
     panel_copy.start()
     chunk = chunk_width(col_ref.shape[1])
     row_copy.wait()
-    left = widened(row_ref[...], scale, 2.0 * scale, True).T
+    left = half_left(row_ref[...], scale, 1 - half_ref[0], left_ref)
     col_copy.wait()
     for c in range(0, col_ref.shape[1], chunk):
         right = widened(col_ref[:, c : c + chunk], scale, 1.0, False)
         tile_ref[:, c : c + chunk] = exponent(left, right)
     panel_copy.wait()
-    total_ref[...] = contract(tile_ref[...], panel_ref[...], 1, 0)
-    half, rows = half_ref[0], keep_ref.shape[0]
-    keep_ref[...] = total_ref[pl.ds(pl.multiple_of(half * rows, rows), rows), :]
-    send_ref[...] = total_ref[pl.ds(pl.multiple_of((1 - half) * rows, rows), rows), :]
+    send_ref[...] = contract(tile_ref[...], panel_ref[...], 1, 0)
+
+
+def sketch_keep_body(scale, half_ref, row_ref, col_ref, panel_ref, keep_ref, left_ref):
+    left = half_left(row_ref[...], scale, half_ref[0], left_ref)
+    chunk = chunk_width(col_ref.shape[1])
+    total = jnp.zeros(keep_ref.shape, F32)
+    for c in range(0, col_ref.shape[1], chunk):
+        tile = exponent(left, widened(col_ref[:, c : c + chunk], scale, 1.0, False))
+        total = total + contract(tile, panel_ref[c : c + chunk, :], 1, 0)
+    keep_ref[...] = total
 
 
 def sketch_halves(row_points, col_points, panel, half):
@@ -70,24 +84,42 @@
     col_dev, width = panel.shape
     part = jax.ShapeDtypeStruct((rows // 2, width), F32)
     whole, remote = pl.BlockSpec(memory_space=pltpu.VMEM), pl.BlockSpec(memory_space=pltpu.HBM)
-    return pl.pallas_call(
-        functools.partial(sketch_body, 2.0 / dim),
-        in_specs=[pl.BlockSpec(memory_space=pltpu.SMEM), remote, remote, remote],
-        out_specs=[whole, whole],
-        out_shape=[part, part],
+    scalar = pl.BlockSpec(memory_space=pltpu.SMEM)
+    send, col_near, panel_near = pl.pallas_call(
+        functools.partial(sketch_send_body, 2.0 / dim),
+        in_specs=[scalar, remote, remote, remote],
+        out_specs=[whole, whole, whole],
+        out_shape=[
+            part,
+            jax.ShapeDtypeStruct((dim, col_dev), BF16),
+            jax.ShapeDtypeStruct((col_dev, width), BF16),
+        ],
         scratch_shapes=[
             pltpu.VMEM((dim, rows), BF16),
-            pltpu.VMEM((dim, col_dev), BF16),
-            pltpu.VMEM((col_dev, width), BF16),
-            pltpu.VMEM((rows, col_dev), BF16),
-            pltpu.VMEM((rows, width), F32),
+            pltpu.VMEM((rows, dim + 16), BF16),
+            pltpu.VMEM((rows // 2, col_dev), BF16),
             pltpu.SemaphoreType.DMA,
             pltpu.SemaphoreType.DMA,
             pltpu.SemaphoreType.DMA,
         ],
-        compiler_params=pltpu.CompilerParams(vmem_limit_bytes=VMEM_BYTES),
-        name="sketch",
+        compiler_params=pltpu.CompilerParams(vmem_limit_bytes=SKETCH_VMEM_BYTES),
+        name="sketch_send",
     )(half, *[pltpu.with_memory_space_constraint(a, pltpu.HBM) for a in (row_points, col_points, panel)])
+    keep = pl.pallas_call(
+        functools.partial(sketch_keep_body, 2.0 / dim),
+        in_specs=[scalar, whole, whole, whole],
+        out_specs=whole,
+        out_shape=part,
+        scratch_shapes=[pltpu.VMEM((rows, dim + 16), BF16)],
+        compiler_params=pltpu.CompilerParams(vmem_limit_bytes=SKETCH_VMEM_BYTES),
+        cost_estimate=pl.CostEstimate(
+            flops=rows * col_dev * (dim + 16 + width),
+            bytes_accessed=2 * col_dev * (dim + 16 + width),
+            transcendentals=rows // 2 * col_dev,
+        ),
+        name="sketch_keep",
+    )(half, row_points, col_near, panel_near)
+    return keep, send
 
 
 def inverse_factor(gram, after_step):
@@ -156,10 +188,13 @@
     blocks, _, rows = row_ref.shape
     sketch = sketch_ref[...]
     width = sketch.shape[1]
-    gram = contract(sketch, sketch, 0, 0, EXACT)
-    high, middle, _ = bf16_terms(sketch)
-    sketch_t_ref[:width, :] = high.T
-    sketch_t_ref[width:, :] = middle.T
+    high, middle, low = bf16_terms(sketch)
+    for k, term in enumerate((high, middle, low)):
+        sketch_t_ref[k * width : (k + 1) * width, :] = term.T
+    with_high = contract(sketch_t_ref[...], high, 1, 0)
+    mixed = with_high[width : 2 * width] + with_high[2 * width :]
+    middles = contract(sketch_t_ref[width : 2 * width, :], middle, 1, 0)
+    gram = with_high[:width] + ((mixed + mixed.T) + middles)
     for k in range(blocks):
         left_ref[k * rows : (k + 1) * rows, :] = widened(row_ref[k], scale, 2.0 * scale, True).T
     starts = list(range(0, col_ref.shape[1], chunk))
@@ -167,7 +202,7 @@
 
     def finish_pending():
         for c, tile in pending:
-            product = contract(sketch_t_ref[...], tile, 1, 0)
+            product = contract(sketch_t_ref[: 2 * width, :], tile, 1, 0)
             for ref, term in zip(term_refs, bf16_terms(product[:width] + product[width:])):
                 ref[:, c : c + chunk] = term
         pending.clear()
@@ -216,7 +251,7 @@
         scratch_shapes=[
             pltpu.VMEM((width, width), F32),
             pltpu.VMEM((total, dim + 16), BF16),
-            pltpu.VMEM((2 * width, total), BF16),
+            pltpu.VMEM((3 * width, total), BF16),
             *[pltpu.VMEM((width, col_dev), BF16)] * 3,
         ],
         compiler_params=pltpu.CompilerParams(vmem_limit_bytes=VMEM_BYTES),
@@ -277,15 +312,17 @@
         return both(jnp.where(half == 0, mine, other), jnp.where(half == 0, other, mine), axis)
 
     part = keep + swapped(send, 0, x_bit)
+    part, col_points = lax.optimization_barrier((part, col_points))
     for bit in z_bits:
         part = part + swapped(part, 0, bit)
 
     dim, rows = row_points.shape
     points = lax.dynamic_slice_in_dim(row_points, half * (rows // 2), rows // 2, 1).astype(F32)
-    message = both(part, points)
+    message, part = lax.optimization_barrier((both(part, points), part))
     y_bit = y_bits[-1]
+    far = swapped(message, core_bit | y_bit, 0)
+    cross = swapped(message, y_bit, x_bit)
     near = swapped(part, core_bit, x_bit)
-    cross, far = swapped(message, y_bit, x_bit), swapped(message, core_bit | y_bit, 0)
     split = part.shape[0]
     held = jnp.concatenate([part, near, far[:split], cross[:split]])
     held_points = jnp.stack([row_points, both(far[split:], cross[split:], 1).astype(BF16)])

time: 38.6 us -> 37.2 us (0.964)
  waiting for transfers between devices: 12.1 us -> 10 us
  Pallas kernels: 12.5 us -> 13.1 us
    ppermute x9, waiting for transfers between devices: 12.1 us -> 10 us  [swapped(): return lax.ppermute(value, ('row', 'col'), pairs)]
    pallas_call x1 -> x2, Pallas kernels: 3.92 us -> 4.64 us  [the longest x1 2.72 us: sketch_halves(): pl.pallas_call(functools.partial(sketch_send_body, 2.0 / dim), in_specs=[...]
  transfers between devices with their start and end apart: 9 -> 9, of which waited for: 7 -> 7; matrix products, arithmetic and copies ran while one was open for 1% -> 1% of each run, Pallas kernels for 2% -> 7%
where the time goes in v6:
time: 37.2 us; the launch traced here: 37.1 us
  Pallas kernels  13.1 us (35%)
  starting transfers between devices  12.8 us (34%)
  waiting for transfers between devices  10 us (27%)
  between operations  0.84 us (2%)
    ppermute x9, starting transfers between devices, swapped(): return lax.ppermute(value, ('row', 'col'), pairs)  12.8 us
    ppermute x9, waiting for transfers between devices, swapped(): return lax.ppermute(value, ('row', 'col'), pairs)  10 us
    pallas_call x1, Pallas kernels, finish(): pl.pallas_call(functools.partial(finish_body, 2.0 / dim, math.sqrt(total)...  7.02 us
    pallas_call x1, Pallas kernels, sketch_halves(): pl.pallas_call(functools.partial(sketch_send_body, 2.0 / dim), in_specs=[...  2.72 us
    pallas_call x1, Pallas kernels, sketch_halves(): pl.pallas_call(functools.partial(sketch_keep_body, 2.0 / dim), in_specs=[...  1.91 us
    pallas_call x2, Pallas kernels, placed(): pl.pallas_call(place_body, in_specs=specs, out_specs=remote, out_shape=ja...  1.42 us
  transfers between devices with their start and end apart: 9, of which 7 were waited for; matrix products, arithmetic and copies ran while one was open for 1% of the time, Pallas kernels for 7%

profile of v6, /device:TPU:0, one launch (start us, length us, event | category | flops | bytes accessed | tf_op | source)
XLA Modules:
  0.0 37.1 jit_solution(15501295887200376373)
XLA Ops:
  0.7 2.7 %sketch_send.1 = (f32[128,128]{1,0:T(8,128)S(1)}, bf16[64,8192]{1,0:T(8,128)(2,1)S(1)}, bf16[8192,128]{1,0:T(8,128)(2,1)S(1)}) custom-call(s32[1]{0:T(128)} %bitcast.2.half_ref, bf16[64,256]{1,0:T(8,128)(2,1)} %row_ref.1, bf16[64,8192]{1,0:T(8,128)(2,1)} %col_hbm.1, bf16[8192,128]{1,0:T(8,128)(2,1)} %panel_hbm.1), custom_call_target="tpu_custom_call" | custom-call | tf_op jit(solution)/shard_map/sketch_send/pallas_call | solution.py:88
  3.4 3.0 %collective-permute-start = (f32[128,128]{1,0:T(8,128)S(1)}, f32[128,128]{1,0:T(8,128)S(1)}, u32[]{:S(2)}, u32[]{:S(2)}) collective-permute-start(f32[128,128]{1,0:T(8,128)S(1)} %get-tuple-element.14), channel_id=1, source_target_pairs={{0,1},{1,0},{2,3},{3,2},{4,5},{5,4},{6,7},{7,6},{8,9},{9,8},{10,11... | collective-permute-start | bytes 196616 | tf_op jit(solution)/shard_map/ppermute | solution.py:295
  6.4 1.9 %sketch_keep.1 = f32[128,128]{1,0:T(8,128)S(1)} custom-call(s32[1]{0:T(128)} %bitcast.2.half_ref, bf16[64,256]{1,0:T(8,128)(2,1)S(1)} %copy-done, bf16[64,8192]{1,0:T(8,128)(2,1)S(1)} %get-tuple-element.12.col_ref, bf16[8192,128]{1,0:T(8,128)(2,1)S(1)} %get-tuple-element.13.panel_ref), custom_call_target="tpu_custom_call" | custom-call | flops 436207616 | bytes 3407872 | tf_op jit(solution)/shard_map/sketch_keep/pallas_call | solution.py:108
  8.3 0.3 collective-permute-done
  8.6 2.2 %collective-permute-start.1 = (f32[128,128]{1,0:T(8,128)S(1)}, f32[128,128]{1,0:T(8,128)S(1)}, u32[]{:S(2)}, u32[]{:S(2)}) collective-permute-start(f32[128,128]{1,0:T(8,128)S(1)} %add.23), channel_id=1, source_target_pairs={{0,2},{1,3},{2,0},{3,1},{4,6},{5,7},{6,4},{7,5},{8,10},{9,11},{10,... | collective-permute-start | bytes 196616 | tf_op jit(solution)/shard_map/ppermute | solution.py:295
  10.8 2.2 %collective-permute-done.1 = f32[128,128]{1,0:T(8,128)S(1)} collective-permute-done((f32[128,128]{1,0:T(8,128)S(1)}, f32[128,128]{1,0:T(8,128)S(1)}, u32[]{:S(2)}, u32[]{:S(2)}) %collective-permute-start.1) | collective-permute-done | bytes 65568 | tf_op jit(solution)/shard_map/ppermute | solution.py:295
  13.1 3.1 %collective-permute-start.2 = (f32[128,128]{1,0:T(8,128)S(1)}, f32[128,128]{1,0:T(8,128)S(1)}, u32[]{:S(2)}, u32[]{:S(2)}) collective-permute-start(f32[128,128]{1,0:T(8,128)S(1)} %add.24), channel_id=1, source_target_pairs={{0,4},{1,5},{2,6},{3,7},{4,0},{5,1},{6,2},{7,3},{8,12},{9,13},{10,... | collective-permute-start | bytes 196616 | tf_op jit(solution)/shard_map/ppermute | solution.py:295
  16.2 0.1 pad_add_fusion.rank_ref
  16.2 2.2 %collective-permute-done.2 = f32[128,128]{1,0:T(8,128)S(1)} collective-permute-done((f32[128,128]{1,0:T(8,128)S(1)}, f32[128,128]{1,0:T(8,128)S(1)}, u32[]{:S(2)}, u32[]{:S(2)}) %collective-permute-start.2) | collective-permute-done | bytes 65568 | tf_op jit(solution)/shard_map/ppermute | solution.py:295
  18.4 0.1 collective-permute-start.4
  18.6 2.8 %collective-permute-start.5 = (f32[192,128]{1,0:T(8,128)S(1)}, f32[192,128]{1,0:T(8,128)S(1)}, u32[]{:S(2)}, u32[]{:S(2)}) collective-permute-start(f32[192,128]{1,0:T(8,128)S(1)} %pad_maximum_fusion.2), channel_id=1, source_target_pairs={{0,17},{1,16},{2,19},{3,18},{4,21},{5,20},{6,23},{7,22},{8,25},{9,... | collective-permute-start | bytes 294920 | tf_op jit(solution)/shard_map/ppermute | solution.py:295
  21.4 0.3 collective-permute-start.3
  21.8 3.6 %collective-permute-done.4 = f32[192,128]{1,0:T(8,128)S(1)} collective-permute-done((f32[192,128]{1,0:T(8,128)S(1)}, f32[192,128]{1,0:T(8,128)S(1)}, u32[]{:S(2)}, u32[]{:S(2)}) %collective-permute-start.4) | collective-permute-done | bytes 98336 | tf_op jit(solution)/shard_map/ppermute | solution.py:295
  25.4 0.0 collective-permute-done.5
  25.4 0.5 %collective-permute-start.7 = (bf16[2,64,256]{2,1,0:T(8,128)(2,1)S(1)}, bf16[2,64,256]{2,1,0:T(8,128)(2,1)S(1)}, u32[]{:S(2)}, u32[]{:S(2)}) collective-permute-start(bf16[2,64,256]{2,1,0:T(8,128)(2,1)S(1)} %maximum_maximum_fusion), channel_id=1, source_target_pairs={{0,8},{1,9},{2,10},{3,11},{4,12},{5,13},{6,14},{7,15},{8,0},{9,1},... | collective-permute-start | bytes 196616 | tf_op jit(solution)/shard_map/ppermute | solution.py:295
  25.9 0.0 collective-permute-done.3
  26.0 0.4 collective-permute-start.6
  26.3 0.5 %collective-permute-done.7 = bf16[2,64,256]{2,1,0:T(8,128)(2,1)S(1)} collective-permute-done((bf16[2,64,256]{2,1,0:T(8,128)(2,1)S(1)}, bf16[2,64,256]{2,1,0:T(8,128)(2,1)S(1)}, u32[]{:S(2)}, u32[]{:S(2)}) %collective-permute-start.7) | collective-permute-done | bytes 65568 | tf_op jit(solution)/shard_map/ppermute | solution.py:295
  26.9 0.7 %collective-permute-done.6 = f32[512,128]{1,0:T(8,128)S(1)} collective-permute-done((f32[512,128]{1,0:T(8,128)S(1)}, f32[512,128]{1,0:T(8,128)S(1)}, u32[]{:S(2)}, u32[]{:S(2)}) %collective-permute-start.6) | collective-permute-done | bytes 262176 | tf_op jit(solution)/shard_map/ppermute | solution.py:295
  27.7 7.0 %finish.1 = (f32[256,128]{1,0:T(8,128)}, bf16[32,4096]{1,0:T(8,128)(2,1)S(1)}, bf16[32,4096]{1,0:T(8,128)(2,1)S(1)}) custom-call(s32[2]{0:T(128)S(1)} %pad_add_fusion.rank_ref, f32[1024,128]{1,0:T(8,128)S(1)} %select_dynamic-update-slice_fusion.sketch_ref, bf16[4,64,256]{2,1,0:T(8,128)(2,1)S(1)} %pad_maximum_fusion.1.row_ref, ...), custom_call_target="tpu_custom_call" | custom-call | tf_op jit(solution)/shard_map/finish/pallas_call | solution.py:246
  34.8 0.4 %collective-permute-start.8 = (bf16[32,4096]{1,0:T(8,128)(2,1)S(1)}, bf16[32,4096]{1,0:T(8,128)(2,1)S(1)}, u32[]{:S(2)}, u32[]{:S(2)}) collective-permute-start(bf16[32,4096]{1,0:T(8,128)(2,1)S(1)} %get-tuple-element.20), channel_id=1, source_target_pairs={{0,8},{1,9},{2,10},{3,11},{4,12},{5,13},{6,14},{7,15},{8,0},{9,1},... | collective-permute-start | bytes 786440 | tf_op jit(solution)/shard_map/ppermute | solution.py:295
  35.1 0.7 %placed.2.refs_0_ = bf16[32,8192]{1,0:T(8,128)(2,1)} custom-call(s32[1]{0:T(128)} %bitcast.10.at_ref, bf16[32,4096]{1,0:T(8,128)(2,1)S(1)} %get-tuple-element.21.part_ref), custom_call_target="tpu_custom_call" | custom-call | bytes 524288 | tf_op jit(solution)/shard_map/placed/pallas_call | solution.py:279
  35.8 0.5 %collective-permute-done.8.part_ref = bf16[32,4096]{1,0:T(8,128)(2,1)S(1)} collective-permute-done((bf16[32,4096]{1,0:T(8,128)(2,1)S(1)}, bf16[32,4096]{1,0:T(8,128)(2,1)S(1)}, u32[]{:S(2)}, u32[]{:S(2)}) %collective-permute-start.8) | collective-permute-done | bytes 262176 | tf_op jit(solution)/shard_map/ppermute | solution.py:295
  36.4 0.7 %placed.3 = bf16[32,8192]{1,0:T(8,128)(2,1)} custom-call(s32[1]{0:T(128)} %bitcast.9.at_ref, bf16[32,4096]{1,0:T(8,128)(2,1)S(1)} %collective-permute-done.8.part_ref, bf16[32,8192]{1,0:T(8,128)(2,1)} %placed.2.refs_0_), custom_call_target="tpu_custom_call", output_to_operand_aliasing={{}: (2, {})} | custom-call | bytes 524288 | tf_op jit(solution)/shard_map/placed/pallas_call | solution.py:279
  (28 shorter events, 0.3 us)
Async XLA Ops:
  0.6 5.8 %copy-start = (bf16[64,256]{1,0:T(8,128)(2,1)S(1)}, bf16[64,256]{1,0:T(8,128)(2,1)}, u32[]{:S(2)}) copy-start(bf16[64,256]{1,0:T(8,128)(2,1)} %row_ref.1) | copy-start | bytes 98308
  3.4 5.3 %collective-permute-start = (f32[128,128]{1,0:T(8,128)S(1)}, f32[128,128]{1,0:T(8,128)S(1)}, u32[]{:S(2)}, u32[]{:S(2)}) collective-permute-start(f32[128,128]{1,0:T(8,128)S(1)} %get-tuple-element.14), channel_id=1, source_target_pairs={{0,1},{1,0},{2,3},{3,2},{4,5},{5,4},{6,7},{7,6},{8,9},{9,8},{10,11... | collective-permute-start | bytes 196616 | tf_op jit(solution)/shard_map/ppermute | solution.py:295
  6.4 12.1 %copy-start.1 = (bf16[64,8192]{1,0:T(8,128)(2,1)S(1)}, bf16[64,8192]{1,0:T(8,128)(2,1)}, u32[]{:S(2)}) copy-start(bf16[64,8192]{1,0:T(8,128)(2,1)} %col_hbm.1) | copy-start | bytes 3145732
  8.6 4.4 %collective-permute-start.1 = (f32[128,128]{1,0:T(8,128)S(1)}, f32[128,128]{1,0:T(8,128)S(1)}, u32[]{:S(2)}, u32[]{:S(2)}) collective-permute-start(f32[128,128]{1,0:T(8,128)S(1)} %add.23), channel_id=1, source_target_pairs={{0,2},{1,3},{2,0},{3,1},{4,6},{5,7},{6,4},{7,5},{8,10},{9,11},{10,... | collective-permute-start | bytes 196616 | tf_op jit(solution)/shard_map/ppermute | solution.py:295
  13.1 5.3 %collective-permute-start.2 = (f32[128,128]{1,0:T(8,128)S(1)}, f32[128,128]{1,0:T(8,128)S(1)}, u32[]{:S(2)}, u32[]{:S(2)}) collective-permute-start(f32[128,128]{1,0:T(8,128)S(1)} %add.24), channel_id=1, source_target_pairs={{0,4},{1,5},{2,6},{3,7},{4,0},{5,1},{6,2},{7,3},{8,12},{9,13},{10,... | collective-permute-start | bytes 196616 | tf_op jit(solution)/shard_map/ppermute | solution.py:295
  18.4 6.9 %collective-permute-start.4 = (f32[192,128]{1,0:T(8,128)S(1)}, f32[192,128]{1,0:T(8,128)S(1)}, u32[]{:S(2)}, u32[]{:S(2)}) collective-permute-start(f32[192,128]{1,0:T(8,128)S(1)} %pad_maximum_fusion.2), channel_id=1, source_target_pairs={{0,24},{1,25},{2,26},{3,27},{4,28},{5,29},{6,30},{7,31},{8,16},{9,... | collective-permute-start | bytes 294920 | tf_op jit(solution)/shard_map/ppermute | solution.py:295
  18.6 6.8 %collective-permute-start.5 = (f32[192,128]{1,0:T(8,128)S(1)}, f32[192,128]{1,0:T(8,128)S(1)}, u32[]{:S(2)}, u32[]{:S(2)}) collective-permute-start(f32[192,128]{1,0:T(8,128)S(1)} %pad_maximum_fusion.2), channel_id=1, source_target_pairs={{0,17},{1,16},{2,19},{3,18},{4,21},{5,20},{6,23},{7,22},{8,25},{9,... | collective-permute-start | bytes 294920 | tf_op jit(solution)/shard_map/ppermute | solution.py:295
  21.4 4.5 %collective-permute-start.3 = (f32[128,128]{1,0:T(8,128)S(1)}, f32[128,128]{1,0:T(8,128)S(1)}, u32[]{:S(2)}, u32[]{:S(2)}) collective-permute-start(f32[128,128]{1,0:T(8,128)S(1)} %add.25), channel_id=1, source_target_pairs={{0,9},{1,8},{2,11},{3,10},{4,13},{5,12},{6,15},{7,14},{8,1},{9,0},... | collective-permute-start | bytes 196616 | tf_op jit(solution)/shard_map/ppermute | solution.py:295
  25.4 1.4 %collective-permute-start.7 = (bf16[2,64,256]{2,1,0:T(8,128)(2,1)S(1)}, bf16[2,64,256]{2,1,0:T(8,128)(2,1)S(1)}, u32[]{:S(2)}, u32[]{:S(2)}) collective-permute-start(bf16[2,64,256]{2,1,0:T(8,128)(2,1)S(1)} %maximum_maximum_fusion), channel_id=1, source_target_pairs={{0,8},{1,9},{2,10},{3,11},{4,12},{5,13},{6,14},{7,15},{8,0},{9,1},... | collective-permute-start | bytes 196616 | tf_op jit(solution)/shard_map/ppermute | solution.py:295
  26.0 1.6 %collective-permute-start.6 = (f32[512,128]{1,0:T(8,128)S(1)}, f32[512,128]{1,0:T(8,128)S(1)}, u32[]{:S(2)}, u32[]{:S(2)}) collective-permute-start(f32[512,128]{1,0:T(8,128)S(1)} %pad_maximum_fusion), channel_id=1, source_target_pairs={{0,8},{1,9},{2,10},{3,11},{4,12},{5,13},{6,14},{7,15},{8,0},{9,1},... | collective-permute-start | bytes 786440 | tf_op jit(solution)/shard_map/ppermute | solution.py:295
  34.8 1.6 %collective-permute-start.8 = (bf16[32,4096]{1,0:T(8,128)(2,1)S(1)}, bf16[32,4096]{1,0:T(8,128)(2,1)S(1)}, u32[]{:S(2)}, u32[]{:S(2)}) collective-permute-start(bf16[32,4096]{1,0:T(8,128)(2,1)S(1)} %get-tuple-element.20), channel_id=1, source_target_pairs={{0,8},{1,9},{2,10},{3,11},{4,12},{5,13},{6,14},{7,15},{8,0},{9,1},... | collective-permute-start | bytes 786440 | tf_op jit(solution)/shard_map/ppermute | solution.py:295

commit v7 on v6

--- a/solution.py
+++ b/solution.py
@@ -313,30 +313,28 @@
 
     part = keep + swapped(send, 0, x_bit)
     part, col_points = lax.optimization_barrier((part, col_points))
-    for bit in z_bits:
-        part = part + swapped(part, 0, bit)
-
-    dim, rows = row_points.shape
-    points = lax.dynamic_slice_in_dim(row_points, half * (rows // 2), rows // 2, 1).astype(F32)
-    message, part = lax.optimization_barrier((both(part, points), part))
     y_bit = y_bits[-1]
-    far = swapped(message, core_bit | y_bit, 0)
-    cross = swapped(message, y_bit, x_bit)
+    for k, bit in enumerate(z_bits):
+        if k == 0:
+            row_points, part = lax.optimization_barrier((row_points, part))
+            y_points = swapped(row_points, core_bit | y_bit, 0)
+        moved = swapped(part, 0, bit)
+        if k == 1:
+            moved, y_points = lax.optimization_barrier((moved, y_points))
+        part = part + moved
+
+    far = swapped(part, core_bit | y_bit, 0)
+    cross = swapped(part, y_bit, x_bit)
     near = swapped(part, core_bit, x_bit)
     split = part.shape[0]
-    held = jnp.concatenate([part, near, far[:split], cross[:split]])
-    held_points = jnp.stack([row_points, both(far[split:], cross[split:], 1).astype(BF16)])
+    held, held_points = jnp.concatenate([part, near, far, cross]), jnp.stack([row_points, y_points])
     there, there_points = swapped(held, core_bit, 0), swapped(held_points, core_bit, 0)
     part, near, far, cross = held.reshape(4, split, -1)
     part_there, near_there, far_there, cross_there = there.reshape(4, split, -1)
-    (points, far_points, cross_points), (points_there, far_points_there, cross_points_there) = [
-        (a[0], a[1][:, : rows // 2], a[1][:, rows // 2 :]) for a in (held_points, there_points)
-    ]
     sketch = [ordered(part, near_there), ordered(part_there, near)]
-    row_blocks = [points, points_there]
     sketch += [ordered(far, cross_there), ordered(far_there, cross)]
-    row_blocks += [ordered(far_points, cross_points_there, 1), ordered(far_points_there, cross_points, 1)]
-    sketch, row_blocks = jnp.concatenate(sketch), jnp.stack(row_blocks)
+    sketch = jnp.concatenate(sketch)
+    row_blocks = jnp.stack([row_points, there_points[0], y_points, there_points[1]])
     for bit in y_bits[:-1]:
         sketch, row_blocks = [both(a, swapped(a, bit, 0)) for a in (sketch, row_blocks)]
 

time: 37.2 us -> 36.5 us (0.981)
  waiting for transfers between devices: 10 us -> 9.32 us
    ppermute x9 -> x10, waiting for transfers between devices: 10 us -> 9.32 us  [swapped(): return lax.ppermute(value, ('row', 'col'), pairs)]
    ppermute x9 -> x10, starting transfers between devices: 12.8 us -> 12.9 us  [swapped(): return lax.ppermute(value, ('row', 'col'), pairs)]
  transfers between devices with their start and end apart: 9 -> 10, of which waited for: 7 -> 7; matrix products, arithmetic and copies ran while one was open for 1% -> 0% of each run, Pallas kernels for 7% -> 7%
where the time goes in v7:
time: 36.5 us; the launch traced here: 36.3 us
  Pallas kernels  13.1 us (36%)
  starting transfers between devices  12.9 us (35%)
  waiting for transfers between devices  9.32 us (26%)
  between operations  0.79 us (2%)
    ppermute x10, starting transfers between devices, swapped(): return lax.ppermute(value, ('row', 'col'), pairs)  12.9 us
    ppermute x10, waiting for transfers between devices, swapped(): return lax.ppermute(value, ('row', 'col'), pairs)  9.32 us
    pallas_call x1, Pallas kernels, finish(): pl.pallas_call(functools.partial(finish_body, 2.0 / dim, math.sqrt(total)...  7.03 us
    pallas_call x1, Pallas kernels, sketch_halves(): pl.pallas_call(functools.partial(sketch_send_body, 2.0 / dim), in_specs=[...  2.72 us
    pallas_call x1, Pallas kernels, sketch_halves(): pl.pallas_call(functools.partial(sketch_keep_body, 2.0 / dim), in_specs=[...  1.91 us
    pallas_call x2, Pallas kernels, placed(): pl.pallas_call(place_body, in_specs=specs, out_specs=remote, out_shape=ja...  1.42 us
  transfers between devices with their start and end apart: 10, of which 7 were waited for; matrix products, arithmetic and copies ran while one was open for 0% of the time, Pallas kernels for 7%

profile of v7, /device:TPU:0, one launch (start us, length us, event | category | flops | bytes accessed | tf_op | source)
XLA Modules:
  0.0 36.3 jit_solution(16912640693858612872)
XLA Ops:
  0.7 2.7 %sketch_send.1 = (f32[128,128]{1,0:T(8,128)S(1)}, bf16[64,8192]{1,0:T(8,128)(2,1)S(1)}, bf16[8192,128]{1,0:T(8,128)(2,1)S(1)}) custom-call(s32[1]{0:T(128)} %bitcast.2.half_ref, bf16[64,256]{1,0:T(8,128)(2,1)} %row_ref.1, bf16[64,8192]{1,0:T(8,128)(2,1)} %col_hbm.1, bf16[8192,128]{1,0:T(8,128)(2,1)} %panel_hbm.1), custom_call_target="tpu_custom_call" | custom-call | tf_op jit(solution)/shard_map/sketch_send/pallas_call | solution.py:88
  3.4 3.0 %collective-permute-start = (f32[128,128]{1,0:T(8,128)S(1)}, f32[128,128]{1,0:T(8,128)S(1)}, u32[]{:S(2)}, u32[]{:S(2)}) collective-permute-start(f32[128,128]{1,0:T(8,128)S(1)} %get-tuple-element.16), channel_id=1, source_target_pairs={{0,1},{1,0},{2,3},{3,2},{4,5},{5,4},{6,7},{7,6},{8,9},{9,8},{10,11... | collective-permute-start | bytes 196616 | tf_op jit(solution)/shard_map/ppermute | solution.py:295
  6.4 1.9 %sketch_keep.1 = f32[128,128]{1,0:T(8,128)S(1)} custom-call(s32[1]{0:T(128)} %bitcast.2.half_ref, bf16[64,256]{1,0:T(8,128)(2,1)S(1)} %copy-done, bf16[64,8192]{1,0:T(8,128)(2,1)S(1)} %get-tuple-element.14.col_ref, bf16[8192,128]{1,0:T(8,128)(2,1)S(1)} %get-tuple-element.15.panel_ref), custom_call_target="tpu_custom_call" | custom-call | flops 436207616 | bytes 3407872 | tf_op jit(solution)/shard_map/sketch_keep/pallas_call | solution.py:108
  8.3 0.3 collective-permute-done
  8.6 2.2 %collective-permute-start.1 = (f32[128,128]{1,0:T(8,128)S(1)}, f32[128,128]{1,0:T(8,128)S(1)}, u32[]{:S(2)}, u32[]{:S(2)}) collective-permute-start(f32[128,128]{1,0:T(8,128)S(1)} %add.20), channel_id=1, source_target_pairs={{0,2},{1,3},{2,0},{3,1},{4,6},{5,7},{6,4},{7,5},{8,10},{9,11},{10,... | collective-permute-start | bytes 196616 | tf_op jit(solution)/shard_map/ppermute | solution.py:295
  10.8 0.1 pad_add_fusion.rank_ref
  10.9 0.0 collective-permute-start.3
  10.9 2.2 %collective-permute-done.1 = f32[128,128]{1,0:T(8,128)S(1)} collective-permute-done((f32[128,128]{1,0:T(8,128)S(1)}, f32[128,128]{1,0:T(8,128)S(1)}, u32[]{:S(2)}, u32[]{:S(2)}) %collective-permute-start.1) | collective-permute-done | bytes 65568 | tf_op jit(solution)/shard_map/ppermute | solution.py:295
  13.1 3.1 %collective-permute-start.2 = (f32[128,128]{1,0:T(8,128)S(1)}, f32[128,128]{1,0:T(8,128)S(1)}, u32[]{:S(2)}, u32[]{:S(2)}) collective-permute-start(f32[128,128]{1,0:T(8,128)S(1)} %add.21), channel_id=1, source_target_pairs={{0,4},{1,5},{2,6},{3,7},{4,0},{5,1},{6,2},{7,3},{8,12},{9,13},{10,... | collective-permute-start | bytes 196616 | tf_op jit(solution)/shard_map/ppermute | solution.py:295
  16.2 0.0 collective-permute-done.3
  16.2 2.2 %collective-permute-done.2 = f32[128,128]{1,0:T(8,128)S(1)} collective-permute-done((f32[128,128]{1,0:T(8,128)S(1)}, f32[128,128]{1,0:T(8,128)S(1)}, u32[]{:S(2)}, u32[]{:S(2)}) %collective-permute-start.2) | collective-permute-done | bytes 65568 | tf_op jit(solution)/shard_map/ppermute | solution.py:295
  18.4 2.8 %collective-permute-start.6 = (f32[128,128]{1,0:T(8,128)S(1)}, f32[128,128]{1,0:T(8,128)S(1)}, u32[]{:S(2)}, u32[]{:S(2)}) collective-permute-start(f32[128,128]{1,0:T(8,128)S(1)} %add.22), channel_id=1, source_target_pairs={{0,17},{1,16},{2,19},{3,18},{4,21},{5,20},{6,23},{7,22},{8,25},{9,... | collective-permute-start | bytes 196616 | tf_op jit(solution)/shard_map/ppermute | solution.py:295
  21.3 0.4 %collective-permute-start.4 = (f32[128,128]{1,0:T(8,128)S(1)}, f32[128,128]{1,0:T(8,128)S(1)}, u32[]{:S(2)}, u32[]{:S(2)}) collective-permute-start(f32[128,128]{1,0:T(8,128)S(1)} %add.22), channel_id=1, source_target_pairs={{0,9},{1,8},{2,11},{3,10},{4,13},{5,12},{6,15},{7,14},{8,1},{9,0},... | collective-permute-start | bytes 196616 | tf_op jit(solution)/shard_map/ppermute | solution.py:295
  21.7 0.3 collective-permute-start.8
  22.0 1.8 %collective-permute-done.6 = f32[128,128]{1,0:T(8,128)S(1)} collective-permute-done((f32[128,128]{1,0:T(8,128)S(1)}, f32[128,128]{1,0:T(8,128)S(1)}, u32[]{:S(2)}, u32[]{:S(2)}) %collective-permute-start.6) | collective-permute-done | bytes 65568 | tf_op jit(solution)/shard_map/ppermute | solution.py:295
  23.8 1.3 %collective-permute-done.5 = f32[128,128]{1,0:T(8,128)S(1)} collective-permute-done((f32[128,128]{1,0:T(8,128)S(1)}, f32[128,128]{1,0:T(8,128)S(1)}, u32[]{:S(2)}, u32[]{:S(2)}) %collective-permute-start.5) | collective-permute-done | bytes 65568 | tf_op jit(solution)/shard_map/ppermute | solution.py:295
  25.1 0.0 collective-permute-done.4
  25.1 0.6 %collective-permute-start.7 = (f32[512,128]{1,0:T(8,128)S(1)}, f32[512,128]{1,0:T(8,128)S(1)}, u32[]{:S(2)}, u32[]{:S(2)}) collective-permute-start(f32[512,128]{1,0:T(8,128)S(1)} %pad_maximum_fusion), channel_id=1, source_target_pairs={{0,8},{1,9},{2,10},{3,11},{4,12},{5,13},{6,14},{7,15},{8,0},{9,1},... | collective-permute-start | bytes 786440 | tf_op jit(solution)/shard_map/ppermute | solution.py:295
  25.7 1.1 %collective-permute-done.7 = f32[512,128]{1,0:T(8,128)S(1)} collective-permute-done((f32[512,128]{1,0:T(8,128)S(1)}, f32[512,128]{1,0:T(8,128)S(1)}, u32[]{:S(2)}, u32[]{:S(2)}) %collective-permute-start.7) | collective-permute-done | bytes 262176 | tf_op jit(solution)/shard_map/ppermute | solution.py:295
  27.0 7.0 %finish.1 = (f32[256,128]{1,0:T(8,128)}, bf16[32,4096]{1,0:T(8,128)(2,1)S(1)}, bf16[32,4096]{1,0:T(8,128)(2,1)S(1)}) custom-call(s32[2]{0:T(128)S(1)} %pad_add_fusion.rank_ref, f32[1024,128]{1,0:T(8,128)S(1)} %select_dynamic-update-slice_fusion.sketch_ref, bf16[4,64,256]{2,1,0:T(8,128)(2,1)S(1)} %pad_maximum_fusion.1.row_ref, ...), custom_call_target="tpu_custom_call" | custom-call | tf_op jit(solution)/shard_map/finish/pallas_call | solution.py:246
  34.0 0.4 %collective-permute-start.9 = (bf16[32,4096]{1,0:T(8,128)(2,1)S(1)}, bf16[32,4096]{1,0:T(8,128)(2,1)S(1)}, u32[]{:S(2)}, u32[]{:S(2)}) collective-permute-start(bf16[32,4096]{1,0:T(8,128)(2,1)S(1)} %get-tuple-element.24), channel_id=1, source_target_pairs={{0,8},{1,9},{2,10},{3,11},{4,12},{5,13},{6,14},{7,15},{8,0},{9,1},... | collective-permute-start | bytes 786440 | tf_op jit(solution)/shard_map/ppermute | solution.py:295
  34.5 0.7 %placed.2.refs_0_ = bf16[32,8192]{1,0:T(8,128)(2,1)} custom-call(s32[1]{0:T(128)} %bitcast.6.at_ref, bf16[32,4096]{1,0:T(8,128)(2,1)S(1)} %get-tuple-element.25.part_ref), custom_call_target="tpu_custom_call" | custom-call | bytes 524288 | tf_op jit(solution)/shard_map/placed/pallas_call | solution.py:279
  35.2 0.4 %collective-permute-done.9.part_ref = bf16[32,4096]{1,0:T(8,128)(2,1)S(1)} collective-permute-done((bf16[32,4096]{1,0:T(8,128)(2,1)S(1)}, bf16[32,4096]{1,0:T(8,128)(2,1)S(1)}, u32[]{:S(2)}, u32[]{:S(2)}) %collective-permute-start.9) | collective-permute-done | bytes 262176 | tf_op jit(solution)/shard_map/ppermute | solution.py:295
  35.6 0.7 %placed.3 = bf16[32,8192]{1,0:T(8,128)(2,1)} custom-call(s32[1]{0:T(128)} %bitcast.5.at_ref, bf16[32,4096]{1,0:T(8,128)(2,1)S(1)} %collective-permute-done.9.part_ref, bf16[32,8192]{1,0:T(8,128)(2,1)} %placed.2.refs_0_), custom_call_target="tpu_custom_call", output_to_operand_aliasing={{}: (2, {})} | custom-call | bytes 524288 | tf_op jit(solution)/shard_map/placed/pallas_call | solution.py:279
  (22 shorter events, 0.2 us)
Async XLA Ops:
  0.6 5.8 %copy-start = (bf16[64,256]{1,0:T(8,128)(2,1)S(1)}, bf16[64,256]{1,0:T(8,128)(2,1)}, u32[]{:S(2)}) copy-start(bf16[64,256]{1,0:T(8,128)(2,1)} %row_ref.1) | copy-start | bytes 98308
  3.4 5.3 %collective-permute-start = (f32[128,128]{1,0:T(8,128)S(1)}, f32[128,128]{1,0:T(8,128)S(1)}, u32[]{:S(2)}, u32[]{:S(2)}) collective-permute-start(f32[128,128]{1,0:T(8,128)S(1)} %get-tuple-element.16), channel_id=1, source_target_pairs={{0,1},{1,0},{2,3},{3,2},{4,5},{5,4},{6,7},{7,6},{8,9},{9,8},{10,11... | collective-permute-start | bytes 196616 | tf_op jit(solution)/shard_map/ppermute | solution.py:295
  6.4 9.8 %copy-start.1 = (bf16[64,8192]{1,0:T(8,128)(2,1)S(1)}, bf16[64,8192]{1,0:T(8,128)(2,1)}, u32[]{:S(2)}) copy-start(bf16[64,8192]{1,0:T(8,128)(2,1)} %col_hbm.1) | copy-start | bytes 3145732
  8.6 4.4 %collective-permute-start.1 = (f32[128,128]{1,0:T(8,128)S(1)}, f32[128,128]{1,0:T(8,128)S(1)}, u32[]{:S(2)}, u32[]{:S(2)}) collective-permute-start(f32[128,128]{1,0:T(8,128)S(1)} %add.20), channel_id=1, source_target_pairs={{0,2},{1,3},{2,0},{3,1},{4,6},{5,7},{6,4},{7,5},{8,10},{9,11},{10,... | collective-permute-start | bytes 196616 | tf_op jit(solution)/shard_map/ppermute | solution.py:295
  10.9 5.3 %collective-permute-start.3 = (bf16[64,256]{1,0:T(8,128)(2,1)S(1)}, bf16[64,256]{1,0:T(8,128)(2,1)S(1)}, u32[]{:S(2)}, u32[]{:S(2)}) collective-permute-start(bf16[64,256]{1,0:T(8,128)(2,1)S(1)} %copy-done), channel_id=1, source_target_pairs={{0,24},{1,25},{2,26},{3,27},{4,28},{5,29},{6,30},{7,31},{8,16},{9,... | collective-permute-start | bytes 98312 | tf_op jit(solution)/shard_map/ppermute | solution.py:295
  13.1 5.3 %collective-permute-start.2 = (f32[128,128]{1,0:T(8,128)S(1)}, f32[128,128]{1,0:T(8,128)S(1)}, u32[]{:S(2)}, u32[]{:S(2)}) collective-permute-start(f32[128,128]{1,0:T(8,128)S(1)} %add.21), channel_id=1, source_target_pairs={{0,4},{1,5},{2,6},{3,7},{4,0},{5,1},{6,2},{7,3},{8,12},{9,13},{10,... | collective-permute-start | bytes 196616 | tf_op jit(solution)/shard_map/ppermute | solution.py:295
  18.4 5.3 %collective-permute-start.6 = (f32[128,128]{1,0:T(8,128)S(1)}, f32[128,128]{1,0:T(8,128)S(1)}, u32[]{:S(2)}, u32[]{:S(2)}) collective-permute-start(f32[128,128]{1,0:T(8,128)S(1)} %add.22), channel_id=1, source_target_pairs={{0,17},{1,16},{2,19},{3,18},{4,21},{5,20},{6,23},{7,22},{8,25},{9,... | collective-permute-start | bytes 196616 | tf_op jit(solution)/shard_map/ppermute | solution.py:295
  21.3 3.8 %collective-permute-start.5 = (f32[128,128]{1,0:T(8,128)S(1)}, f32[128,128]{1,0:T(8,128)S(1)}, u32[]{:S(2)}, u32[]{:S(2)}) collective-permute-start(f32[128,128]{1,0:T(8,128)S(1)} %add.22), channel_id=1, source_target_pairs={{0,24},{1,25},{2,26},{3,27},{4,28},{5,29},{6,30},{7,31},{8,16},{9,... | collective-permute-start | bytes 196616 | tf_op jit(solution)/shard_map/ppermute | solution.py:295
  21.3 3.8 %collective-permute-start.4 = (f32[128,128]{1,0:T(8,128)S(1)}, f32[128,128]{1,0:T(8,128)S(1)}, u32[]{:S(2)}, u32[]{:S(2)}) collective-permute-start(f32[128,128]{1,0:T(8,128)S(1)} %add.22), channel_id=1, source_target_pairs={{0,9},{1,8},{2,11},{3,10},{4,13},{5,12},{6,15},{7,14},{8,1},{9,0},... | collective-permute-start | bytes 196616 | tf_op jit(solution)/shard_map/ppermute | solution.py:295
  21.7 4.0 %collective-permute-start.8 = (bf16[2,64,256]{2,1,0:T(8,128)(2,1)S(1)}, bf16[2,64,256]{2,1,0:T(8,128)(2,1)S(1)}, u32[]{:S(2)}, u32[]{:S(2)}) collective-permute-start(bf16[2,64,256]{2,1,0:T(8,128)(2,1)S(1)} %pad_maximum_fusion.2), channel_id=1, source_target_pairs={{0,8},{1,9},{2,10},{3,11},{4,12},{5,13},{6,14},{7,15},{8,0},{9,1},... | collective-permute-start | bytes 196616 | tf_op jit(solution)/shard_map/ppermute | solution.py:295
  25.1 1.8 %collective-permute-start.7 = (f32[512,128]{1,0:T(8,128)S(1)}, f32[512,128]{1,0:T(8,128)S(1)}, u32[]{:S(2)}, u32[]{:S(2)}) collective-permute-start(f32[512,128]{1,0:T(8,128)S(1)} %pad_maximum_fusion), channel_id=1, source_target_pairs={{0,8},{1,9},{2,10},{3,11},{4,12},{5,13},{6,14},{7,15},{8,0},{9,1},... | collective-permute-start | bytes 786440 | tf_op jit(solution)/shard_map/ppermute | solution.py:295
  34.0 1.6 %collective-permute-start.9 = (bf16[32,4096]{1,0:T(8,128)(2,1)S(1)}, bf16[32,4096]{1,0:T(8,128)(2,1)S(1)}, u32[]{:S(2)}, u32[]{:S(2)}) collective-permute-start(bf16[32,4096]{1,0:T(8,128)(2,1)S(1)} %get-tuple-element.24), channel_id=1, source_target_pairs={{0,8},{1,9},{2,10},{3,11},{4,12},{5,13},{6,14},{7,15},{8,0},{9,1},... | collective-permute-start | bytes 786440 | tf_op jit(solution)/shard_map/ppermute | solution.py:295

commit v8 on v7

--- a/solution.py
+++ b/solution.py
@@ -323,8 +323,8 @@
             moved, y_points = lax.optimization_barrier((moved, y_points))
         part = part + moved
 
-    far = swapped(part, core_bit | y_bit, 0)
-    cross = swapped(part, y_bit, x_bit)
+    far = swapped(part, y_bit, 0)
+    cross = swapped(part, core_bit | y_bit, x_bit)
     near = swapped(part, core_bit, x_bit)
     split = part.shape[0]
     held, held_points = jnp.concatenate([part, near, far, cross]), jnp.stack([row_points, y_points])
@@ -334,7 +334,7 @@
     sketch = [ordered(part, near_there), ordered(part_there, near)]
     sketch += [ordered(far, cross_there), ordered(far_there, cross)]
     sketch = jnp.concatenate(sketch)
-    row_blocks = jnp.stack([row_points, there_points[0], y_points, there_points[1]])
+    row_blocks = jnp.stack([row_points, there_points[0], there_points[1], y_points])
     for bit in y_bits[:-1]:
         sketch, row_blocks = [both(a, swapped(a, bit, 0)) for a in (sketch, row_blocks)]
 

time: 36.5 us -> 36.2 us (level)
  waiting for transfers between devices: 9.32 us -> 8.58 us
  starting transfers between devices: 12.9 us -> 13.3 us
    ppermute x10, waiting for transfers between devices: 9.32 us -> 8.58 us  [swapped(): return lax.ppermute(value, ('row', 'col'), pairs)]
    ppermute x10, starting transfers between devices: 12.9 us -> 13.3 us  [swapped(): return lax.ppermute(value, ('row', 'col'), pairs)]
where the time goes in v8:
time: 36.2 us; the launch traced here: 36.1 us
  starting transfers between devices  13.3 us (37%)
  Pallas kernels  13.1 us (36%)
  waiting for transfers between devices  8.58 us (24%)
  between operations  0.79 us (2%)
    ppermute x10, starting transfers between devices, swapped(): return lax.ppermute(value, ('row', 'col'), pairs)  13.3 us
    ppermute x10, waiting for transfers between devices, swapped(): return lax.ppermute(value, ('row', 'col'), pairs)  8.58 us
    pallas_call x1, Pallas kernels, finish(): pl.pallas_call(functools.partial(finish_body, 2.0 / dim, math.sqrt(total)...  7.03 us
    pallas_call x1, Pallas kernels, sketch_halves(): pl.pallas_call(functools.partial(sketch_send_body, 2.0 / dim), in_specs=[...  2.76 us
    pallas_call x1, Pallas kernels, sketch_halves(): pl.pallas_call(functools.partial(sketch_keep_body, 2.0 / dim), in_specs=[...  1.93 us
    pallas_call x2, Pallas kernels, placed(): pl.pallas_call(place_body, in_specs=specs, out_specs=remote, out_shape=ja...  1.42 us
  transfers between devices with their start and end apart: 10, of which 7 were waited for; matrix products, arithmetic and copies ran while one was open for 0% of the time, Pallas kernels for 7%

profile of v8, /device:TPU:0, one launch (start us, length us, event | category | flops | bytes accessed | tf_op | source)
XLA Modules:
  0.0 36.1 jit_solution(17920207707325605528)
XLA Ops:
  0.7 2.8 %sketch_send.1 = (f32[128,128]{1,0:T(8,128)S(1)}, bf16[64,8192]{1,0:T(8,128)(2,1)S(1)}, bf16[8192,128]{1,0:T(8,128)(2,1)S(1)}) custom-call(s32[1]{0:T(128)} %bitcast.2.half_ref, bf16[64,256]{1,0:T(8,128)(2,1)} %row_ref.1, bf16[64,8192]{1,0:T(8,128)(2,1)} %col_hbm.1, bf16[8192,128]{1,0:T(8,128)(2,1)} %panel_hbm.1), custom_call_target="tpu_custom_call" | custom-call | tf_op jit(solution)/shard_map/sketch_send/pallas_call | solution.py:88
  3.4 3.0 %collective-permute-start = (f32[128,128]{1,0:T(8,128)S(1)}, f32[128,128]{1,0:T(8,128)S(1)}, u32[]{:S(2)}, u32[]{:S(2)}) collective-permute-start(f32[128,128]{1,0:T(8,128)S(1)} %get-tuple-element.16), channel_id=1, source_target_pairs={{0,1},{1,0},{2,3},{3,2},{4,5},{5,4},{6,7},{7,6},{8,9},{9,8},{10,11... | collective-permute-start | bytes 196616 | tf_op jit(solution)/shard_map/ppermute | solution.py:295
  6.4 1.9 %sketch_keep.1 = f32[128,128]{1,0:T(8,128)S(1)} custom-call(s32[1]{0:T(128)} %bitcast.2.half_ref, bf16[64,256]{1,0:T(8,128)(2,1)S(1)} %copy-done, bf16[64,8192]{1,0:T(8,128)(2,1)S(1)} %get-tuple-element.14.col_ref, bf16[8192,128]{1,0:T(8,128)(2,1)S(1)} %get-tuple-element.15.panel_ref), custom_call_target="tpu_custom_call" | custom-call | flops 436207616 | bytes 3407872 | tf_op jit(solution)/shard_map/sketch_keep/pallas_call | solution.py:108
  8.4 0.3 collective-permute-done
  8.7 2.2 %collective-permute-start.1 = (f32[128,128]{1,0:T(8,128)S(1)}, f32[128,128]{1,0:T(8,128)S(1)}, u32[]{:S(2)}, u32[]{:S(2)}) collective-permute-start(f32[128,128]{1,0:T(8,128)S(1)} %add.20), channel_id=1, source_target_pairs={{0,2},{1,3},{2,0},{3,1},{4,6},{5,7},{6,4},{7,5},{8,10},{9,11},{10,... | collective-permute-start | bytes 196616 | tf_op jit(solution)/shard_map/ppermute | solution.py:295
  10.9 0.0 collective-permute-start.3
  10.9 2.2 %collective-permute-done.1 = f32[128,128]{1,0:T(8,128)S(1)} collective-permute-done((f32[128,128]{1,0:T(8,128)S(1)}, f32[128,128]{1,0:T(8,128)S(1)}, u32[]{:S(2)}, u32[]{:S(2)}) %collective-permute-start.1) | collective-permute-done | bytes 65568 | tf_op jit(solution)/shard_map/ppermute | solution.py:295
  13.1 3.1 %collective-permute-start.2 = (f32[128,128]{1,0:T(8,128)S(1)}, f32[128,128]{1,0:T(8,128)S(1)}, u32[]{:S(2)}, u32[]{:S(2)}) collective-permute-start(f32[128,128]{1,0:T(8,128)S(1)} %add.21), channel_id=1, source_target_pairs={{0,4},{1,5},{2,6},{3,7},{4,0},{5,1},{6,2},{7,3},{8,12},{9,13},{10,... | collective-permute-start | bytes 196616 | tf_op jit(solution)/shard_map/ppermute | solution.py:295
  16.2 0.1 pad_add_fusion.rank_ref
  16.3 0.0 collective-permute-done.3
  16.3 2.2 %collective-permute-done.2 = f32[128,128]{1,0:T(8,128)S(1)} collective-permute-done((f32[128,128]{1,0:T(8,128)S(1)}, f32[128,128]{1,0:T(8,128)S(1)}, u32[]{:S(2)}, u32[]{:S(2)}) %collective-permute-start.2) | collective-permute-done | bytes 65568 | tf_op jit(solution)/shard_map/ppermute | solution.py:295
  18.5 0.1 collective-permute-start.6
  18.6 1.9 %collective-permute-start.5 = (f32[128,128]{1,0:T(8,128)S(1)}, f32[128,128]{1,0:T(8,128)S(1)}, u32[]{:S(2)}, u32[]{:S(2)}) collective-permute-start(f32[128,128]{1,0:T(8,128)S(1)} %add.22), channel_id=1, source_target_pairs={{0,16},{1,17},{2,18},{3,19},{4,20},{5,21},{6,22},{7,23},{8,24},{9,... | collective-permute-start | bytes 196616 | tf_op jit(solution)/shard_map/ppermute | solution.py:295
  20.5 1.1 %collective-permute-start.4 = (f32[128,128]{1,0:T(8,128)S(1)}, f32[128,128]{1,0:T(8,128)S(1)}, u32[]{:S(2)}, u32[]{:S(2)}) collective-permute-start(f32[128,128]{1,0:T(8,128)S(1)} %add.22), channel_id=1, source_target_pairs={{0,9},{1,8},{2,11},{3,10},{4,13},{5,12},{6,15},{7,14},{8,1},{9,0},... | collective-permute-start | bytes 196616 | tf_op jit(solution)/shard_map/ppermute | solution.py:295
  21.6 0.6 %collective-permute-start.8 = (bf16[2,64,256]{2,1,0:T(8,128)(2,1)S(1)}, bf16[2,64,256]{2,1,0:T(8,128)(2,1)S(1)}, u32[]{:S(2)}, u32[]{:S(2)}) collective-permute-start(bf16[2,64,256]{2,1,0:T(8,128)(2,1)S(1)} %pad_maximum_fusion.2), channel_id=1, source_target_pairs={{0,8},{1,9},{2,10},{3,11},{4,12},{5,13},{6,14},{7,15},{8,0},{9,1},... | collective-permute-start | bytes 196616 | tf_op jit(solution)/shard_map/ppermute | solution.py:295
  22.1 1.4 %collective-permute-done.6 = f32[128,128]{1,0:T(8,128)S(1)} collective-permute-done((f32[128,128]{1,0:T(8,128)S(1)}, f32[128,128]{1,0:T(8,128)S(1)}, u32[]{:S(2)}, u32[]{:S(2)}) %collective-permute-start.6) | collective-permute-done | bytes 65568 | tf_op jit(solution)/shard_map/ppermute | solution.py:295
  23.6 0.9 %collective-permute-done.5 = f32[128,128]{1,0:T(8,128)S(1)} collective-permute-done((f32[128,128]{1,0:T(8,128)S(1)}, f32[128,128]{1,0:T(8,128)S(1)}, u32[]{:S(2)}, u32[]{:S(2)}) %collective-permute-start.5) | collective-permute-done | bytes 65568 | tf_op jit(solution)/shard_map/ppermute | solution.py:295
  24.5 0.9 %collective-permute-start.7 = (f32[512,128]{1,0:T(8,128)S(1)}, f32[512,128]{1,0:T(8,128)S(1)}, u32[]{:S(2)}, u32[]{:S(2)}) collective-permute-start(f32[512,128]{1,0:T(8,128)S(1)} %pad_maximum_fusion), channel_id=1, source_target_pairs={{0,8},{1,9},{2,10},{3,11},{4,12},{5,13},{6,14},{7,15},{8,0},{9,1},... | collective-permute-start | bytes 786440 | tf_op jit(solution)/shard_map/ppermute | solution.py:295
  25.5 1.1 %collective-permute-done.7 = f32[512,128]{1,0:T(8,128)S(1)} collective-permute-done((f32[512,128]{1,0:T(8,128)S(1)}, f32[512,128]{1,0:T(8,128)S(1)}, u32[]{:S(2)}, u32[]{:S(2)}) %collective-permute-start.7) | collective-permute-done | bytes 262176 | tf_op jit(solution)/shard_map/ppermute | solution.py:295
  26.7 7.0 %finish.1 = (f32[256,128]{1,0:T(8,128)}, bf16[32,4096]{1,0:T(8,128)(2,1)S(1)}, bf16[32,4096]{1,0:T(8,128)(2,1)S(1)}) custom-call(s32[2]{0:T(128)S(1)} %pad_add_fusion.rank_ref, f32[1024,128]{1,0:T(8,128)S(1)} %select_dynamic-update-slice_fusion.sketch_ref, bf16[4,64,256]{2,1,0:T(8,128)(2,1)S(1)} %pad_maximum_fusion.1.row_ref, ...), custom_call_target="tpu_custom_call" | custom-call | tf_op jit(solution)/shard_map/finish/pallas_call | solution.py:246
  33.8 0.4 %collective-permute-start.9 = (bf16[32,4096]{1,0:T(8,128)(2,1)S(1)}, bf16[32,4096]{1,0:T(8,128)(2,1)S(1)}, u32[]{:S(2)}, u32[]{:S(2)}) collective-permute-start(bf16[32,4096]{1,0:T(8,128)(2,1)S(1)} %get-tuple-element.24), channel_id=1, source_target_pairs={{0,8},{1,9},{2,10},{3,11},{4,12},{5,13},{6,14},{7,15},{8,0},{9,1},... | collective-permute-start | bytes 786440 | tf_op jit(solution)/shard_map/ppermute | solution.py:295
  34.2 0.7 %placed.2.refs_0_ = bf16[32,8192]{1,0:T(8,128)(2,1)} custom-call(s32[1]{0:T(128)} %bitcast.6.at_ref, bf16[32,4096]{1,0:T(8,128)(2,1)S(1)} %get-tuple-element.25.part_ref), custom_call_target="tpu_custom_call" | custom-call | bytes 524288 | tf_op jit(solution)/shard_map/placed/pallas_call | solution.py:279
  34.9 0.4 %collective-permute-done.9.part_ref = bf16[32,4096]{1,0:T(8,128)(2,1)S(1)} collective-permute-done((bf16[32,4096]{1,0:T(8,128)(2,1)S(1)}, bf16[32,4096]{1,0:T(8,128)(2,1)S(1)}, u32[]{:S(2)}, u32[]{:S(2)}) %collective-permute-start.9) | collective-permute-done | bytes 262176 | tf_op jit(solution)/shard_map/ppermute | solution.py:295
  35.4 0.7 %placed.3 = bf16[32,8192]{1,0:T(8,128)(2,1)} custom-call(s32[1]{0:T(128)} %bitcast.5.at_ref, bf16[32,4096]{1,0:T(8,128)(2,1)S(1)} %collective-permute-done.9.part_ref, bf16[32,8192]{1,0:T(8,128)(2,1)} %placed.2.refs_0_), custom_call_target="tpu_custom_call", output_to_operand_aliasing={{}: (2, {})} | custom-call | bytes 524288 | tf_op jit(solution)/shard_map/placed/pallas_call | solution.py:279
  (21 shorter events, 0.2 us)
Async XLA Ops:
  0.6 5.8 %copy-start = (bf16[64,256]{1,0:T(8,128)(2,1)S(1)}, bf16[64,256]{1,0:T(8,128)(2,1)}, u32[]{:S(2)}) copy-start(bf16[64,256]{1,0:T(8,128)(2,1)} %row_ref.1) | copy-start | bytes 98308
  3.4 5.3 %collective-permute-start = (f32[128,128]{1,0:T(8,128)S(1)}, f32[128,128]{1,0:T(8,128)S(1)}, u32[]{:S(2)}, u32[]{:S(2)}) collective-permute-start(f32[128,128]{1,0:T(8,128)S(1)} %get-tuple-element.16), channel_id=1, source_target_pairs={{0,1},{1,0},{2,3},{3,2},{4,5},{5,4},{6,7},{7,6},{8,9},{9,8},{10,11... | collective-permute-start | bytes 196616 | tf_op jit(solution)/shard_map/ppermute | solution.py:295
  6.4 19.0 %copy-start.1 = (bf16[64,8192]{1,0:T(8,128)(2,1)S(1)}, bf16[64,8192]{1,0:T(8,128)(2,1)}, u32[]{:S(2)}) copy-start(bf16[64,8192]{1,0:T(8,128)(2,1)} %col_hbm.1) | copy-start | bytes 3145732
  8.7 4.4 %collective-permute-start.1 = (f32[128,128]{1,0:T(8,128)S(1)}, f32[128,128]{1,0:T(8,128)S(1)}, u32[]{:S(2)}, u32[]{:S(2)}) collective-permute-start(f32[128,128]{1,0:T(8,128)S(1)} %add.20), channel_id=1, source_target_pairs={{0,2},{1,3},{2,0},{3,1},{4,6},{5,7},{6,4},{7,5},{8,10},{9,11},{10,... | collective-permute-start | bytes 196616 | tf_op jit(solution)/shard_map/ppermute | solution.py:295
  10.9 5.4 %collective-permute-start.3 = (bf16[64,256]{1,0:T(8,128)(2,1)S(1)}, bf16[64,256]{1,0:T(8,128)(2,1)S(1)}, u32[]{:S(2)}, u32[]{:S(2)}) collective-permute-start(bf16[64,256]{1,0:T(8,128)(2,1)S(1)} %copy-done), channel_id=1, source_target_pairs={{0,24},{1,25},{2,26},{3,27},{4,28},{5,29},{6,30},{7,31},{8,16},{9,... | collective-permute-start | bytes 98312 | tf_op jit(solution)/shard_map/ppermute | solution.py:295
  13.1 5.3 %collective-permute-start.2 = (f32[128,128]{1,0:T(8,128)S(1)}, f32[128,128]{1,0:T(8,128)S(1)}, u32[]{:S(2)}, u32[]{:S(2)}) collective-permute-start(f32[128,128]{1,0:T(8,128)S(1)} %add.21), channel_id=1, source_target_pairs={{0,4},{1,5},{2,6},{3,7},{4,0},{5,1},{6,2},{7,3},{8,12},{9,13},{10,... | collective-permute-start | bytes 196616 | tf_op jit(solution)/shard_map/ppermute | solution.py:295
  18.5 5.1 %collective-permute-start.6 = (f32[128,128]{1,0:T(8,128)S(1)}, f32[128,128]{1,0:T(8,128)S(1)}, u32[]{:S(2)}, u32[]{:S(2)}) collective-permute-start(f32[128,128]{1,0:T(8,128)S(1)} %add.22), channel_id=1, source_target_pairs={{0,25},{1,24},{2,27},{3,26},{4,29},{5,28},{6,31},{7,30},{8,17},{9,... | collective-permute-start | bytes 196616 | tf_op jit(solution)/shard_map/ppermute | solution.py:295
  18.6 5.9 %collective-permute-start.5 = (f32[128,128]{1,0:T(8,128)S(1)}, f32[128,128]{1,0:T(8,128)S(1)}, u32[]{:S(2)}, u32[]{:S(2)}) collective-permute-start(f32[128,128]{1,0:T(8,128)S(1)} %add.22), channel_id=1, source_target_pairs={{0,16},{1,17},{2,18},{3,19},{4,20},{5,21},{6,22},{7,23},{8,24},{9,... | collective-permute-start | bytes 196616 | tf_op jit(solution)/shard_map/ppermute | solution.py:295
  20.5 4.0 %collective-permute-start.4 = (f32[128,128]{1,0:T(8,128)S(1)}, f32[128,128]{1,0:T(8,128)S(1)}, u32[]{:S(2)}, u32[]{:S(2)}) collective-permute-start(f32[128,128]{1,0:T(8,128)S(1)} %add.22), channel_id=1, source_target_pairs={{0,9},{1,8},{2,11},{3,10},{4,13},{5,12},{6,15},{7,14},{8,1},{9,0},... | collective-permute-start | bytes 196616 | tf_op jit(solution)/shard_map/ppermute | solution.py:295
  21.6 3.9 %collective-permute-start.8 = (bf16[2,64,256]{2,1,0:T(8,128)(2,1)S(1)}, bf16[2,64,256]{2,1,0:T(8,128)(2,1)S(1)}, u32[]{:S(2)}, u32[]{:S(2)}) collective-permute-start(bf16[2,64,256]{2,1,0:T(8,128)(2,1)S(1)} %pad_maximum_fusion.2), channel_id=1, source_target_pairs={{0,8},{1,9},{2,10},{3,11},{4,12},{5,13},{6,14},{7,15},{8,0},{9,1},... | collective-permute-start | bytes 196616 | tf_op jit(solution)/shard_map/ppermute | solution.py:295
  24.5 2.1 %collective-permute-start.7 = (f32[512,128]{1,0:T(8,128)S(1)}, f32[512,128]{1,0:T(8,128)S(1)}, u32[]{:S(2)}, u32[]{:S(2)}) collective-permute-start(f32[512,128]{1,0:T(8,128)S(1)} %pad_maximum_fusion), channel_id=1, source_target_pairs={{0,8},{1,9},{2,10},{3,11},{4,12},{5,13},{6,14},{7,15},{8,0},{9,1},... | collective-permute-start | bytes 786440 | tf_op jit(solution)/shard_map/ppermute | solution.py:295
  33.8 1.6 %collective-permute-start.9 = (bf16[32,4096]{1,0:T(8,128)(2,1)S(1)}, bf16[32,4096]{1,0:T(8,128)(2,1)S(1)}, u32[]{:S(2)}, u32[]{:S(2)}) collective-permute-start(bf16[32,4096]{1,0:T(8,128)(2,1)S(1)} %get-tuple-element.24), channel_id=1, source_target_pairs={{0,8},{1,9},{2,10},{3,11},{4,12},{5,13},{6,14},{7,15},{8,0},{9,1},... | collective-permute-start | bytes 786440 | tf_op jit(solution)/shard_map/ppermute | solution.py:295
